TPU v7x, 32 devices: a whole 2x2x4 slice. The times are simulated.
32 devices in a mesh: section: 2 (over core), tensor: 4 (over z), dp: 4 (over y, x).
Axes of the slice: x: 2, y: 2, z: 4, core: 2. Of those that a mesh axis runs over, the one named last changes fastest.
Arguments:
- layer_input: bfloat16 [2, 1024, 1024], P(None, 'dp'), may hold values from -6 to 6
- out_cotangent: bfloat16 [2, 1024, 1024], P(None, 'dp'), may hold values from -6 to 6
- seq_lengths: int32 [2, 3], replicated, may hold values from 64 to 768, as said below
- norm_gain: float32 [2, 1024], P('section'), may hold values from 0.25 to 1.75
- norm_bias: float32 [2, 1024], P('section'), may hold values from -1.5 to 1.5
- wide_weight: bfloat16 [2, 1024, 3072], P('section', None, 'tensor'), may hold values from -0.1875 to 0.1875
- wide_bias: float32 [2, 3072], P('section', 'tensor'), may hold values from -2.5 to 2.5
- narrow_weight: bfloat16 [2, 1024, 512], P('section', None, 'tensor'), may hold values from -0.1875 to 0.1875
- narrow_bias: float32 [2, 512], P('section', 'tensor'), may hold values from -2.5 to 2.5
- ssm_decay: float32 [2, 512, 64], P('section', 'tensor'), may hold values from 1.953125e-05 to 0.03
- ssm_input: float32 [2, 512, 64], P('section', 'tensor'), may hold values from -4 to 4
- ssm_output: float32 [2, 512, 64], P('section', 'tensor'), may hold values from -0.75 to 0.75
- ssm_skip: float32 [2, 512], P('section', 'tensor'), may hold values from -4 to 4
- lift_weight: bfloat16 [2, 512, 3072], P('section', None, 'tensor'), may hold values from -0.25 to 0.25
- lift_bias: float32 [2, 3072], P('section', 'tensor'), may hold values from -2.5 to 2.5
- down_weight: bfloat16 [2, 3072, 1024], P('section', 'tensor'), may hold values from -0.21875 to 0.21875
- down_bias: float32 [2, 1024], P('section'), may hold values from -2.5 to 2.5
Outputs:
- section_output: float32 [2, 2, 1024, 1024], P('section', None, 'dp', 'tensor')
- input_grad: float32 [2, 2, 1024, 1024], P('section', None, 'dp', 'tensor')
- grad_norm_gain: float32 [2, 1024], P('section', ('tensor', 'dp'))
- grad_norm_bias: float32 [2, 1024], P('section', ('tensor', 'dp'))
- grad_wide_weight: float32 [2, 1024, 3072], P('section', 'dp', 'tensor')
- grad_wide_bias: float32 [2, 3072], P('section', ('tensor', 'dp'))
- grad_narrow_weight: float32 [2, 1024, 512], P('section', 'dp', 'tensor')
- grad_narrow_bias: float32 [2, 512], P('section', ('tensor', 'dp'))
- grad_ssm_decay: float32 [2, 512, 64], P('section', ('tensor', 'dp'))
- grad_ssm_input: float32 [2, 512, 64], P('section', ('tensor', 'dp'))
- grad_ssm_output: float32 [2, 512, 64], P('section', ('tensor', 'dp'))
- grad_ssm_skip: float32 [2, 512], P('section', ('tensor', 'dp'))
- grad_lift_weight: float32 [2, 512, 3072], P('section', 'dp', 'tensor')
- grad_lift_bias: float32 [2, 3072], P('section', ('tensor', 'dp'))
- grad_down_weight: float32 [2, 3072, 1024], P('section', ('tensor', 'dp'))
- grad_down_bias: float32 [2, 1024], P('section', 'dp')
Inputs may be any that keep to these rules, and one draw needn't show every extreme that they name: `seq_lengths`: each row holds 3 lengths that add up to 1024; the second is 768, the first and the last add up to 256.
All inputs are finite; a program needn't handle non-finite values.
Results may differ from a plain program's by a relative error of at most 0.015.
Values may be sent and summed in bfloat16 or wider, within the bound.
No kernel may reach another device: no remote copies, remote signals or barrier semaphores. Data moves between devices by JAX's collectives and lax.ppermute only.
A program may use at most 256 MiB of HBM per device.

v0:
```python
from functools import partial

import jax
import jax.numpy as jnp
from jax import lax
from jax.sharding import PartitionSpec as P

HIGHEST_PRECISION = lax.Precision.HIGHEST
NORM_EPSILON = 1e-05


def entering_2(value, axis, join, neutral):
    count, mine = (lax.axis_size(axis), lax.axis_index(axis))
    pieces = jax.tree.map(lambda part: lax.all_gather(part, axis), value)
    so_far = jax.tree.map(
        lambda part, zero: jnp.full_like(part, 0) + jnp.asarray(zero, part.dtype), value, neutral
    )

    def entering_hop(position, so_far):
        longer = join(so_far, jax.tree.map(lambda part: part[position], pieces))
        return jax.tree.map(lambda new, old: jnp.where(position < mine, new, old), longer, so_far)

    return lax.fori_loop(0, count - 1, entering_hop, so_far)


def carried_in(x, axis, combine, identity):
    count, index = (lax.axis_size(axis), lax.axis_index(axis))
    everything = jax.tree.map(
        lambda part, kind: lax.all_gather(part.astype(kind), axis),
        x,
        jax.tree.map(lambda a: jnp.bfloat16 if a.dtype == jnp.float32 else a.dtype, x),
    )
    start = jax.tree.map(
        lambda part, zero: jnp.broadcast_to(jnp.asarray(zero, part.dtype), part.shape), x, identity
    )

    def carried_hop(k, before):
        at = count - 1 - k
        reached = at > index
        new = combine(
            before, jax.tree.map(lambda part, own: part[at].astype(own.dtype), everything, x)
        )
        return jax.tree.map(lambda a, b: jnp.where(reached, a, b), new, before)

    return lax.fori_loop(0, count, carried_hop, start)


def passed_along(block, axis, distance):
    devices = range(lax.axis_size(axis))
    route = [(i - distance, i) for i in devices if i - distance in devices]
    return lax.ppermute(block, axis, route)


def shortened(x):
    return jax.tree.map(lambda a: a.astype(jnp.bfloat16) if a.dtype == jnp.float32 else a, x)


def layer_norm(input_rows, scale, shift_term):
    center = jnp.mean(input_rows, axis=-1, keepdims=True)
    offset = input_rows - center
    spread = jnp.mean(offset * offset, axis=-1, keepdims=True)
    return offset * lax.rsqrt(spread + NORM_EPSILON) * scale + shift_term


def norm_pieces(input_rows):
    center = jnp.mean(input_rows, axis=-1, keepdims=True)
    offset = input_rows - center
    spread = jnp.mean(offset * offset, axis=-1, keepdims=True)
    inverse_deviation = lax.rsqrt(spread + NORM_EPSILON)
    return (offset * inverse_deviation, inverse_deviation)


def ssm_block(tables, state, pieces):
    powers, after, kernel, rate_eff, read_out, skip_gain = tables
    input_rows, starts = pieces
    length = input_rows.shape[0]
    counts = jnp.cumsum(starts)
    places = jnp.arange(length)
    spacing = places[:, None] - places[None, :]
    inside = ((spacing >= 0) & (counts[:, None] == counts[None, :])).astype(jnp.float32)
    selector = (spacing[:, :, None] == places[None, None, :]).astype(jnp.float32)
    toeplitz = (
        jnp.einsum("tsk,kc->tsc", selector, kernel, precision=HIGHEST_PRECISION)
        * inside[:, :, None]
    )
    alive = (counts == 0).astype(jnp.float32)
    tail = (counts == counts[length - 1]).astype(jnp.float32)
    outputs = jnp.einsum("tsc,sc->tc", toeplitz, input_rows, precision=HIGHEST_PRECISION)
    outputs = outputs + alive[:, None] * jnp.einsum(
        "tcn,cn->tc", after, read_out * state, precision=HIGHEST_PRECISION
    )
    outputs = outputs + skip_gain[None] * input_rows
    fresh = (
        jnp.einsum(
            "scn,sc->cn", powers[::-1], input_rows * tail[:, None], precision=HIGHEST_PRECISION
        )
        * rate_eff
    )
    return (fresh + alive[length - 1] * after[length - 1] * state, outputs)


def local_scan(input_rows, starts, decay_rate, rate_input, read_out, skip_gain):
    length = min(128, input_rows.shape[0])
    blocks = input_rows.shape[0] // length
    steps = jnp.arange(length).astype(jnp.float32)
    powers = jnp.exp(-steps[:, None, None] * decay_rate[None])
    after = powers * jnp.exp(-decay_rate)[None]
    rate_eff = rate_input * -jnp.expm1(-decay_rate)
    kernel = jnp.einsum("kcn,cn->kc", powers, read_out * rate_eff, precision=HIGHEST_PRECISION)
    stepper = jax.checkpoint(
        partial(ssm_block, (powers, after, kernel, rate_eff, read_out, skip_gain))
    )
    start_state = jnp.zeros(decay_rate.shape, jnp.float32)
    final, outputs = lax.scan(
        stepper,
        start_state,
        (input_rows.reshape(blocks, length, -1), starts.reshape(blocks, length)),
    )
    return (outputs.reshape(input_rows.shape), final)


def carry_term(state, starts, decay_rate, read_out):
    alive = (jnp.cumsum(starts) == 0).astype(jnp.float32)
    steps = jnp.arange(1, starts.shape[0] + 1).astype(jnp.float32)
    powers = jnp.exp(-steps[:, None, None] * decay_rate[None])
    return alive[:, None] * jnp.einsum(
        "tcn,cn->tc", powers, read_out * state, precision=HIGHEST_PRECISION
    )


def shard_decay(starts, decay_rate):
    through = (jnp.sum(starts) == 0).astype(jnp.float32)
    return through * jnp.exp(-starts.shape[0] * decay_rate)


def ssm_shard(input_rows, decay_rate, rate_input, read_out, skip_gain, state, starts):
    local_out, final = local_scan(input_rows, starts, decay_rate, rate_input, read_out, skip_gain)
    outputs = local_out + carry_term(state, starts, decay_rate, read_out)
    return (outputs, final, shard_decay(starts, decay_rate))


def chain_combine(earlier, later):
    return (earlier[0] * later[0], later[0] * earlier[1] + later[1])


def gelu_back(pre, grad):
    return jax.vjp(jax.nn.gelu, pre)[1](grad)[0]


def contract_last(left, right):
    return lax.dot_general(
        left, right, (((1,), (1,)), ((), ())), preferred_element_type=jnp.float32
    )


def contract_first(left, right):
    return lax.dot_general(
        left, right, (((0,), (0,)), ((), ())), preferred_element_type=jnp.float32
    )


def local(
    layer_input,
    out_cotangent,
    seq_lengths,
    norm_gain,
    norm_bias,
    wide_weight,
    wide_bias,
    narrow_weight,
    narrow_bias,
    ssm_decay,
    ssm_input,
    ssm_output,
    ssm_skip,
    lift_weight,
    lift_bias,
    down_weight,
    down_bias,
):
    section = lax.axis_index("section")
    first_section = section == 0
    micro = layer_input.shape[0]
    shard_len = layer_input.shape[1]
    feature_width = layer_input.shape[2]
    share_width = feature_width // lax.axis_size("tensor")
    share_start = lax.axis_index("tensor") * share_width

    def column_count(values):
        return lax.dynamic_slice_in_dim(values, share_start, share_width, values.ndim - 1)

    (
        norm_scale,
        norm_shift,
        wide_mat,
        wide_add,
        narrow_mat,
        narrow_add,
        decay_rate,
        rate_input,
        read_out,
        skip_gain,
        lift_mat,
        lift_add,
        down_mat,
        down_add,
    ) = tuple(
        (
            part[0]
            for part in (
                norm_gain,
                norm_bias,
                wide_weight,
                wide_bias,
                narrow_weight,
                narrow_bias,
                ssm_decay,
                ssm_input,
                ssm_output,
                ssm_skip,
                lift_weight,
                lift_bias,
                down_weight,
                down_bias,
            )
        )
    )
    positions = lax.axis_index("dp") * shard_len + jnp.arange(shard_len, dtype=jnp.int32)
    begins = jnp.cumsum(seq_lengths, axis=1) - seq_lengths
    starts_all = jnp.sum((positions[None, :, None] == begins[:, None, :]).astype(jnp.int32), axis=2)
    state_ones = jnp.ones(decay_rate.shape, jnp.float32)
    state_zeros = jnp.zeros(decay_rate.shape, jnp.float32)

    def layer_backward(output_gradient, kept, starts):
        (
            input_rows,
            normed_low,
            wide_pre,
            narrow_pre,
            narrow_act,
            entering,
            scanned_full,
            lifted,
            gated_low,
        ) = kept
        out_low = output_gradient.astype(jnp.bfloat16)
        d_gated = contract_last(out_low, down_mat)
        lift_low = (d_gated * jax.nn.gelu(wide_pre)).astype(jnp.bfloat16)
        wide_low = gelu_back(wide_pre, d_gated * lifted).astype(jnp.bfloat16)
        d_scanned = lax.psum_scatter(
            contract_last(lift_low, lift_mat), "tensor", scatter_dimension=1, tiled=True
        )
        entry_grad = jax.vjp(
            partial(carry_term, starts=starts, decay_rate=decay_rate, read_out=read_out), entering
        )[1](d_scanned)[0]
        through = shard_decay(starts, decay_rate)
        final_grad = carried_in(
            (through, entry_grad), "dp", chain_combine, (state_ones, state_zeros)
        )[1]
        _, ssm_back = jax.vjp(
            partial(ssm_shard, starts=starts),
            narrow_act,
            decay_rate,
            rate_input,
            read_out,
            skip_gain,
            entering,
        )
        d_narrow, grad_decay, grad_input, grad_output, grad_skip, _ = ssm_back(
            (d_scanned, final_grad, entering * final_grad)
        )
        narrow_low = gelu_back(narrow_pre, d_narrow).astype(jnp.bfloat16)
        partial_normed = contract_last(wide_low, wide_mat) + contract_last(narrow_low, narrow_mat)
        standardized_input, inverse_deviation = norm_pieces(input_rows)
        normalized_gradient = lax.psum(partial_normed, "tensor")
        scaled_values = normalized_gradient * norm_scale
        first_moment = jnp.sum(scaled_values, axis=1, keepdims=True) / feature_width
        second_moment = (
            jnp.sum(scaled_values * standardized_input, axis=1, keepdims=True) / feature_width
        )
        sent_values = output_gradient + inverse_deviation * (
            scaled_values - first_moment - standardized_input * second_moment
        )
        grad_share = column_count(sent_values)
        scale_gradient = column_count(jnp.sum(normalized_gradient * standardized_input, axis=0))
        grad_shift = column_count(jnp.sum(normalized_gradient, axis=0))
        small = (scale_gradient, grad_shift, grad_decay, grad_input, grad_output, grad_skip)
        return (grad_share, sent_values, small, (out_low, lift_low, wide_low, narrow_low))

    received = jnp.zeros((shard_len, feature_width), jnp.float32)
    outputs_list = []
    kept_list = []
    for moment in range(micro + 1):
        owned = jnp.clip(moment - section, 0, micro - 1)
        starts = lax.dynamic_index_in_dim(starts_all, owned, 0, keepdims=False)
        fresh = layer_input[min(moment, micro - 1)].astype(jnp.float32)
        layer_input_rows = jnp.where(first_section, fresh, received)
        layer_normed_low = layer_norm(layer_input_rows, norm_scale, norm_shift).astype(jnp.bfloat16)
        layer_wide_pre = (
            jnp.dot(layer_normed_low, wide_mat, preferred_element_type=jnp.float32) + wide_add
        )
        layer_narrow_pre = (
            jnp.dot(layer_normed_low, narrow_mat, preferred_element_type=jnp.float32) + narrow_add
        )
        layer_narrow_act = jax.nn.gelu(layer_narrow_pre)
        local_out, final = local_scan(
            layer_narrow_act, starts, decay_rate, rate_input, read_out, skip_gain
        )
        layer_through = shard_decay(starts, decay_rate)
        layer_entering = entering_2(
            (layer_through, final), "dp", chain_combine, (state_ones, state_zeros)
        )[1]
        scanned = local_out + carry_term(layer_entering, starts, decay_rate, read_out)
        layer_scanned_full = lax.all_gather(
            scanned.astype(jnp.bfloat16), "tensor", axis=1, tiled=True
        )
        layer_lifted = (
            jnp.dot(layer_scanned_full, lift_mat, preferred_element_type=jnp.float32) + lift_add
        )
        layer_gated_low = (layer_lifted * jax.nn.gelu(layer_wide_pre)).astype(jnp.bfloat16)
        term = jnp.dot(layer_gated_low, down_mat, preferred_element_type=jnp.float32)
        layer_sent_values = layer_input_rows + lax.psum(term, "tensor") + down_add
        output = column_count(layer_sent_values)
        output, sent_values, kept = (
            output,
            layer_sent_values,
            (
                layer_input_rows,
                layer_normed_low,
                layer_wide_pre,
                layer_narrow_pre,
                layer_narrow_act,
                layer_entering,
                layer_scanned_full,
                layer_lifted,
                layer_gated_low,
            ),
        )
        outputs_list.append(output)
        kept_list.append(kept)
        if moment < micro:
            received = passed_along(sent_values, "section", 1)
    outputs_all = jnp.stack(outputs_list)
    kept_all = tuple((jnp.stack(group) for group in zip(*kept_list)))
    received = jnp.zeros((shard_len, feature_width), jnp.float32)
    grads_list = []
    small_list = []
    acts_list = []
    for moment in range(micro + 1):
        owned = jnp.clip(moment - 1 + section, 0, micro - 1)
        forward_at = jnp.clip(moment - 1 + 2 * section, 0, micro)
        kept = tuple(
            (lax.dynamic_index_in_dim(group, forward_at, 0, keepdims=False) for group in kept_all)
        )
        starts = lax.dynamic_index_in_dim(starts_all, owned, 0, keepdims=False)
        fresh = out_cotangent[min(moment, micro - 1)].astype(jnp.float32)
        grad_share, sent_values, small, acts = layer_backward(
            jnp.where(first_section, received, fresh), kept, starts
        )
        grads_list.append(grad_share)
        small_list.append(small)
        acts_list.append(acts)
        if moment < micro:
            received = passed_along(sent_values.astype(jnp.bfloat16), "section", -1).astype(
                sent_values.dtype
            )
    grads_all = jnp.stack(grads_list)
    small_all = tuple((jnp.stack(group) for group in zip(*small_list)))
    acts_all = tuple((jnp.stack(group) for group in zip(*acts_list)))
    totals = ()
    for micro_index in range(micro):
        back_at = micro_index + 1 - section
        forward_at = micro_index + section
        normed_low = lax.dynamic_index_in_dim(kept_all[1], forward_at, 0, keepdims=False)
        scanned_full = lax.dynamic_index_in_dim(kept_all[6], forward_at, 0, keepdims=False)
        gated_low = lax.dynamic_index_in_dim(kept_all[8], forward_at, 0, keepdims=False)
        out_low, lift_low, wide_low, narrow_low = tuple(
            (lax.dynamic_index_in_dim(group, back_at, 0, keepdims=False) for group in acts_all)
        )
        scale_gradient, grad_shift, grad_decay, grad_input, grad_output, grad_skip = tuple(
            (lax.dynamic_index_in_dim(group, back_at, 0, keepdims=False) for group in small_all)
        )
        terms = (
            scale_gradient,
            grad_shift,
            contract_first(normed_low, wide_low),
            jnp.sum(wide_low.astype(jnp.float32), axis=0),
            contract_first(normed_low, narrow_low),
            jnp.sum(narrow_low.astype(jnp.float32), axis=0),
            grad_decay,
            grad_input,
            grad_output,
            grad_skip,
            contract_first(scanned_full, lift_low),
            jnp.sum(lift_low.astype(jnp.float32), axis=0),
            contract_first(gated_low, out_low),
            jnp.sum(out_low.astype(jnp.float32), axis=0),
        )
        totals = (
            terms
            if micro_index == 0
            else tuple((left + right for left, right in zip(totals, terms)))
        )
    totals = jax.tree.map(
        lambda part: part.astype(jnp.float32),
        lax.psum_scatter(shortened(totals), "dp", scatter_dimension=0, tiled=True),
    )
    section_output = lax.dynamic_slice_in_dim(outputs_all, section, micro, 0)[None]
    input_grad = lax.dynamic_slice_in_dim(grads_all, 1 - section, micro, 0)[None]
    return (section_output, input_grad) + tuple((total[None] for total in totals))


def solution(mesh):
    placed = (
        P(None, "dp", None),
        P(None, "dp", None),
        P(),
        P("section", None),
        P("section", None),
        P("section", None, "tensor"),
        P("section", "tensor"),
        P("section", None, "tensor"),
        P("section", "tensor"),
        P("section", "tensor", None),
        P("section", "tensor", None),
        P("section", "tensor", None),
        P("section", "tensor"),
        P("section", None, "tensor"),
        P("section", "tensor"),
        P("section", "tensor", None),
        P("section", None),
    )
    return jax.shard_map(
        local,
        mesh=mesh,
        in_specs=placed,
        out_specs=(
            P("section", None, "dp", "tensor"),
            P("section", None, "dp", "tensor"),
            P("section", ("tensor", "dp")),
            P("section", ("tensor", "dp")),
            P("section", "dp", "tensor"),
            P("section", ("tensor", "dp")),
            P("section", "dp", "tensor"),
            P("section", ("tensor", "dp")),
            P("section", ("tensor", "dp"), None),
            P("section", ("tensor", "dp"), None),
            P("section", ("tensor", "dp"), None),
            P("section", ("tensor", "dp")),
            P("section", "dp", "tensor"),
            P("section", ("tensor", "dp")),
            P("section", ("tensor", "dp"), None),
            P("section", "dp"),
        ),
        check_vma=False,
    )
```

profile of v0, /device:TPU:0, one launch (start us, length us, event | category | flops | bytes accessed | tf_op | source)
XLA Modules:
  0.0 1449.3 jit_solution(12180271518291048875)
XLA Ops:
  17.0 10.6 all_gather.69
  50.0 49.4 %while.261 = (s32[]{:T(128)}, f32[128,64]{1,0:T(8,128)}, f32[2,128,128]{2,1,0:T(8,128)}, f32[2,128,128]{2,1,0:T(8,128)S(1)}, s32[2,128]{1,0:T(2,128)}, /*index=5...) while((s32[]{:T(128)}, f32[128,64]{1,0:T(8,128)}, ...), condition=%wide.region_6.7_spmd.clone, body=%wide.region_4.6_spmd.clone.sunk | while | flops 3235062272 | bytes 15409427 | solution.py:114
  65.0 8.9 multiply_reduce_fusion.78
  89.7 8.9 multiply_reduce_fusion.78
  99.4 9.9 all-gather
  122.2 14.0 all_gather.72
  144.5 50.6 %all-reduce.18.cloned.1.call-done = f32[256,1024]{1,0:T(8,128)} async-done(((f32[256,1024]{1,0:T(8,128)}), f32[256,1024]{1,0:T(8,128)}) %all-reduce.18.cloned.1.call-update) | async-done | bytes 1048592 | tf_op jit(solution)/shard_map/psum | solution.py:322
  200.7 9.8 all_gather.73
  217.7 44.0 %while.263 = (s32[]{:T(128)}, f32[128,64]{1,0:T(8,128)S(1)}, f32[2,128,128]{2,1,0:T(8,128)}, f32[2,128,128]{2,1,0:T(8,128)S(1)}, s32[2,128]{1,0:T(2,128)}, /*ind...) while((s32[]{:T(128)}, f32[128,64]{1,0:T(8,128)S(1)}, ...), condition=%wide.region_17.18_spmd.clone, body=%wide.region_15.17_spmd.clone.sunk | while | flops 3235062272 | bytes 15151407 | solution.py:114
  229.1 9.8 multiply_reduce_fusion.81
  251.1 9.8 multiply_reduce_fusion.81
  261.7 8.8 all-gather.1
  279.2 12.8 all_gather.76
  298.0 7.9 rev.68
  306.8 8.8 all_gather.77
  315.7 31.6 %all-reduce.20.cloned.1.call-done = f32[256,1024]{1,0:T(8,128)} async-done(((f32[256,1024]{1,0:T(8,128)}), f32[256,1024]{1,0:T(8,128)}) %all-reduce.20.cloned.1.call-update) | async-done | bytes 1048592 | tf_op jit(solution)/shard_map/psum | solution.py:322
  350.9 9.3 all_gather.81
  370.6 44.2 %while.265 = (s32[]{:T(128)}, f32[128,64]{1,0:T(8,128)}, f32[2,128,128]{2,1,0:T(8,128)}, f32[2,128,128]{2,1,0:T(8,128)S(1)}, s32[2,128]{1,0:T(2,128)}, /*index=5...) while((s32[]{:T(128)}, f32[128,64]{1,0:T(8,128)}, ...), condition=%wide.region_28.29_spmd.clone, body=%wide.region_26.28_spmd.clone.sunk | while | flops 3235062272 | bytes 15409455 | solution.py:114
  382.1 9.8 multiply_reduce_fusion.84
  404.2 9.8 multiply_reduce_fusion.84
  414.8 8.9 all-gather.2
  430.1 12.8 all_gather.80
  451.9 18.2 %while.268 = (s32[]{:T(128)}, f32[128,64]{1,0:T(8,128)S(1)}, f32[2,128,64]{2,1,0:T(8,128)}, f32[2,128,128]{2,1,0:T(8,128)S(1)}, s32[2,128]{1,0:T(2,128)S(1)}, /*...) while((s32[]{:T(128)}, f32[128,64]{1,0:T(8,128)S(1)}, ...), condition=%wide.region_45.46_spmd.clone, body=%wide.region_43.45_spmd.clone.sunk | while | flops 2171013 | bytes 4691098 | solution.py:114
  490.2 126.1 %while.273 = (s32[]{:T(128)}, f32[128,128]{1,0:T(8,128)}, f32[128,64]{1,0:T(8,128)S(1)}, f32[128,128,64]{2,1,0:T(8,128)}, f32[128]{0:T(128)S(1)}, /*index=5*/f32...) while((s32[]{:T(128)}, f32[128,128]{1,0:T(8,128)}, ...), condition=%wide.region_49.50_spmd.clone.clone.clone, body=%wide.region_46.49_spmd.clone.clone.clone.sunk | while | flops 6474253312 | bytes 67809712 | solution.py:114
  499.7 7.6 multiply_reduce_fusion.91
  524.4 9.4 select_add_fusion.12
  538.5 11.2 fusion.559
  559.7 7.6 multiply_reduce_fusion.91
  584.3 11.8 select_add_fusion.12
  596.1 8.0 fusion.561
  604.1 11.2 fusion.559
  626.4 45.7 %all-reduce.22.cloned.1.call-done = f32[256,1024]{1,0:T(8,128)} async-done(((f32[256,1024]{1,0:T(8,128)}), f32[256,1024]{1,0:T(8,128)}) %all-reduce.22.cloned.1.call-update) | async-done | bytes 1048592 | tf_op jit(solution)/shard_map/psum | solution.py:275
  680.6 8.8 all_gather.84
  695.2 16.9 %while.270 = (s32[]{:T(128)}, f32[128,64]{1,0:T(8,128)S(1)}, f32[2,128,64]{2,1,0:T(8,128)S(1)}, f32[2,128,128]{2,1,0:T(8,128)S(1)}, s32[2,128]{1,0:T(2,128)S(1)}...) while((s32[]{:T(128)}, f32[128,64]{1,0:T(8,128)S(1)}, ...), condition=%wide.region_63.64_spmd.clone, body=%wide.region_61.63_spmd.clone.sunk | while | flops 2171013 | bytes 4723358 | solution.py:114
  718.2 8.2 all-gather.4
  730.9 127.1 %while.274 = (s32[]{:T(128)}, f32[128,128]{1,0:T(8,128)}, f32[128,64]{1,0:T(8,128)S(1)}, f32[128,128,64]{2,1,0:T(8,128)}, f32[128]{0:T(128)}, /*index=5*/f32[128...) while((s32[]{:T(128)}, f32[128,128]{1,0:T(8,128)}, ...), condition=%wide.region_67.68_spmd.clone.clone.clone, body=%wide.region_64.67_spmd.clone.clone.clone.sunk | while | flops 6474253312 | bytes 66761088 | solution.py:114
  739.6 7.6 multiply_reduce_fusion.95
  764.8 9.4 select_add_fusion.13
  779.4 11.2 fusion.566
  799.7 7.6 multiply_reduce_fusion.95
  824.8 11.8 select_add_fusion.13
  836.6 8.0 fusion.568
  845.8 11.2 fusion.566
  864.9 48.9 %all-reduce.24.cloned.1.call-done = f32[256,1024]{1,0:T(8,128)} async-done(((f32[256,1024]{1,0:T(8,128)}), f32[256,1024]{1,0:T(8,128)}) %all-reduce.24.cloned.1.call-update) | async-done | bytes 1048592 | tf_op jit(solution)/shard_map/psum | solution.py:275
  921.6 9.0 all_gather.87
  940.4 18.2 %while.272 = (s32[]{:T(128)}, f32[128,64]{1,0:T(8,128)S(1)}, f32[2,128,64]{2,1,0:T(8,128)}, f32[2,128,128]{2,1,0:T(8,128)S(1)}, s32[2,128]{1,0:T(2,128)S(1)}, /*...) while((s32[]{:T(128)}, f32[128,64]{1,0:T(8,128)S(1)}, ...), condition=%wide.region_81.82_spmd.clone, body=%wide.region_79.81_spmd.clone.sunk | while | flops 2171013 | bytes 4691098 | solution.py:114
  979.8 8.2 all-gather.5
  992.6 125.8 %while.275 = (s32[]{:T(128)}, f32[128,128]{1,0:T(8,128)}, f32[128,64]{1,0:T(8,128)S(1)}, f32[128,128,64]{2,1,0:T(8,128)}, f32[128]{0:T(128)S(1)}, /*index=5*/f32...) while((s32[]{:T(128)}, f32[128,128]{1,0:T(8,128)}, ...), condition=%wide.region_85.86_spmd.clone.clone.clone, body=%wide.region_82.85_spmd.clone.clone.clone.sunk | while | flops 6474253312 | bytes 66498908 | solution.py:114
  1001.2 8.6 multiply_reduce_fusion.99
  1026.8 9.4 select_add_fusion.14
  1040.8 11.2 fusion.573
  1061.0 8.6 multiply_reduce_fusion.99
  1086.6 11.8 select_add_fusion.14
  1098.4 7.9 fusion.575
  1106.4 11.2 fusion.573
  1118.4 8.9 multiply_reduce_fusion.29
  1127.7 16.6 %multiply_reduce_fusion.37 = (f32[128,64]{1,0:T(8,128)S(1)}, f32[128,64]{1,0:T(8,128)S(1)}, f32[128,64]{1,0:T(8,128)S(1)}, f32[128,64]{1,0:T(8,128)S(1)}, f32[128,64]{1,0:T(8,128)S(1)}, /*index=5*/f32[128,64]{1,0:T(8,128)S(1)}) fusion(f32[128,128,64]{2,1,0:T(8,128)} %get-tuple-element.2180, f32[128,64]{1,0:T(8,128)S(1)} %copy-done.81, ...), kind=kLoop, calls=%fused_computation.298 | loop fusion | flops 29310976 | bytes 25657856 | tf_op jit(solution)/shard_map/transpose(jvp())/reduce_sum | solution.py:107
  1208.2 18.4 %reduce-scatter.31.cloned.1.call-done = bf16[32,64]{1,0:T(8,128)(2,1)} async-done(((bf16[128,64]{1,0:T(8,128)(2,1)}), bf16[32,64]{1,0:T(8,128)(2,1)}) %reduce-scatter.31.cloned.1.call-update) | async-done | bytes 4112
  1228.1 26.2 %reduce-scatter.25.cloned.1.call-done = bf16[256,128]{1,0:T(8,128)(2,1)} async-done(((bf16[1024,128]{1,0:T(8,128)(2,1)}), bf16[256,128]{1,0:T(8,128)(2,1)}) %reduce-scatter.25.cloned.1.call-update) | async-done | bytes 65552 | tf_op jit(solution)/shard_map/reduce_scatter | solution.py:406
  1255.8 28.0 %reduce-scatter.27.cloned.1.call-done = bf16[128,768]{1,0:T(8,128)(2,1)} async-done(((bf16[512,768]{1,0:T(8,128)(2,1)}), bf16[128,768]{1,0:T(8,128)(2,1)}) %reduce-scatter.27.cloned.1.call-update) | async-done | bytes 196624 | tf_op jit(solution)/shard_map/reduce_scatter | solution.py:406
  1285.5 87.8 %all-reduce.26.cloned.1.call-done = (f32[256,1024]{1,0:T(8,128)}, f32[256,1024]{1,0:T(8,128)}) async-done(((f32[256,1024]{1,0:T(8,128)}, f32[256,1024]{1,0:T(8,128)}), (f32[256,1024]{1,0:T(8,128)}, f32[256,1024]{1,0:T(8,128)})) %all-reduce.26.cloned.1.call-update) | async-done | bytes 2097168 | tf_op jit(solution)/shard_map/psum | solution.py:322
  1376.4 10.1 all-reduce.11
  1394.9 11.5 reduce-scatter.29.cloned.1.call-done
  1408.3 32.1 %reduce-scatter.23.cloned.1.call-done = bf16[256,768]{1,0:T(8,128)(2,1)} async-done(((bf16[1024,768]{1,0:T(8,128)(2,1)}), bf16[256,768]{1,0:T(8,128)(2,1)}) %reduce-scatter.23.cloned.1.call-update) | async-done | bytes 393232 | tf_op jit(solution)/shard_map/reduce_scatter | solution.py:406
  (1122 shorter events, 620.5 us)
Async XLA Ops:
  7.2 135.6 %copy-start = (bf16[1,768,1024]{2,1,0:T(8,128)(2,1)S(1)}, bf16[1,768,1024]{2,1,0:T(8,128)(2,1)}, u32[]{:S(2)}) copy-start(bf16[1,768,1024]{2,1,0:T(8,128)(2,1)} %param.62) | copy-start | bytes 4718596
  7.2 187.9 %all-reduce.18.cloned.1.call-start = ((), (), s32[]{:S(2)}) async-start(), calls=%async_computation.10 | async-start | bytes 2097152 | tf_op jit(solution)/shard_map/psum | solution.py:322
  50.0 87.6 %copy-start.11 = (bf16[1,1024,768]{2,1,0:T(8,128)(2,1)S(1)}, bf16[1,1024,768]{2,1,0:T(8,128)(2,1)}, u32[]{:S(2)}) copy-start(bf16[1,1024,768]{2,1,0:T(8,128)(2,1)} %param.52) | copy-start | bytes 4718596
  136.9 76.5 %copy-start.170 = (f32[768]{0:T(1024)}, f32[768]{0:T(1024)S(1)}, u32[]{:S(2)}) copy-start(f32[768]{0:T(1024)S(1)} %reduce.55) | copy-start | bytes 9220
  137.6 75.1 %copy-start.168 = (f32[768]{0:T(1024)}, f32[768]{0:T(1024)S(1)}, u32[]{:S(2)}) copy-start(f32[768]{0:T(1024)S(1)} %reduce.54) | copy-start | bytes 9220
  137.6 75.1 %copy-start.92 = (f32[1,1024]{1,0:T(1,128)S(1)}, f32[1,1024]{1,0:T(1,128)}, u32[]{:S(2)}) copy-start(f32[1,1024]{1,0:T(1,128)} %param.50) | copy-start | bytes 12292
  137.6 75.1 %copy-start.121 = (f32[1,1024]{1,0:T(1,128)S(1)}, f32[1,1024]{1,0:T(1,128)}, u32[]{:S(2)}) copy-start(f32[1,1024]{1,0:T(1,128)} %param.51) | copy-start | bytes 12292
  140.2 72.8 %copy-start.14 = (bf16[1,1024,128]{2,1,0:T(8,128)(2,1)S(1)}, bf16[1,1024,128]{2,1,0:T(8,128)(2,1)}, u32[]{:S(2)}) copy-start(bf16[1,1024,128]{2,1,0:T(8,128)(2,1)} %param.54) | copy-start | bytes 786436
  140.2 72.8 %copy-start.154 = (f32[1,128]{1,0:T(1,128)S(1)}, f32[1,128]{1,0:T(1,128)}, u32[]{:S(2)}) copy-start(f32[1,128]{1,0:T(1,128)} %param.55) | copy-start | bytes 1540
  144.4 202.9 %all-reduce.20.cloned.1.call-start = ((), (), s32[]{:S(2)}) async-start(), calls=%async_computation.11 | async-start | bytes 2097152 | tf_op jit(solution)/shard_map/psum | solution.py:322
  196.7 14.6 %collective-permute-start = (f32[256,1024]{1,0:T(8,128)S(1)}, f32[256,1024]{1,0:T(8,128)}, u32[]{:S(2)}, u32[]{:S(2)}) collective-permute-start(f32[256,1024]{1,0:T(8,128)S(1)} %fusion.175), channel_id=1, source_target_pairs={{0,16},{1,17},{2,18},{3,19},{4,20},{5,21},{6,22},{7,23},{8,24},{9,... | collective-permute-start | bytes 3145736 | tf_op jit(solution)/shard_map/ppermute | solution.py:51
  212.5 259.4 %copy-start.5 = (f32[256,1024]{1,0:T(8,128)}, f32[256,1024]{1,0:T(8,128)S(1)}, u32[]{:S(2)}) copy-start(f32[256,1024]{1,0:T(8,128)S(1)} %get-tuple-element.4856) | copy-start | bytes 3145732
  297.8 177.6 %reduce-scatter.17.cloned.1.call-start = ((), (), s32[]{:S(2)}) async-start(), calls=%async_computation.12 | async-start | bytes 655360 | tf_op jit(solution)/shard_map/reduce_scatter | solution.py:250
  305.9 61.5 %copy-start.155 = (f32[1,128]{1,0:T(1,128)S(1)}, f32[1,128]{1,0:T(1,128)}, u32[]{:S(2)}) copy-start(f32[1,128]{1,0:T(1,128)} %param.55) | copy-start | bytes 1540
  305.9 61.8 %copy-start.171 = (f32[768]{0:T(1024)S(1)}, f32[768]{0:T(1024)}, u32[]{:S(2)}) copy-start(f32[768]{0:T(1024)} %copy-done.170) | copy-start | bytes 9220
  348.9 16.1 %collective-permute-start.1 = (f32[256,1024]{1,0:T(8,128)S(1)}, f32[256,1024]{1,0:T(8,128)S(1)}, u32[]{:S(2)}, u32[]{:S(2)}) collective-permute-start(f32[256,1024]{1,0:T(8,128)S(1)} %add_add_fusion), channel_id=1, source_target_pairs={{0,16},{1,17},{2,18},{3,19},{4,20},{5,21},{6,22},{7,23},{8,24},{9,... | collective-permute-start | bytes 3145736 | tf_op jit(solution)/shard_map/ppermute | solution.py:51
  370.6 72.3 %copy-start.169 = (f32[768]{0:T(1024)S(1)}, f32[768]{0:T(1024)}, u32[]{:S(2)}) copy-start(f32[768]{0:T(1024)} %copy-done.168) | copy-start | bytes 9220
  449.3 222.7 %all-reduce.22.cloned.1.call-start = ((), (), s32[]{:S(2)}) async-start(), calls=%async_computation.13 | async-start | bytes 2097152 | tf_op jit(solution)/shard_map/psum | solution.py:275
  490.1 128.9 %copy-start.15 = (bf16[1,1024,128]{2,1,0:T(8,128)(2,1)S(1)}, bf16[1,1024,128]{2,1,0:T(8,128)(2,1)}, u32[]{:S(2)}) copy-start(bf16[1,1024,128]{2,1,0:T(8,128)(2,1)} %param.54) | copy-start | bytes 786436
  616.3 62.5 %copy-start.39 = (f32[128,64]{1,0:T(8,128)}, f32[128,64]{1,0:T(8,128)S(1)}, u32[]{:S(2)}) copy-start(f32[128,64]{1,0:T(8,128)S(1)} %get-tuple-element.2170) | copy-start | bytes 98308
  616.3 62.5 %copy-start.41 = (f32[128,64]{1,0:T(8,128)}, f32[128,64]{1,0:T(8,128)S(1)}, u32[]{:S(2)}) copy-start(f32[128,64]{1,0:T(8,128)S(1)} %get-tuple-element.2182) | copy-start | bytes 98308
  616.3 62.5 %copy-start.137 = (f32[128]{0:T(128)}, f32[128]{0:T(128)S(1)}, u32[]{:S(2)}) copy-start(f32[128]{0:T(128)S(1)} %get-tuple-element.2185) | copy-start | bytes 1540
  619.3 60.9 %copy-start.160 = (s32[1,256]{1,0:T(1,128)S(1)}, s32[1,256]{1,0:T(1,128)}, u32[]{:S(2)}) copy-start(s32[1,256]{1,0:T(1,128)} %get-tuple-element.4958) | copy-start | bytes 3076
  619.4 61.3 %copy-start.131 = (bf16[1,128,64]{1,2,0:T(8,128)(2,1)S(1)}, bf16[1,128,64]{1,2,0:T(8,128)(2,1)}, u32[]{:S(2)}) copy-start(bf16[1,128,64]{1,2,0:T(8,128)(2,1)} %get-tuple-element.4952) | copy-start | bytes 49156
  622.5 93.0 %reduce-scatter.19.cloned.1.call-start = ((), (), s32[]{:S(2)}) async-start(), calls=%async_computation.14 | async-start | bytes 655360 | tf_op jit(solution)/shard_map/reduce_scatter | solution.py:250
  626.3 66.8 %copy-start.153 = (f32[256]{0:T(256)}, f32[256]{0:T(256)S(1)}, u32[]{:S(2)}) copy-start(f32[256]{0:T(256)S(1)} %broadcast_multiply_fusion.6) | copy-start | bytes 3076
  626.3 66.8 %copy-start.146 = (f32[256]{0:T(256)}, f32[256]{0:T(256)S(1)}, u32[]{:S(2)}) copy-start(f32[256]{0:T(256)S(1)} %broadcast_multiply_fusion.9) | copy-start | bytes 3076
  626.4 67.6 %copy-start.21 = (bf16[1,512,768]{2,1,0:T(8,128)(2,1)S(1)}, bf16[1,512,768]{2,1,0:T(8,128)(2,1)}, u32[]{:S(2)}) copy-start(bf16[1,512,768]{2,1,0:T(8,128)(2,1)} %param.60) | copy-start | bytes 2359300
  678.8 10.8 collective-permute-start.2
  695.1 218.7 %all-reduce.24.cloned.1.call-start = ((), (), s32[]{:S(2)}) async-start(), calls=%async_computation.15 | async-start | bytes 2097152 | tf_op jit(solution)/shard_map/psum | solution.py:275
  730.9 130.0 %copy-start.16 = (bf16[1,1024,128]{2,1,0:T(8,128)(2,1)S(1)}, bf16[1,1024,128]{2,1,0:T(8,128)(2,1)}, u32[]{:S(2)}) copy-start(bf16[1,1024,128]{2,1,0:T(8,128)(2,1)} %param.54) | copy-start | bytes 786436
  730.9 133.6 %copy-start.159 = (s32[1,256]{1,0:T(1,128)S(1)}, s32[1,256]{1,0:T(1,128)}, u32[]{:S(2)}) copy-start(s32[1,256]{1,0:T(1,128)} %get-tuple-element.4956) | copy-start | bytes 3076
  730.9 134.1 %copy-start.173 = (f32[256]{0:T(256)S(1)}, f32[256]{0:T(256)}, u32[]{:S(2)}) copy-start(f32[256]{0:T(256)} %get-tuple-element.4490) | copy-start | bytes 3076
  730.9 183.0 %copy-start.94 = (f32[1,1024]{1,0:T(1,128)S(1)}, f32[1,1024]{1,0:T(1,128)}, u32[]{:S(2)}) copy-start(f32[1,1024]{1,0:T(1,128)} %param.50) | copy-start | bytes 12292
  730.9 182.9 %copy-start.147 = (f32[256]{0:T(256)S(1)}, f32[256]{0:T(256)}, u32[]{:S(2)}) copy-start(f32[256]{0:T(256)} %copy-done.146) | copy-start | bytes 3076
  858.0 76.0 %copy-start.44 = (f32[128,64]{1,0:T(8,128)}, f32[128,64]{1,0:T(8,128)S(1)}, u32[]{:S(2)}) copy-start(f32[128,64]{1,0:T(8,128)S(1)} %get-tuple-element.6738) | copy-start | bytes 98308
  858.0 76.0 %copy-start.45 = (f32[128,64]{1,0:T(8,128)}, f32[128,64]{1,0:T(8,128)S(1)}, u32[]{:S(2)}) copy-start(f32[128,64]{1,0:T(8,128)S(1)} %get-tuple-element.6742) | copy-start | bytes 98308
  858.0 63.6 %copy-start.130 = (bf16[1,128,64]{1,2,0:T(8,128)(2,1)S(1)}, bf16[1,128,64]{1,2,0:T(8,128)(2,1)}, u32[]{:S(2)}) copy-start(bf16[1,128,64]{1,2,0:T(8,128)(2,1)} %get-tuple-element.4953) | copy-start | bytes 49156
  858.1 72.6 %copy-start.6 = (f32[256,1024]{1,0:T(8,128)S(1)}, f32[256,1024]{1,0:T(8,128)}, u32[]{:S(2)}) copy-start(f32[256,1024]{1,0:T(8,128)} %copy-done.5) | copy-start | bytes 3145732
  858.1 72.6 %copy-start.122 = (f32[1,1024]{1,0:T(1,128)S(1)}, f32[1,1024]{1,0:T(1,128)}, u32[]{:S(2)}) copy-start(f32[1,1024]{1,0:T(1,128)} %param.51) | copy-start | bytes 12292
  858.1 72.6 %copy-start.143 = (f32[256]{0:T(256)S(1)}, f32[256]{0:T(256)}, u32[]{:S(2)}) copy-start(f32[256]{0:T(256)} %copy-done.142) | copy-start | bytes 3076
  858.1 72.6 %copy-start.149 = (f32[256]{0:T(256)S(1)}, f32[256]{0:T(256)}, u32[]{:S(2)}) copy-start(f32[256]{0:T(256)} %copy-done.148) | copy-start | bytes 3076
  864.4 112.6 %reduce-scatter.21.cloned.1.call-start = ((), (), s32[]{:S(2)}) async-start(), calls=%async_computation.16 | async-start | bytes 655360 | tf_op jit(solution)/shard_map/reduce_scatter | solution.py:250
  920.1 11.6 collective-permute-start.3
  939.6 265.7 %reduce-scatter.35.cloned.1.call-start = ((), (), s32[]{:S(2)}) async-start(), calls=%async_computation.23 | async-start | bytes 40960
  992.6 125.9 %copy-start.81 = (f32[128,64]{1,0:T(8,128)S(1)}, f32[128,64]{1,0:T(8,128)}, u32[]{:S(2)}) copy-start(f32[128,64]{1,0:T(8,128)} %copy-done.80) | copy-start | bytes 98308
  992.6 125.9 %copy-start.125 = (f32[128,128]{1,0:T(8,128)S(1)}, f32[128,128]{1,0:T(8,128)}, u32[]{:S(2)}) copy-start(f32[128,128]{1,0:T(8,128)} %get-tuple-element.2171) | copy-start | bytes 196612
  992.6 134.9 %copy-start.100 = (f32[128,64]{1,0:T(8,128)S(1)}, f32[128,64]{1,0:T(8,128)}, u32[]{:S(2)}) copy-start(f32[128,64]{1,0:T(8,128)} %copy-done.99) | copy-start | bytes 98308
  1151.6 55.1 %reduce-scatter.33.cloned.1.call-start = ((), (), s32[]{:S(2)}) async-start(), calls=%async_computation.22 | async-start | bytes 40960
  1155.3 71.4 %reduce-scatter.31.cloned.1.call-start = ((), (), s32[]{:S(2)}) async-start(), calls=%async_computation.21 | async-start | bytes 40960
  1156.9 97.5 %reduce-scatter.25.cloned.1.call-start = ((), (), s32[]{:S(2)}) async-start(), calls=%async_computation.18 | async-start | bytes 327680 | tf_op jit(solution)/shard_map/reduce_scatter | solution.py:406
  1161.5 122.4 %reduce-scatter.27.cloned.1.call-start = ((), (), s32[]{:S(2)}) async-start(), calls=%async_computation.19 | async-start | bytes 983040 | tf_op jit(solution)/shard_map/reduce_scatter | solution.py:406
  1166.7 206.6 %all-reduce.26.cloned.1.call-start = ((), (), s32[]{:S(2)}) async-start(), calls=%async_computation.24 | async-start | bytes 4194304 | tf_op jit(solution)/shard_map/psum | solution.py:322
  1173.3 233.0 %reduce-scatter.29.cloned.1.call-start = ((), (), s32[]{:S(2)}) async-start(), calls=%async_computation.20 | async-start | bytes 1966080 | tf_op jit(solution)/shard_map/reduce_scatter | solution.py:406
  1179.3 261.1 %reduce-scatter.23.cloned.1.call-start = ((), (), s32[]{:S(2)}) async-start(), calls=%async_computation.17 | async-start | bytes 1966080 | tf_op jit(solution)/shard_map/reduce_scatter | solution.py:406
  1198.4 174.9 %copy-start.95 = (f32[1,1024]{1,0:T(1,128)S(1)}, f32[1,1024]{1,0:T(1,128)}, u32[]{:S(2)}) copy-start(f32[1,1024]{1,0:T(1,128)} %param.50) | copy-start | bytes 12292
  1201.0 175.3 %copy-start.165 = (f32[256]{0:T(256)S(1)}, f32[256]{0:T(256)}, u32[]{:S(2)}) copy-start(f32[256]{0:T(256)} %dynamic_slice.481) | copy-start | bytes 3076
  1201.0 175.3 %copy-start.167 = (f32[256]{0:T(256)S(1)}, f32[256]{0:T(256)}, u32[]{:S(2)}) copy-start(f32[256]{0:T(256)} %dynamic_slice.482) | copy-start | bytes 3076
  1201.0 175.3 %copy-start.164 = (f32[256]{0:T(256)S(1)}, f32[256]{0:T(256)}, u32[]{:S(2)}) copy-start(f32[256]{0:T(256)} %dynamic_slice.486) | copy-start | bytes 3076
  1201.0 175.3 %copy-start.166 = (f32[256]{0:T(256)S(1)}, f32[256]{0:T(256)}, u32[]{:S(2)}) copy-start(f32[256]{0:T(256)} %dynamic_slice.487) | copy-start | bytes 3076
  1201.1 189.7 %copy-start.152 = (f32[256]{0:T(256)S(1)}, f32[256]{0:T(256)}, u32[]{:S(2)}) copy-start(f32[256]{0:T(256)} %add_rsqrt_fusion) | copy-start | bytes 3076
  1201.1 189.7 %copy-start.157 = (f32[256]{0:T(256)S(1)}, f32[256]{0:T(256)}, u32[]{:S(2)}) copy-start(f32[256]{0:T(256)} %dynamic-slice.14) | copy-start | bytes 3076
  1201.7 192.3 %copy-start.70 = (f32[1,256,256]{2,1,0:T(8,128)S(1)}, f32[1,256,256]{2,1,0:T(8,128)}, u32[]{:S(2)}) copy-start(f32[1,256,256]{2,1,0:T(8,128)} %dynamic-slice_bitcast_fusion.15) | copy-start | bytes 786436
  1203.5 190.5 %copy-start.71 = (f32[1,256,256]{2,1,0:T(8,128)S(1)}, f32[1,256,256]{2,1,0:T(8,128)}, u32[]{:S(2)}) copy-start(f32[1,256,256]{2,1,0:T(8,128)} %dynamic-slice_bitcast_fusion.14) | copy-start | bytes 786436
  (162 other events, 2256.3 us)
Sparse Core Ops, SparseCore 0:
  144.6 50.5 all-reduce.17
  297.9 49.3 all-reduce.19
  449.5 19.2 reduce-scatter.16
  622.7 49.3 all-reduce.21
  695.3 20.1 reduce-scatter.18
  864.6 49.2 all-reduce.23
  939.7 20.2 reduce-scatter.20
  1151.8 22.1 reduce-scatter.34
  1176.9 23.5 reduce-scatter.32
  1203.0 23.5 reduce-scatter.30
  1230.2 24.0 reduce-scatter.24
  1257.7 26.1 reduce-scatter.26
  1286.2 87.0 all-reduce.25
  1376.4 29.8 reduce-scatter.28
  1409.5 30.9 reduce-scatter.22
where the time goes:
time: 1470 us; the launch traced here: 1450 us
  other arithmetic  518 us (35%)
  waiting for transfers between devices  384 us (26%)
  matrix products  228 us (16%)
  blocking collectives  158 us (11%)
  local copies, waits for them, and re-layouts  122 us (8%)
  between operations  23.6 us (2%)
    dot_general x18, matrix products, ssm_block(): jnp.einsum('tsk,kc->tsc', selector, kernel, precision=HIGHEST_PRECISION)  172 us
    psum x3, waiting for transfers between devices, local(): layer_sent_values = layer_input_rows + lax.psum(term, 'tensor') + down_add  170 us
    add_any x18, other arithmetic, local_scan(): lax.scan(stepper, start_state, (input_rows.reshape(blocks, length, -1), s...  103 us
    reduce_scatter x4, waiting for transfers between devices, local(): lax.psum_scatter(shortened(totals), 'dp', scatter_dimension=0, tiled=True)  97.8 us
    psum x2, waiting for transfers between devices, layer_backward(): normalized_gradient = lax.psum(partial_normed, 'tensor')  94.6 us
    dot_general x12, other arithmetic, ssm_block(): jnp.einsum('tcn,cn->tc', after, read_out * state, precision=HIGHEST_PRECI...  65.1 us
    all_gather x6, blocking collectives, entering_2(): pieces = jax.tree.map(lambda part: lax.all_gather(part, axis), value)  56.8 us
    all_gather x6, blocking collectives, carried_in(): lax.all_gather(part.astype(kind), axis)  51 us
  transfers between devices with their start and end apart: 19, of which 11 were waited for; matrix products, arithmetic and copies ran while one was open for 12% of the time, Pallas kernels for 0%

commit v1 on v0

v1 whole, which is shorter than its diff:
```python
from functools import partial

import jax
import jax.numpy as jnp
from jax import lax
from jax.experimental import pallas as pl
from jax.experimental.pallas import tpu as pltpu
from jax.sharding import PartitionSpec as P

F32, BF16 = jnp.float32, jnp.bfloat16
NORM_EPSILON = 1e-05
LANES = 128
GELU_SCALE, GELU_CUBE = 0.7978845608028654, 0.044715
GAIN, SHIFT, DOWN_B, WIDE_B, LIFT_B, NARROW_B, SKIP = 0, 8, 16, 24, 30, 36, 37
MEGA = 1024 * 1024
SPAN = 40_000_000_000
SEGMENTS = 4
IN_VMEM = pl.BlockSpec(memory_space=pltpu.VMEM)
IN_SMEM = pl.BlockSpec(memory_space=pltpu.SMEM)
IN_PLACE = pl.BlockSpec(memory_space=pl.ANY)
IN_HBM = pl.BlockSpec(memory_space=pltpu.HBM)


def mm(left, right):
    return jnp.dot(left, right, preferred_element_type=F32)


def mm_last(left, right):
    return lax.dot_general(left, right, (((1,), (1,)), ((), ())), preferred_element_type=F32)


def mm_first(left, right, precision=None):
    return lax.dot_general(
        left, right, (((0,), (0,)), ((), ())), preferred_element_type=F32, precision=precision
    )


def gelu(z):
    return 0.5 * z * (1.0 + jnp.tanh(GELU_SCALE * (z + GELU_CUBE * z * z * z)))


def gelu_slope(z):
    square = z * z
    bend = jnp.tanh(GELU_SCALE * (z + GELU_CUBE * z * square))
    return 0.5 * (1.0 + bend) + 0.5 * z * (1.0 - bend * bend) * GELU_SCALE * (
        1.0 + 3.0 * GELU_CUBE * square
    )


class Kernel:
    def __init__(self, lengths, length, layer):
        self.lengths, self.length, self.layer = lengths, length, layer

    def __call__(
        self, name, body, outs, vin=(), places=(), picked=(), scratch=(), after=(), spare=6, span=1, keep=False, direct=(), onto=0
    ):
        n_v, n_a, n_p, n_o, n_s = len(vin), len(places), len(picked), len(outs), len(scratch)
        n_w, n_k = len(after), len(picked) if keep else 0
        layer = self.layer

        def run(*refs):
            k = KernelRefs()
            k.meta = placing(refs[0], self.length)
            at = 1
            k.vin = refs[at : at + n_v]
            at += n_v
            k.places = refs[at : at + n_a]
            at += n_a
            pairs = refs[at : at + 2 * n_p]
            at += 2 * n_p + n_w
            k.outs = refs[at : at + n_o]
            at += n_o
            buffers = refs[at : at + n_k]
            at += n_k
            k.scratch = refs[at : at + n_s]
            at += n_s
            if not keep:
                buffers = refs[at : at + n_p]
                at += n_p
            if n_p:
                sems = refs[at]
                mine = k.meta[0] == layer

                def fetch(source):
                    for i in range(n_p):
                        pltpu.make_async_copy(pairs[2 * i + source], buffers[i], sems.at[i]).start()

                pl.when(mine)(partial(fetch, 0))
                pl.when(jnp.logical_not(mine))(partial(fetch, 1))

                def get(i):
                    pltpu.make_async_copy(pairs[2 * i], buffers[i], sems.at[i]).wait()
                    return buffers[i]

                k.get = get
            body(k)

        extra = [] if keep else [pltpu.VMEM(own.shape, own.dtype) for own, _ in picked]
        if n_p:
            extra.append(pltpu.SemaphoreType.DMA((n_p,)))
        held = sum(
            _size(ref.shape) * ref.dtype.itemsize
            for ref in (*scratch, *extra)
            if ref.memory_space == pltpu.VMEM
        )
        flat = [part for pair in picked for part in pair]
        operands = (self.lengths, *vin, *places, *flat, *after)
        return pl.pallas_call(
            run,
            out_shape=[jax.ShapeDtypeStruct(s, d) for s, d in outs]
            + [jax.ShapeDtypeStruct(own.shape, own.dtype) for own, _ in picked[:n_k]],
            in_specs=[IN_SMEM]
            + [IN_VMEM] * n_v
            + [IN_PLACE] * n_a
            + [IN_HBM] * (2 * n_p)
            + [IN_PLACE] * n_w,
            out_specs=[IN_PLACE if i in direct else IN_VMEM for i in range(n_o + n_k)],
            input_output_aliases={1 + n_v + i: i for i in range(onto)},
            scratch_shapes=[*scratch, *extra],
            compiler_params=pltpu.CompilerParams(vmem_limit_bytes=held + spare * MEGA),
            cost_estimate=pl.CostEstimate(flops=span, bytes_accessed=1, transcendentals=0),
            name=name,
        )(*operands)


class KernelRefs:
    pass


def placing(lengths, length):
    section, ti, di = (lax.axis_index(axis) for axis in ("section", "tensor", "dp"))
    first = -di * length
    second = first + lengths[section, 0]
    return [section, ti, di, first, second, second + lengths[section, 1]]


def _size(shape):
    total = 1
    for extent in shape:
        total *= extent
    return total


def vec(pack, first, count):
    column = pack.shape[1] - LANES
    rows = [pack[first + i : first + i + 1, column:] for i in range(count)]
    return rows[0] if count == 1 else jnp.concatenate(rows, axis=1)


def tables(pack):
    return [pack[:, i * LANES : (i + 1) * LANES] for i in range(4)]


def start_in(meta, first, count):
    hit = False
    for i in range(3):
        hit = jnp.logical_or(hit, (meta[3 + i] >= first) & (meta[3 + i] < first + count))
    return hit


def keep_at(meta, place):
    return jnp.where(start_in(meta, place, 1), 0.0, 1.0)


BLOCK = 32


def scan_blocks(meta, length, carry, step, backward=False, block=BLOCK):
    blocks = length // block

    def one(i, carry):
        t0 = pl.multiple_of((blocks - 1 - i if backward else i) * block, block)
        return lax.cond(
            start_in(meta, t0, block),
            lambda c: step(t0, c, True),
            lambda c: step(t0, c, False),
            carry,
        )

    return lax.fori_loop(0, blocks, one, carry)


def row_groups(ref, t0, block, backward=False):
    groups = range(0, block, 8)
    for g in reversed(groups) if backward else groups:
        rows = ref[pl.ds(t0 + g, 8), :]
        for j in reversed(range(8)) if backward else range(8):
            yield g + j, rows[j : j + 1, :]


def end_state(meta, ref, decay, length, backward=False):
    span = length // SEGMENTS
    a = jnp.exp(-decay)

    def step(i, carried, masked):
        out = []
        for g, state in enumerate(carried):
            t0 = pl.multiple_of(g * span + i * 8, 8)
            for j, row in row_groups(ref, t0, 8, backward):
                if backward:
                    state = a * (state + row)
                    if masked:
                        state = state * keep_at(meta, t0 + j)
                else:
                    if masked:
                        state = state * keep_at(meta, t0 + j)
                    state = a * state + row
            out.append(state)
        return tuple(out)

    def one(i, carried):
        i = span // 8 - 1 - i if backward else i
        hit = False
        for g in range(SEGMENTS):
            hit = jnp.logical_or(hit, start_in(meta, g * span + i * 8, 8))
        return lax.cond(hit, lambda c: step(i, c, True), lambda c: step(i, c, False), carried)

    zero = jnp.zeros_like(decay)
    ends = lax.fori_loop(0, span // 8, one, (zero,) * SEGMENTS)
    across = jnp.exp(decay * (-float(span)))
    order = range(SEGMENTS)
    total = zero
    for g in reversed(order) if backward else order:
        through = jnp.where(start_in(meta, g * span, span), 0.0, 1.0)
        total = ends[g] + through * across * total
    return total


def one_minus_exp(d):
    series = 1.0
    for k in range(8, 1, -1):
        series = 1.0 - d * (1.0 / k) * series
    return jnp.where(d < 0.25, d * series, 1.0 - jnp.exp(-d))


def crossing(meta, arrived, decay, length, direction):
    total = jnp.zeros_like(decay)
    for s, part in enumerate(arrived):
        apart = direction * (meta[2] - jnp.bitwise_xor(meta[2], len(arrived) - s)) - 1
        first = -apart * length if direction == 1 else length
        open_way = jnp.logical_and(apart >= 0, jnp.logical_not(start_in(meta, first, apart * length)))
        reach = jnp.exp(decay * (-float(length)) * jnp.maximum(apart, 0).astype(F32))
        total = total + jnp.where(open_way, reach * part[...], 0.0)
    return total


def local(
    layer_input,
    out_cotangent,
    seq_lengths,
    norm_gain,
    norm_bias,
    wide_weight,
    wide_bias,
    narrow_weight,
    narrow_bias,
    ssm_decay,
    ssm_input,
    ssm_output,
    ssm_skip,
    lift_weight,
    lift_bias,
    down_weight,
    down_bias,
):
    section = lax.axis_index("section")
    nt, nd = lax.axis_size("tensor"), lax.axis_size("dp")
    T, D = layer_input.shape[1], layer_input.shape[2]
    FW = wide_weight.shape[2]
    HC = narrow_weight.shape[2]
    H = lift_weight.shape[1]
    N = ssm_decay.shape[2]
    DC = D // nt
    kernels = [Kernel(seq_lengths, T, 0), Kernel(seq_lengths, T, 1)]

    flip = [(0, 1), (1, 0)]

    def swap(x):
        return lax.ppermute(x, "section", flip)

    def make_pack():
        vectors = (
            (norm_gain, GAIN),
            (norm_bias, SHIFT),
            (down_bias, DOWN_B),
            (wide_bias, WIDE_B),
            (lift_bias, LIFT_B),
            (narrow_bias, NARROW_B),
            (ssm_skip, SKIP),
        )
        sources = [ssm_decay, ssm_input, ssm_output]
        sources = [jnp.swapaxes(part, 1, 2)[0] for part in sources]

        def body(k):
            pack, held, sems = k.outs[0], k.scratch[:-1], k.scratch[-1]
            copies = [
                pltpu.make_async_copy(source, target, sems.at[i])
                for i, (source, target) in enumerate(zip(k.places, held))
            ]
            for copy in copies:
                copy.start()
            column = 4 * LANES
            pack[:, column:] = jnp.zeros((N, LANES), F32)
            for copy in copies:
                copy.wait()
            for i, source in zip((0, 2, 3), held):
                pack[:, i * LANES : (i + 1) * LANES] = source[...]
            pack[:, LANES : 2 * LANES] = one_minus_exp(held[0][...])
            for (source, first), ref in zip(vectors, held[3:]):
                for i in range(source.shape[1] // LANES):
                    pack[first + i : first + i + 1, column:] = ref[
                        :, i * LANES : (i + 1) * LANES
                    ]

        places = (*sources, *(v for v, _ in vectors))
        return kernels[0](
            "make_pack",
            body,
            [((N, 5 * LANES), F32)],
            places=places,
            scratch=[pltpu.VMEM(part.shape, F32) for part in places]
            + [pltpu.SemaphoreType.DMA((len(places),))],
            spare=56,
            span=SPAN,
        )[0]

    pack = make_pack()
    pack_other = swap(pack)
    narrow_w = (narrow_weight[0], swap(narrow_weight[0]))
    wide_w = (wide_weight[0], swap(wide_weight[0]))
    lift_w = (lift_weight[0], swap(lift_weight[0]))
    down_w = (down_weight[0], swap(down_weight[0]))

    def paired(part, axis, s):
        n = lax.axis_size(axis)
        return lax.ppermute(part, axis, [(i, i ^ s) for i in range(n)])

    def scatter(parts, axis="tensor"):
        n = len(parts)
        return (parts[0], *(paired(parts[s], axis, n - s) for s in range(1, n)))

    def gather(part, forward=False):
        if forward and nt == 4:
            across = paired(part, "tensor", 2)
            beside = paired(part, "tensor", 1)
            return (part, paired(across, "tensor", 1), across, beside)
        return (part, *(paired(part, "tensor", nt - s) for s in range(1, nt)))

    def paired_parts(meta, keep, give, part):
        for i in range(nt // 2):
            for bit, out in ((0, keep), (1, give)):
                out[i] = part(jnp.bitwise_xor(meta[1], 2 * i + bit)).astype(out.dtype)

    def paired_outs(width):
        return [((nt // 2, T, width), F32), ((nt // 2, T, width), BF16)]

    def parts_join(layer, keep, arrived, after):
        half, width = keep.shape[0] // 2, keep.shape[2]

        def body(k):
            for i in range(2 * half):
                out = k.outs[i % 2]
                out[i // 2] = (k.vin[0][i] + k.vin[1][i].astype(F32)).astype(out.dtype)

        return kernels[layer](
            f"parts_join{layer}",
            body,
            [((half, T, width), F32), ((half, T, width), BF16)],
            vin=(keep, arrived),
            after=after,
        )

    def paired_sum(layer, keep, give, arrived, after):
        step = 2
        while step < nt:
            keep, give = parts_join(layer, keep, arrived, after)
            arrived = paired(give, "tensor", step)
            step *= 2
        return keep, arrived

    def line(value):
        return tuple(paired(value, "dp", nd - 1 - s) for s in range(nd - 1))

    def target(mine, s, n):
        return jnp.bitwise_xor(mine, (n - s) % n)

    HALVES = (FW // 2, FW // 2, D // 2)
    RIGHT = sum(HALVES)

    def turn(layer, sources, after):
        def body(k):
            row = 0
            for source in k.vin:
                for c in range(0, source.shape[1], 256):
                    block = source[:, c : c + 256].astype(F32)
                    k.outs[0][row : row + 256, :] = jnp.transpose(block).astype(BF16)
                    row += 256

        height = sum(part.shape[1] for part in sources)
        return kernels[layer](f"turn{layer}", body, [((height, T), BF16)], vin=sources, after=after)[0]

    def halve(layer, sources, after):
        def body(k):
            at = 0
            for source, width in zip(k.vin, HALVES):
                for out, which in zip(k.outs, (k.meta[0], 1 - k.meta[0])):
                    here = pl.ds(pl.multiple_of(which * width, LANES), width)
                    out[:, at : at + width] = source[:, here]
                at += width

        return kernels[layer](
            f"halve{layer}", body, [((T, RIGHT), BF16)] * 2, vin=sources, after=after
        )

    def choose(layer, pairs, after):
        def body(k):
            for i in range(len(pairs)):
                k.get(i)

        return kernels[layer](f"choose{layer}", body, [], picked=pairs, after=after, keep=True, spare=30)

    def norm_rows(rows, emit):
        def block(i, _):
            here = pl.ds(pl.multiple_of(i * 32, 32), 32)
            x = rows[here, :].astype(F32)
            offset = x - jnp.mean(x, axis=1, keepdims=True)
            spread = jnp.mean(offset * offset, axis=1, keepdims=True)
            inverse = lax.rsqrt(spread + NORM_EPSILON)
            emit(here, offset * inverse, inverse)
            return 0

        lax.fori_loop(0, T // 32, block, 0, unroll=4)

    def norm0(after):
        def body(k):
            xhat, rstd = k.outs
            rows, sems = k.scratch
            copy = pltpu.make_async_copy(k.places[0].at[k.meta[0]], rows, sems.at[0])
            copy.start()
            copy.wait()

            def emit(here, standard, inverse):
                xhat[here, :] = standard
                rstd[here, :] = jnp.broadcast_to(inverse, (32, LANES))

            norm_rows(rows, emit)

        return kernels[0](
            "norm0",
            body,
            [((T, D), F32), ((T, LANES), F32)],
            places=(layer_input,),
            after=after,
            scratch=[pltpu.VMEM((T, D), BF16), pltpu.SemaphoreType.DMA((1,))],
            span=SPAN,
        )

    def front(layer, source, pack, narrow, after=()):
        def body(k):
            meta = k.meta
            normed, narrow_pre, act, final = k.outs[:4]
            if layer == 0:
                pk, upper = k.outs[4:]
                keep_or_give(meta, pk, upper, k.vin[1][...], k.vin[2][...], False)
            else:
                xhat, rstd = k.outs[4:]
                rows = k.scratch[0]
                assemble(meta, k.vin, rows)
                pk, weight = k.vin[nt:]
            gain, shift = vec(pk, GAIN, D // LANES), vec(pk, SHIFT, D // LANES)
            if layer == 0:
                for r in range(0, T, 32):
                    here = slice(r, r + 32)
                    normed[here, :] = (k.vin[0][here, :] * gain + shift).astype(BF16)
                weight = k.get(0)
            else:

                def emit(here, standard, inverse):
                    xhat[here, :] = standard
                    rstd[here, :] = jnp.broadcast_to(inverse, (32, LANES))
                    normed[here, :] = (standard * gain + shift).astype(BF16)

                norm_rows(rows, emit)
            pre = mm(normed[...], weight[...]) + vec(pk, NARROW_B, 1)
            narrow_pre[...] = pre
            act[...] = gelu(pre)
            final[...] = end_state(meta, act, tables(pk)[0], T)

        return kernels[layer](
            f"front{layer}",
            body,
            [((T, D), BF16), ((T, HC), F32), ((T, HC), F32), ((N, HC), F32)]
            + (
                [(pack[0].shape, F32)] * 2
                if layer == 0
                else [((T, D), F32), ((T, LANES), F32)]
            ),
            after=after,
            vin=(source, *pack) if layer == 0 else (*source, pack, narrow),
            picked=(narrow,) if layer == 0 else (),
            keep=True,
            scratch=[] if layer == 0 else [pltpu.VMEM((T, D), BF16)],
            span=SPAN,
        )

    def wide0(normed, pack):
        def body(k):
            bias = vec(k.vin[1], WIDE_B, FW // LANES)
            weight = k.get(0)
            for c in range(0, FW, 256):
                k.outs[0][:, c : c + 256] = (
                    mm(k.vin[0][...], weight[:, c : c + 256]) + bias[:, c : c + 256]
                )

        return kernels[0](
            "wide0",
            body,
            [((T, FW), F32)],
            vin=(normed, pack),
            picked=(wide_w,),
            keep=True,
            spare=6,
        )

    def wide1(normed, d_gated, pack, wide, lift, after):
        def body(k):
            wide_pre, lift_low = k.outs[:2]
            pk, weight, lift = k.vin[2:]
            bias = vec(pk, WIDE_B, FW // LANES)
            for c in range(0, FW, 256):
                pre = mm(k.vin[0][...], weight[:, c : c + 256]) + bias[:, c : c + 256]
                wide_pre[:, c : c + 256] = pre
                lift_low[:, c : c + 256] = (k.vin[1][:, c : c + 256] * gelu(pre)).astype(BF16)
            lift_parts(k.meta, lift_low, lift, k.outs[2:])

        return kernels[1](
            "wide1",
            body,
            [((T, FW), F32), ((T, FW), BF16)] + parted(HC),
            vin=(normed, d_gated, pack, wide, lift),
            after=after,
            span=SPAN,
        )

    def parted(width, rows=T):
        return [((rows, width), F32)] + [((rows, width), BF16)] * (nt - 1)

    def lift_parts(meta, lift_low, lift, sends):
        for s in range(nt):
            at = target(meta[1], s, nt) * HC
            part = mm_last(lift_low[...], lift[pl.ds(pl.multiple_of(at, HC), HC), :])
            sends[s][...] = part.astype(sends[s].dtype)

    def carry(layer, act, arrived, pack, after=()):
        def body(k):
            meta = k.meta
            u = k.vin[0]
            entering, scanned = k.outs
            local_out = k.scratch[0]
            pk = k.vin[1]
            decay, grown, rate_in, read_out = tables(pk)
            skip = vec(pk, SKIP, 1)
            a, read = jnp.exp(-decay), read_out * rate_in * grown
            state = crossing(meta, k.vin[2:], decay, T, 1)
            entering[...] = state

            def step(t0, state, masked):
                outs = []
                for j, row in row_groups(u, t0, BLOCK):
                    if masked:
                        state = state * keep_at(meta, t0 + j)
                    state = a * state + row
                    outs.append(jnp.sum(read * state, axis=0, keepdims=True) + skip * row)
                for g in range(0, BLOCK, 8):
                    local_out[pl.ds(t0 + g, 8), :] = jnp.concatenate(outs[g : g + 8], axis=0)
                return state

            scan_blocks(meta, T, state, step)
            scanned[...] = local_out[...].astype(BF16)

        return kernels[layer](
            f"carry{layer}",
            body,
            [((N, HC), F32), ((T, HC), BF16)],
            vin=(act, pack, *arrived),
            after=after,
            scratch=[pltpu.VMEM((T, HC), F32)],
            span=SPAN,
        )

    def assemble(meta, parts, whole):
        width = parts[0].shape[1]
        for s in range(nt):
            at = target(meta[1], s, nt) * width
            whole[:, pl.ds(pl.multiple_of(at, width), width)] = parts[s][...]

    def down_parts(meta, gated, down, sends):
        for s in range(nt):
            at = target(meta[1], s, nt) * DC
            part = mm(gated[...], down[:, pl.ds(pl.multiple_of(at, DC), DC)])
            sends[s][...] = part.astype(sends[s].dtype)

    def middle0(pieces, wide_pre, pack, lift, down):
        def body(k):
            scanned, lifted, gated = k.outs[:3]
            assemble(k.meta, k.vin[:nt], scanned)
            wide_pre, pk, lift, down = k.vin[nt:]
            bias = vec(pk, LIFT_B, FW // LANES)
            for c in range(0, FW, 256):
                part = mm(scanned[...], lift[:, c : c + 256]) + bias[:, c : c + 256]
                lifted[:, c : c + 256] = part
                gated[:, c : c + 256] = (part * gelu(wide_pre[:, c : c + 256])).astype(BF16)
            down_parts(k.meta, gated, down, k.outs[3:])

        return kernels[0](
            "middle0",
            body,
            [((T, H), BF16), ((T, FW), F32), ((T, FW), BF16)] + parted(DC),
            vin=(*pieces, wide_pre, pack, lift, down),
            span=SPAN,
        )

    def middle1(pieces, wide_pre, d_gated, pack, lift):
        def body(k):
            scanned, gated, wide_low = k.outs
            assemble(k.meta, k.vin[:nt], scanned)
            pre, grad, pk, lift = k.vin[nt:]
            bias = vec(pk, LIFT_B, FW // LANES)
            for c in range(0, FW, 256):
                part = mm(scanned[...], lift[:, c : c + 256]) + bias[:, c : c + 256]
                z = pre[:, c : c + 256]
                gated[:, c : c + 256] = (part * gelu(z)).astype(BF16)
                wide_low[:, c : c + 256] = (grad[:, c : c + 256] * part * gelu_slope(z)).astype(BF16)

        return kernels[1](
            "middle1",
            body,
            [((T, H), BF16), ((T, FW), BF16), ((T, FW), BF16)],
            vin=(*pieces, wide_pre, d_gated, pack, lift),
            span=SPAN,
        )

    def top_parts(gated, down, after):
        def body(k):
            gated, down = k.vin
            paired_parts(
                k.meta,
                *k.outs,
                lambda at: mm(gated[...], down[:, pl.ds(pl.multiple_of(at * DC, DC), DC)]),
            )

        return kernels[1]("top_parts", body, paired_outs(DC), vin=(gated, down), after=after)

    def column_rows(pk, first, at):
        per = DC // LANES
        best = vec(pk, first, per)
        for i in range(1, nt):
            best = jnp.where(at == i, vec(pk, first + i * per, per), best)
        return best

    def keep_or_give(meta, keep, give, first, second, by_layer=True):
        lower = meta[0] == 0
        keep[...] = jnp.where(lower, first, second)
        give[0 : keep.shape[0], :] = jnp.where(lower, second, first).astype(give.dtype)

    def layer_output(layer, before, parts, pack, after=()):
        def body(k):
            meta = k.meta
            if layer == 0:
                rows = k.scratch[0]
                copy = pltpu.make_async_copy(
                    k.places[0].at[meta[0], :, pl.ds(pl.multiple_of(meta[1] * DC, DC), DC)],
                    rows,
                    k.scratch[1].at[0],
                )
                copy.start()
                copy.wait()
                total = rows[...].astype(F32)
            else:
                total = k.vin[-1][...] + k.vin[1][0] + k.vin[2][0].astype(F32)
            for part in k.vin[1 : 1 + nt] if layer == 0 else ():
                total = total + part[...].astype(F32)
            total = total + column_rows(k.vin[0], DOWN_B, meta[1])
            if layer == 0:
                k.outs[0][...] = total
                k.outs[1][...] = total.astype(BF16)
            else:
                keep_or_give(meta, k.outs[0], k.outs[1], k.vin[-1][...], total)

        return kernels[layer](
            f"layer_output{layer}",
            body,
            [((T, DC), F32), ((T, DC), BF16 if layer == 0 else F32)],
            vin=(pack, *parts) if layer == 0 else (pack, *parts, before),
            after=after,
            places=(before,) if layer == 0 else (),
            scratch=[pltpu.VMEM((T, DC), BF16), pltpu.SemaphoreType.DMA((1,))] if layer == 0 else [],
            span=1 if layer else SPAN,
        )

    def grad_gated1(down, after):
        def body(k):
            rows = k.outs[1]
            copy = pltpu.make_async_copy(k.places[0].at[k.meta[0]], rows, k.scratch[0].at[0])
            copy.start()
            copy.wait()
            down = k.vin[0]
            for c in range(0, FW, 256):
                k.outs[0][:, c : c + 256] = mm_last(rows[...], down[c : c + 256, :])

        return kernels[1](
            "grad_gated1",
            body,
            [((T, FW), F32), ((T, D), BF16)],
            places=(out_cotangent,),
            vin=(down,),
            after=after,
            scratch=[pltpu.SemaphoreType.DMA((1,))],
        )

    def grad_middle0(pieces, wide_pre, lifted, down, lift, after=()):
        def body(k):
            wide_low, low, rows = k.outs[:3]
            pre, raised, down, lift = k.vin[nt:]
            assemble(k.meta, k.vin[:nt], rows)
            for c in range(0, FW, 256):
                grad = mm_last(rows[...], down[c : c + 256, :])
                z = pre[:, c : c + 256]
                low[:, c : c + 256] = (grad * gelu(z)).astype(BF16)
                wide_low[:, c : c + 256] = (
                    grad * raised[:, c : c + 256] * gelu_slope(z)
                ).astype(BF16)
            lift_parts(k.meta, low, lift, k.outs[3:])

        return kernels[0](
            "grad_middle0",
            body,
            [((T, FW), BF16), ((T, FW), BF16), ((T, D), BF16)] + parted(HC),
            vin=(*pieces, wide_pre, lifted, down, lift),
            after=after,
            span=SPAN,
        )

    def adjoint_local(layer, parts, pack, after=()):
        def body(k):
            grads, first = k.outs
            total = k.vin[1][...]
            for part in k.vin[2:]:
                total = total + part[...].astype(F32)
            grads[...] = total
            first[...] = end_state(k.meta, grads, tables(k.vin[0])[0], T, backward=True)

        return kernels[layer](
            f"adjoint_local{layer}",
            body,
            [((T, HC), F32), ((N, HC), F32)],
            vin=(pack, *parts),
            after=after,
            span=SPAN,
        )

    def adjoint(layer, d_scanned, narrow_pre, arrived, pack, after=()):
        def body(k):
            meta = k.meta
            grads, pre, pk = k.vin[:3]
            after, narrow_low = k.outs
            d_narrow = k.scratch[0]
            decay, grown, rate_in, read_out = tables(pk)
            skip = vec(pk, SKIP, 1)
            a, read = jnp.exp(-decay), read_out * rate_in * grown
            incoming = crossing(meta, k.vin[3:], decay, T, -1)
            after[...] = incoming

            def step(t0, z, masked):
                outs = [None] * BLOCK
                for j, row in row_groups(grads, t0, BLOCK, True):
                    w = z + row
                    outs[j] = jnp.sum(read * w, axis=0, keepdims=True) + skip * row
                    z = a * w
                    if masked:
                        z = z * keep_at(meta, t0 + j)
                for g in range(0, BLOCK, 8):
                    d_narrow[pl.ds(t0 + g, 8), :] = jnp.concatenate(outs[g : g + 8], axis=0)
                return z

            scan_blocks(meta, T, incoming, step, backward=True)
            narrow_low[...] = (d_narrow[...] * gelu_slope(pre[...])).astype(BF16)

        return kernels[layer](
            f"adjoint{layer}",
            body,
            [((N, HC), F32), ((T, HC), BF16)],
            vin=(d_scanned, narrow_pre, pack, *arrived),
            after=after,
            scratch=[pltpu.VMEM((T, HC), F32)],
            span=SPAN,
        )

    LATE = D // 2 + 2 * N

    def ssm_grads(layer, act, entering, d_scanned, incoming, turned, narrow_low, pack, upper, after):
        def body(k):
            meta = k.meta
            u, enter, grads, incoming, low, pk = k.vin[:6]
            states, lefts, sems = k.scratch[:3]
            late = k.outs[0] if layer == 1 else k.scratch[3]
            copy = pltpu.make_async_copy(k.places[0].at[0:D, :], lefts, sems.at[0])
            copy.start()
            decay, grown, rate_in, read_out = tables(pk)
            a = jnp.exp(-decay)
            zero = jnp.zeros((N, HC), F32)

            def ahead(t0, state, masked):
                for j, row in row_groups(u, t0, BLOCK):
                    if masked:
                        state = state * keep_at(meta, t0 + j)
                    states[t0 + j] = state
                    state = a * state + row
                return state

            scan_blocks(meta, T, enter[...], ahead)

            def back(t0, carried, masked):
                z, with_rows, with_states = carried
                rows = row_groups(u, t0, BLOCK, True)
                for (j, row), (_, grad) in zip(rows, row_groups(grads, t0, BLOCK, True)):
                    w = z + grad
                    with_rows = with_rows + w * row
                    with_states = with_states + w * states[t0 + j]
                    z = a * w
                    if masked:
                        z = z * keep_at(meta, t0 + j)
                return z, with_rows, with_states

            _, with_rows, with_states = scan_blocks(
                meta, T, (incoming[...], zero, zero), back, backward=True
            )
            b = rate_in * grown
            first, second = slice(D // 2, D // 2 + N), slice(D // 2 + N, D // 2 + 2 * N)
            late[first, 0:LANES] = a * read_out * (rate_in * with_rows - b * with_states)
            late[first, LANES:] = grown * read_out * with_rows
            late[second, 0:LANES] = b * with_rows
            late[second, LANES:] = zero
            row = D // 2 + N
            late[row : row + 1, LANES:] = jnp.sum(low[...].astype(F32), axis=0, keepdims=True)
            late[row + 1 : row + 2, LANES:] = jnp.sum(u[...] * grads[...], axis=0, keepdims=True)
            copy.wait()
            for h in range(2):
                late[0 : D // 2, h * LANES : (h + 1) * LANES] = mm(
                    lefts[h * (D // 2) : (h + 1) * (D // 2), :], low[...]
                )
            if layer == 0:
                keep_or_give(meta, k.outs[0], k.outs[1], late[...], k.vin[6][...])

        return kernels[layer](
            f"ssm_grads{layer}",
            body,
            [((LATE, 2 * LANES), F32)] * (2 - layer),
            vin=(act, entering, d_scanned, incoming, narrow_low, pack, *upper),
            places=(turned,),
            span=1 if layer else SPAN,
            after=after,
            scratch=[
                pltpu.VMEM((T, N, HC), F32),
                pltpu.VMEM((D, T), BF16),
                pltpu.SemaphoreType.DMA((1,)),
            ]
            + ([pltpu.VMEM((LATE, 2 * LANES), F32)] if layer == 0 else []),
        )

    def grad_normed(layer, wide_low, narrow_low, xhat, pack, wide, narrow, after=()):
        def body(k):
            meta = k.meta
            wide_low, narrow_in, standard, gains, wide, narrow = k.vin
            ones = jnp.ones((8, DC), BF16)
            sums = jnp.zeros((16, T), F32)
            for s in range(nt):
                at = target(meta[1], s, nt)
                here = pl.ds(pl.multiple_of(at * DC, DC), DC)
                part = mm_last(wide_low[...], wide[here, :]) + mm_last(
                    narrow_in[...], narrow[here, :]
                )
                scaled = part * column_rows(gains, GAIN, at)
                with_x = scaled * standard[:, here]
                sums = sums + jnp.concatenate(
                    [mm_last(ones, scaled.astype(BF16)), mm_last(ones, with_x.astype(BF16))], axis=0
                )
                k.outs[s][0:T, :] = part.astype(k.outs[s].dtype)
            for s in range(nt):
                k.outs[s][T:, :] = sums.astype(k.outs[s].dtype)

        return kernels[layer](
            f"grad_normed{layer}",
            body,
            parted(DC, T + 16),
            vin=(wide_low, narrow_low, xhat, pack, wide, narrow),
            after=after,
            span=SPAN,
        )

    def layer_grad(layer, parts, rstd, xhat, grad_out, pack, after):
        def body(k):
            meta = k.meta
            here = pl.ds(pl.multiple_of(meta[1] * DC, DC), DC)
            standard, sems = k.scratch[0], k.scratch[1]
            copy = pltpu.make_async_copy(k.places[0].at[:, here], standard, sems.at[0])
            copy.start()
            if layer == 1:
                copy_out = pltpu.make_async_copy(
                    k.places[1].at[meta[0], :, here], k.scratch[2], sems.at[1]
                )
                copy_out.start()
            total, sums = k.vin[0][0:T, :], k.vin[0][T:, :]
            for part in k.vin[1:nt]:
                total = total + part[0:T, :].astype(F32)
                sums = sums + part[T:, :].astype(F32)
            inverse = k.vin[nt]
            row = lax.broadcasted_iota(jnp.int32, (16, LANES), 0)
            first = mm_first(sums, (row == 0).astype(F32), lax.Precision.HIGHEST) * (1.0 / D)
            second = mm_first(sums, (row == 8).astype(F32), lax.Precision.HIGHEST) * (1.0 / D)
            scaled = total * column_rows(k.vin[nt + 1], GAIN, meta[1])
            copy.wait()
            if layer == 1:
                copy_out.wait()
                grad_in = k.scratch[2][...].astype(F32)
            else:
                grad_in = k.vin[nt + 2][...]
            if layer == 1:
                result = k.outs[0]
            else:
                keep, give, upper = k.outs[0], k.outs[1], k.vin[nt + 2]
                result = k.scratch[2]
            for c in range(0, DC, LANES):
                x = standard[:, c : c + LANES]
                grad = grad_in[0:T, c : c + LANES] + inverse[...] * (
                    scaled[:, c : c + LANES] - first - x * second
                )
                result[0:T, c : c + LANES] = grad
                if layer == 1:
                    k.outs[1][:, c : c + LANES] = grad.astype(BF16)
            result[T:, :] = jnp.zeros((8, DC), F32)
            result[T : T + 1, :] = jnp.sum(total * standard[...], axis=0, keepdims=True)
            result[T + 1 : T + 2, :] = jnp.sum(total, axis=0, keepdims=True)
            if layer == 0:
                keep_or_give(meta, keep, give, result[...], upper[...])
                give[T + 8 :, :] = jnp.zeros((8, DC), BF16)

        return kernels[layer](
            f"layer_grad{layer}",
            body,
            [((T + 8, DC), F32), ((T, DC), BF16)]
            if layer == 1
            else [((T + 8, DC), F32), ((T + 16, DC), BF16)],
            after=after,
            vin=(*parts, rstd, pack) + (() if layer == 1 else (grad_out,)),
            places=(xhat,) + ((grad_out,) if layer == 1 else ()),
            scratch=[pltpu.VMEM((T, DC), F32), pltpu.SemaphoreType.DMA((2,))]
            + [pltpu.VMEM((T, DC), BF16) if layer == 1 else pltpu.VMEM((T + 8, DC), F32)],
            span=SPAN,
        )

    RW, RL, RD = D // nd, H // nd, FW // nd
    CW, CD = HALVES[0] // LANES, HALVES[2] // LANES
    AT_L = RW * CW
    AT_D = AT_L + RL * CW
    AT_V = AT_D + RD * CD
    BIG = AT_V + 16
    CUT = AT_L + 2 * RL
    STEPS = nd.bit_length() - 1

    def mirrored(s):
        return sum(((s >> b) & 1) << (STEPS - 1 - b) for b in range(STEPS))

    def block_outs(count):
        return [((count, rows, LANES), BF16) for rows in (CUT, BIG - CUT) for _ in range(2)]

    def to_pairs(blocks, step):
        return (
            paired(blocks[1], "dp", 1 << step),
            paired(blocks[3], "dp", 1 << (STEPS - 1 - step)),
        )

    def blocks_join(layer, blocks, arrived, after):
        count = blocks[0].shape[0] // 2

        def body(k):
            for h in range(2):
                for i in range(2 * count):
                    part = k.vin[2 * h][i].astype(F32) + k.vin[2 * h + 1][i].astype(F32)
                    k.outs[2 * h + i % 2][i // 2] = part.astype(BF16)

        return kernels[layer](
            f"blocks_join{layer}",
            body,
            block_outs(count),
            vin=(blocks[0], arrived[0], blocks[2], arrived[1]),
            after=after,
        )

    def put(k, s, row, value):
        first = row < CUT
        i = s if first else mirrored(s)
        out = k.outs[i % 2 if first else 2 + i % 2]
        row -= 0 if first else CUT
        out[i // 2, row : row + value.shape[0], :] = value.astype(BF16)

    def weight_grads(layer, lefts, rights, after):
        def body(k):
            meta = k.meta
            left, right = k.vin[:2], k.vin[2:]

            def product(row, rows, at, width, at_row):
                columns = slice(at, at + width)
                for s in range(nd):
                    first = row + jnp.bitwise_xor(meta[2], s) * rows
                    here = pl.ds(pl.multiple_of(first, 16), rows)
                    part = mm(left[0][here, :], right[0][:, columns])
                    part = part + mm(left[1][here, :], right[1][:, columns])
                    for h in range(0, width, LANES):
                        put(k, s, at_row + h // LANES * rows, part[:, h : h + LANES])

            product(0, RW, 0, HALVES[0], 0)
            product(D, RL, HALVES[0], HALVES[1], AT_L)
            product(D + H, RD, HALVES[0] + HALVES[1], HALVES[2], AT_D)
            sums = k.scratch[0]
            sums[...] = jnp.zeros((16, LANES), F32)
            for i in range(RIGHT // LANES):
                here = slice(i * LANES, (i + 1) * LANES)
                total = jnp.sum(right[0][:, here].astype(F32), axis=0, keepdims=True)
                total = total + jnp.sum(right[1][:, here].astype(F32), axis=0, keepdims=True)
                sums[i : i + 1, :] = total
            for s in range(nd):
                put(k, s, AT_V, sums[...])

        return kernels[layer](
            f"weight_grads{layer}",
            body,
            block_outs(nd // 2),
            vin=(*lefts, *rights),
            after=after,
            scratch=[pltpu.VMEM((16, LANES), F32)],
        )

    SMALL = RW + 3 * N + 16

    def late_join(keep, other, grad, grad_other, after):
        def body(k):
            meta = k.meta
            own, other, grad, grad_other = k.vin
            rest = k.scratch[0]

            def summed(rows, columns):
                return own[rows, columns] + other[rows, columns]

            half = D // 2
            left, right = slice(0, LANES), slice(LANES, 2 * LANES)
            upper = slice(half, half + N)
            rest[0:N, :] = summed(upper, left)
            rest[N : 2 * N, :] = summed(upper, right)
            rest[2 * N : 3 * N, :] = summed(slice(half + N, half + 2 * N), left)
            rest[3 * N : 3 * N + 8, :] = summed(slice(half + N, half + N + 8), right)
            rest[3 * N + 8 :, :] = jnp.zeros((8, LANES), F32)
            per = DC // LANES
            for i in range(2):
                row = grad[T + i : T + i + 1, :] + grad_other[T : T + 16, :].astype(F32)[i : i + 1, :]
                for h in range(per):
                    first = 3 * N + 8 + i * per + h
                    rest[first : first + 1, :] = row[:, h * LANES : (h + 1) * LANES]
            for s in range(nd):
                at = target(meta[2], s, nd) * RW
                here = pl.ds(pl.multiple_of(lax.rem(at, half), 16), RW)
                for h in range(2):

                    def put(h=h, out=k.outs[s]):
                        columns = slice(h * LANES, (h + 1) * LANES)
                        out[0:RW, :] = summed(here, columns).astype(BF16)

                    pl.when(at // half == h)(put)
                k.outs[s][RW:, :] = rest[...].astype(BF16)

        return kernels[0](
            "late_join",
            body,
            [((SMALL, LANES), BF16)] * nd,
            vin=(keep, other, grad, grad_other),
            after=after,
            scratch=[pltpu.VMEM((3 * N + 16, LANES), F32)],
        )

    def pick(meta, flat, out):
        width = out.shape[1]
        best = flat[:, 0:width]
        for i in range(1, nd):
            best = jnp.where(meta[2] == i, flat[:, i * width : (i + 1) * width], best)
        out[...] = best

    def chunk(meta, source, first, count, out):
        flat = [source[first + i : first + i + 1, :] for i in range(count)]
        pick(meta, flat[0] if count == 1 else jnp.concatenate(flat, axis=1), out)

    def big_sum(layer, blocks, arrived, upper, after):
        def body(k):
            for h, (first, rows) in enumerate(((0, CUT), (CUT, BIG - CUT))):
                for r in range(0, rows, 256):
                    inner = slice(r, min(r + 256, rows))
                    here = slice(first + inner.start, first + inner.stop)
                    total = k.vin[2 * h][0, inner, :].astype(F32)
                    total = total + k.vin[2 * h + 1][0, inner, :].astype(F32)
                    if layer == 1:
                        k.outs[0][here, :] = total
                    else:
                        lower = k.meta[0] == 0
                        other = k.vin[4][here, :]
                        k.outs[0][here, :] = jnp.where(lower, total, other)
                        k.outs[1][here, :] = jnp.where(lower, other, total).astype(BF16)

        return kernels[layer](
            f"big_sum{layer}",
            body,
            [((BIG, LANES), F32)] + ([((BIG, LANES), BF16)] if layer == 0 else []),
            vin=(blocks[0], arrived[0], blocks[2], arrived[1], *upper),
            after=after,
        )

    def late_sum(parts):
        def body(k):
            total = k.vin[0][...].astype(F32)
            for part in k.vin[1:]:
                total = total + part[...].astype(F32)
            k.outs[0][...] = total

        return kernels[0]("late_sum", body, [((SMALL, LANES), F32)], vin=parts, span=SPAN)[0]

    def big_places():
        return ((0, RW, CW), (AT_L, RL, CW), (AT_D, RD, CD))

    def own_columns(keep, grad, grad_other, after):
        def body(k):
            meta = k.meta
            *outs, grads = k.outs
            rows, sems = k.scratch
            rows[...] = k.vin[0][0:T, :].astype(F32)
            moves = [(k.places[1].at[0:T, :], grads.at[0, meta[0]]), (rows, grads.at[0, 1 - meta[0]])]
            for out, (first, height, columns) in zip(outs, big_places()):
                for c in range(columns):
                    at = pl.multiple_of((meta[0] * columns + c) * LANES, LANES)
                    moves.append(
                        (
                            k.places[0].at[first + c * height : first + (c + 1) * height, :],
                            out.at[0, :, pl.ds(at, LANES)],
                        )
                    )
            moves = [
                pltpu.make_async_copy(source, out, sems.at[i])
                for i, (source, out) in enumerate(moves)
            ]
            for move in moves:
                move.start()
            for move in moves:
                move.wait()

        return kernels[0](
            "own_columns",
            body,
            [((1, RW, FW), F32), ((1, RL, FW), F32), ((1, RD, D), F32), ((1, 2, T, DC), F32)],
            vin=(grad_other,),
            places=(keep, grad),
            after=after,
            direct=(0, 1, 2, 3),
            scratch=[pltpu.VMEM((T, DC), F32), pltpu.SemaphoreType.DMA((2 + 2 * CW + CD,))],
        )

    def finish(own, big, small, output, output_other):
        def body(k):
            meta = k.meta
            wide, lift, down, rows, turned, sems = k.scratch
            by_wide, by_lift, by_down = k.outs[:3]
            wide_b, lift_b, down_b = k.outs[3:6]
            by_narrow, narrow_b, *by_ssm, by_skip, gain, shift, outputs = k.outs[6:]
            keep, give, late = k.vin
            moves = [
                (k.places[3], outputs.at[0, meta[0]]),
                (k.places[4], outputs.at[0, 1 - meta[0]]),
                (k.places[5].at[0:RW, :], by_narrow.at[0]),
            ]
            moves = [
                pltpu.make_async_copy(source, out, sems.at[3 + i])
                for i, (source, out) in enumerate(moves)
            ]
            for move in moves:
                move.start()
            for q, (buffer, out, (first, height, columns)) in enumerate(
                zip((wide, lift, down), (by_wide, by_lift, by_down), big_places())
            ):
                for c in range(columns):
                    part = give[first + c * height : first + (c + 1) * height, :]
                    buffer[:, c * LANES : (c + 1) * LANES] = part.astype(F32)
                width = columns * LANES
                at = pl.multiple_of((1 - meta[0]) * width, LANES)
                moves.append(
                    pltpu.make_async_copy(buffer, out.at[0, :, pl.ds(at, width)], sems.at[q])
                )
                moves[-1].start()
            lower = meta[0] == 0
            own, other = keep[AT_V:, :], give[AT_V:, :].astype(F32)
            rows[0:16, :] = jnp.where(lower, own, other)
            rows[16:, :] = jnp.where(lower, other, own)
            at = 0
            for columns, out in ((CW, wide_b), (CW, lift_b), (CD, down_b)):
                whole = [rows[h + at + i : h + at + i + 1, :] for h in (0, 16) for i in range(columns)]
                pick(meta, jnp.concatenate(whole, axis=1), out)
                at += columns
            rows[0:16, :] = late[RW + 3 * N :, :]
            chunk(meta, rows, 0, 1, narrow_b)
            chunk(meta, rows, 1, 1, by_skip)
            chunk(meta, rows, 8, DC // LANES, gain)
            chunk(meta, rows, 8 + DC // LANES, DC // LANES, shift)
            per = HC // nd
            for i in range(3):
                turned[...] = jnp.transpose(late[RW + i * N : RW + (i + 1) * N, :])
                by_ssm[i][0] = turned[pl.ds(pl.multiple_of(meta[2] * per, per), per), :]
            for move in moves:
                move.wait()

        return kernels[0](
            "finish",
            body,
            [
                *((part.shape, F32) for part in own),
                ((1, FW // nd), F32),
                ((1, FW // nd), F32),
                ((1, D // nd), F32),
                ((1, RW, HC), F32),
                ((1, HC // nd), F32),
                ((1, HC // nd, N), F32),
                ((1, HC // nd, N), F32),
                ((1, HC // nd, N), F32),
                ((1, HC // nd), F32),
                ((1, DC // nd), F32),
                ((1, DC // nd), F32),
                ((1, 2, T, DC), F32),
            ],
            vin=(*big, small),
            places=(*own, output, output_other, small),
            direct=(0, 1, 2, 6, 14),
            onto=3,
            scratch=[
                pltpu.VMEM((RW, HALVES[0]), F32),
                pltpu.VMEM((RL, HALVES[1]), F32),
                pltpu.VMEM((RD, HALVES[2]), F32),
                pltpu.VMEM((32, LANES), F32),
                pltpu.VMEM((HC, N), F32),
                pltpu.SemaphoreType.DMA((6,)),
            ],
        )

    xhat0, rstd0 = norm0(after=())
    normed0, narrow_pre0, act0, final0, pack0, pack1, narrow_w0 = front(
        0, xhat0, (pack, pack_other), narrow_w
    )
    arrived = line(final0)
    wide_pre0, wide_w0 = wide0(normed0, pack0)
    enter0, scanned0 = carry(0, act0, arrived, pack0, after=(wide_pre0,))
    pieces = gather(scanned0)
    lift_w0, down_w0 = choose(0, (lift_w, down_w), after=(scanned0,))
    scanned_all0, lifted0, gated0, *sends = middle0(pieces, wide_pre0, pack0, lift_w0, down_w0)
    parts = scatter(sends)
    narrow_w1, wide_w1, lift_w1, down_w1 = choose(
        1, (narrow_w, wide_w, lift_w, down_w), after=(sends[0],)
    )
    d_gated1, out_low1 = grad_gated1(down_w1, after=(sends[0],))
    hidden, hidden_low = layer_output(0, layer_input, parts, pack0, after=(d_gated1,))
    pieces = gather(hidden_low, forward=True)
    lefts0 = turn(0, (normed0, scanned_all0, gated0), after=(hidden_low,))
    lefts0_other = swap(lefts0)

    normed1, narrow_pre1, act1, final1, xhat1, rstd1 = front(
        1, pieces, pack1, narrow_w1, after=(lefts0,)
    )
    wide_pre1, lift_low1, *sends = wide1(normed1, d_gated1, pack1, wide_w1, lift_w1, after=(final1,))
    arrived = line(final1)
    parts = scatter(sends)
    enter1, scanned1 = carry(1, act1, arrived, pack1, after=(sends[0],))
    pieces = gather(scanned1)
    d_scanned1, first1 = adjoint_local(1, parts, pack1, after=(scanned1, lefts0_other))
    scanned_all1, gated1, wide_low1 = middle1(pieces, wide_pre1, d_gated1, pack1, lift_w1)
    arrived = line(first1)
    incoming1, narrow_low1 = adjoint(1, d_scanned1, narrow_pre1, arrived, pack1, after=(wide_low1,))
    sends = grad_normed(1, wide_low1, narrow_low1, xhat1, pack1, wide_w1, narrow_w1)
    parts = scatter(sends)
    lefts1 = turn(1, (normed1, scanned_all1, gated1), after=(sends[0],))
    rights1, rights1_give = halve(1, (wide_low1, lift_low1, out_low1), after=(lefts1,))
    lefts1_other, rights1_other = swap(lefts1), swap(rights1_give)
    (late1,) = ssm_grads(
        1,
        act1,
        enter1,
        d_scanned1,
        incoming1,
        lefts1,
        narrow_low1,
        pack1,
        (),
        after=(rights1,),
    )
    grad_mid, grad_low = layer_grad(1, parts, rstd1, xhat1, out_cotangent, pack1, after=(late1,))
    pieces = gather(grad_low)
    weights1 = weight_grads(
        1, (lefts1, lefts1_other), (rights1, rights1_other), after=(grad_low,)
    )
    big1 = to_pairs(weights1, 0)

    top_keep, top_give = top_parts(gated1, down_w1, after=(weights1[0],))
    top_arrived = paired(top_give, "tensor", 1)

    wide_low0, lift_low0, out_low0, *sends = grad_middle0(
        pieces, wide_pre0, lifted0, down_w0, lift_w0, after=(weights1[0], top_keep)
    )
    parts = scatter(sends)
    rights0, rights0_give = halve(0, (wide_low0, lift_low0, out_low0), after=())
    rights0_other = swap(rights0_give)
    for step in range(1, STEPS):
        weights1 = blocks_join(1, weights1, big1, (rights0,))
        big1 = to_pairs(weights1, step)
    d_scanned0, first0 = adjoint_local(0, parts, pack0, after=(rights0, weights1[0]))
    arrived = line(first0)
    weights0 = weight_grads(
        0, (lefts0, lefts0_other), (rights0, rights0_other), after=(first0,)
    )
    big0 = to_pairs(weights0, 0)
    incoming0, narrow_low0 = adjoint(
        0, d_scanned0, narrow_pre0, arrived, pack0, after=(weights0[0], *big1)
    )
    sends = grad_normed(
        0, wide_low0, narrow_low0, xhat0, pack0, wide_w0, narrow_w0
    )
    parts = scatter(sends)
    for step in range(1, STEPS):
        weights0 = blocks_join(0, weights0, big0, (sends[0], top_arrived))
        big0 = to_pairs(weights0, step)
    late, late_give = ssm_grads(
        0,
        act0,
        enter0,
        d_scanned0,
        incoming0,
        lefts0,
        narrow_low0,
        pack0,
        (late1,),
        after=(weights0[0],),
    )
    (sum1,) = big_sum(1, weights1, big1, (), after=(late,))
    top = paired_sum(1, top_keep, top_give, top_arrived, (late,))
    grad, grad_give = layer_grad(
        0, parts, rstd0, xhat0, grad_mid, pack0, after=(late, sum1, top[0], *big0)
    )
    grad_other = swap(grad_give)
    small_parts = late_join(late, swap(late_give), grad, grad_other, after=())
    small_parts_in = scatter(small_parts, "dp")
    keep, give = big_sum(0, weights0, big0, (sum1,), after=(small_parts[0],))
    big_other = swap(give)
    *own, input_grad = own_columns(keep, grad, grad_other, after=())
    output, output_give = layer_output(1, hidden, top, pack1, after=(own[0],))
    (
        by_wide,
        by_lift,
        by_down,
        wide_b,
        lift_b,
        down_b,
        by_narrow,
        narrow_b,
        by_decay,
        by_input,
        by_output,
        by_skip,
        gain,
        shift,
        section_output,
    ) = finish(own, (keep, big_other), late_sum(small_parts_in), output, swap(output_give))
    return (
        section_output,
        input_grad,
        gain,
        shift,
        by_wide,
        wide_b,
        by_narrow,
        narrow_b,
        by_decay,
        by_input,
        by_output,
        by_skip,
        by_lift,
        lift_b,
        by_down,
        down_b,
    )


def solution(mesh):
    placed = (
        P(None, "dp", None),
        P(None, "dp", None),
        P(),
        P("section", None),
        P("section", None),
        P("section", None, "tensor"),
        P("section", "tensor"),
        P("section", None, "tensor"),
        P("section", "tensor"),
        P("section", "tensor", None),
        P("section", "tensor", None),
        P("section", "tensor", None),
        P("section", "tensor"),
        P("section", None, "tensor"),
        P("section", "tensor"),
        P("section", "tensor", None),
        P("section", None),
    )
    return jax.shard_map(
        local,
        mesh=mesh,
        in_specs=placed,
        out_specs=(
            P("section", None, "dp", "tensor"),
            P("section", None, "dp", "tensor"),
            P("section", ("tensor", "dp")),
            P("section", ("tensor", "dp")),
            P("section", "dp", "tensor"),
            P("section", ("tensor", "dp")),
            P("section", "dp", "tensor"),
            P("section", ("tensor", "dp")),
            P("section", ("tensor", "dp"), None),
            P("section", ("tensor", "dp"), None),
            P("section", ("tensor", "dp"), None),
            P("section", ("tensor", "dp")),
            P("section", "dp", "tensor"),
            P("section", ("tensor", "dp")),
            P("section", ("tensor", "dp"), None),
            P("section", "dp"),
        ),
        check_vma=False,
    )
```

time: 1470 us -> 168 us (0.11); the launches traced: 1450 us -> 168 us
  other arithmetic: 518 us -> 0 us
  waiting for transfers between devices: 384 us -> 30.6 us
  matrix products: 228 us -> 0 us
  blocking collectives: 158 us -> 0 us
  local copies, waits for them, and re-layouts: 122 us -> 1.38 us
  Pallas kernels: 0 us -> 65 us
  starting transfers between devices: 8.16 us -> 69.4 us
  between operations: 23.6 us -> 1.47 us
    psum x5 -> x0, waiting for transfers between devices: 265 us -> none  [the longest x3 170 us: local(): layer_sent_values = layer_input_rows + lax.psum(term, 'tensor') + down_add]
    dot_general x50 -> x0, matrix products: 228 us -> none  [the longest x18 172 us: ssm_block(): jnp.einsum('tsk,kc->tsc', selector, kernel, precision=HIGHEST_PRECISION)]
    all_gather x15 -> x0, blocking collectives: 147 us -> none  [the longest x6 56.8 us: entering_2(): pieces = jax.tree.map(lambda part: lax.all_gather(part, axis), value)]
    dot_general x31 -> x0, other arithmetic: 129 us -> none  [the longest x12 65.1 us: ssm_block(): jnp.einsum('tcn,cn->tc', after, read_out * state, precision=HIGHEST_PRECI...]
    add_any x24 -> x0, other arithmetic: 112 us -> none  [the longest x18 103 us: local_scan(): lax.scan(stepper, start_state, (input_rows.reshape(blocks, length, -1), s...]
    reduce_scatter x7 -> x0, waiting for transfers between devices: 101 us -> none  [the longest x4 97.8 us: local(): lax.psum_scatter(shortened(totals), 'dp', scatter_dimension=0, tiled=True)]
    pallas_call x0 -> x42, Pallas kernels: none -> 65 us  [__call__(): pl.pallas_call(run, out_shape=[jax.ShapeDtypeStruct(s, d) for s, d in out...]
    ppermute x4 -> x65, starting transfers between devices: 7.54 us -> 69.4 us  [the longest x52 66.1 us: paired(): return lax.ppermute(part, axis, [(i, i ^ s) for i in range(n)])]
  transfers between devices with their start and end apart: 19 -> 65, of which waited for: 11 -> 19; matrix products, arithmetic and copies ran while one was open for 12% -> 0% of each run, Pallas kernels for 0% -> 33%
where the time goes in v1:
time: 168 us
  starting transfers between devices  69.4 us (41%)
  Pallas kernels  65 us (39%)
  waiting for transfers between devices  30.6 us (18%)
    ppermute x52, starting transfers between devices, paired(): return lax.ppermute(part, axis, [(i, i ^ s) for i in range(n)])  66.1 us
    pallas_call x42, Pallas kernels, __call__(): pl.pallas_call(run, out_shape=[jax.ShapeDtypeStruct(s, d) for s, d in out...  65 us
    ppermute x52, waiting for transfers between devices, paired(): return lax.ppermute(part, axis, [(i, i ^ s) for i in range(n)])  29.5 us
  transfers between devices with their start and end apart: 65, of which 19 were waited for; matrix products, arithmetic and copies ran while one was open for 0% of the time, Pallas kernels for 33%

profile of v1, /device:TPU:0, one launch (start us, length us, event | category | flops | bytes accessed | tf_op | source)
XLA Modules:
  0.0 167.9 jit_solution(6265143707835701597)
XLA Ops:
  1.2 2.4 %make_pack.1.refs_2_ = f32[64,640]{1,0:T(8,128)} custom-call(s32[2,3]{1,0:T(2,128)} %refs_0_.83, f32[64,128]{1,0:T(8,128)} %bitcast.25, f32[64,128]{1,0:T(8,128)} %bitcast.26, f32[64,128]{1,0:T(8,128)} %bitcast.27, f32[1,1024]{1,0:T(1,128)} %refs_4_.1, f32[1,1024]{1,0:T(1,128)} %refs_5_.1, f32[1,1024]{1,0:T(1,128)} %refs_6_.2, f32[1,768]{1,0:T(1,128)} %refs_7_.1, ...), custom_call_target="tpu_custom_call" | custom-call | flops 40000000000 | bytes 1 | tf_op jit(solution)/shard_map/make_pack/pallas_call | solution.py:108
  5.3 2.0 %front0.1 = (bf16[256,1024]{1,0:T(8,128)(2,1)S(1)}, f32[256,128]{1,0:T(8,128)S(1)}, f32[256,128]{1,0:T(8,128)S(1)}, f32[64,128]{1,0:T(8,128)S(1)}, f32[64,640]{1...) custom-call(s32[2,3]{1,0:T(2,128)S(1)} %copy-done.11, ...), custom_call_target="tpu_custom_call" | custom-call | flops 40000000000 | bytes 1 | tf_op jit(solution)/shard_map/front0/pallas_call | solution.py:108
  7.4 3.5 %collective-permute-start.2 = (f32[64,128]{1,0:T(8,128)S(1)}, f32[64,128]{1,0:T(8,128)S(1)}, u32[]{:S(2)}, u32[]{:S(2)}) collective-permute-start(f32[64,128]{1,0:T(8,128)S(1)} %get-tuple-element.147), channel_id=1, source_target_pairs={{0,3},{1,2},{2,1},{3,0},{4,7},{5,6},{6,5},{7,4},{8,11},{9,10},{10,... | collective-permute-start | bytes 98312 | tf_op jit(solution)/shard_map/ppermute | solution.py:336
  12.1 1.3 wide0.1
  13.4 1.5 collective-permute-done.3.refs_4_
  15.3 2.2 %carry0.1 = (f32[64,128]{1,0:T(8,128)S(1)}, bf16[256,128]{1,0:T(8,128)(2,1)S(1)}) custom-call(s32[2,3]{1,0:T(2,128)S(1)} %copy-done.11, f32[256,128]{1,0:T(8,128)S(1)} %get-tuple-element.145.refs_1_, f32[64,640]{1,0:T(8,128)S(1)} %get-tuple-element.146.refs_2_.refs_6_.refs_1_.refs_3_.refs_4_, f32[64,128]{1,0:T(8,128)S(1)} %collective-permute-done.2.refs_3_, ...), custom_call_target="tpu_custom_call" | custom-call | flops 40000000000 | bytes 1 | tf_op jit(solution)/shard_map/carry0/pallas_call | solution.py:108
  17.5 3.7 %collective-permute-start.6 = (bf16[256,128]{1,0:T(8,128)(2,1)S(1)}, bf16[256,128]{1,0:T(8,128)(2,1)S(1)}, u32[]{:S(2)}, u32[]{:S(2)}) collective-permute-start(bf16[256,128]{1,0:T(8,128)(2,1)S(1)} %get-tuple-element.149.refs_5_.refs_1_), channel_id=1, source_target_pairs={{0,12},{4,8},{8,4},{12,0},{1,13},{5,9},{9,5},{13,1},{2,14},{6,10},... | collective-permute-start | bytes 196616 | tf_op jit(solution)/shard_map/ppermute | solution.py:336
  23.6 2.7 %collective-permute-done.7.refs_3_ = bf16[256,128]{1,0:T(8,128)(2,1)S(1)} collective-permute-done((bf16[256,128]{1,0:T(8,128)(2,1)S(1)}, bf16[256,128]{1,0:T(8,128)(2,1)S(1)}, u32[]{:S(2)}, u32[]{:S(2)}) %collective-permute-start.7) | collective-permute-done | bytes 65568 | tf_op jit(solution)/shard_map/ppermute | solution.py:336
  26.4 1.5 middle0.1
  27.9 2.2 %collective-permute-start.11 = (bf16[256,256]{1,0:T(8,128)(2,1)S(1)}, bf16[256,256]{1,0:T(8,128)(2,1)S(1)}, u32[]{:S(2)}, u32[]{:S(2)}) collective-permute-start(bf16[256,256]{1,0:T(8,128)(2,1)S(1)} %get-tuple-element.155), channel_id=1, source_target_pairs={{0,12},{4,8},{8,4},{12,0},{1,13},{5,9},{9,5},{13,1},{2,14},{6,10},... | collective-permute-start | bytes 393224 | tf_op jit(solution)/shard_map/ppermute | solution.py:336
  30.1 2.3 %collective-permute-start.13 = (bf16[256,256]{1,0:T(8,128)(2,1)S(1)}, bf16[256,256]{1,0:T(8,128)(2,1)S(1)}, u32[]{:S(2)}, u32[]{:S(2)}) collective-permute-start(bf16[256,256]{1,0:T(8,128)(2,1)S(1)} %get-tuple-element.157), channel_id=1, source_target_pairs={{0,4},{4,0},{8,12},{12,8},{1,5},{5,1},{9,13},{13,9},{2,6},{6,2},{1... | collective-permute-start | bytes 393224 | tf_op jit(solution)/shard_map/ppermute | solution.py:336
  33.6 1.2 grad_gated1.1
  34.8 1.4 collective-permute-done.11.refs_3_
  36.2 3.9 %collective-permute-done.12.refs_4_ = bf16[256,256]{1,0:T(8,128)(2,1)S(1)} collective-permute-done((bf16[256,256]{1,0:T(8,128)(2,1)S(1)}, bf16[256,256]{1,0:T(8,128)(2,1)S(1)}, u32[]{:S(2)}, u32[]{:S(2)}) %collective-permute-start.12) | collective-permute-done | bytes 131104 | tf_op jit(solution)/shard_map/ppermute | solution.py:336
  40.9 2.5 %collective-permute-start.17 = (bf16[256,256]{1,0:T(8,128)(2,1)S(1)}, bf16[256,256]{1,0:T(8,128)(2,1)S(1)}, u32[]{:S(2)}, u32[]{:S(2)}) collective-permute-start(bf16[256,256]{1,0:T(8,128)(2,1)S(1)} %get-tuple-element.160.refs_4_.refs_1_), channel_id=1, source_target_pairs={{0,4},{4,0},{8,12},{12,8},{1,5},{5,1},{9,13},{13,9},{2,6},{6,2},{1... | collective-permute-start | bytes 393224 | tf_op jit(solution)/shard_map/ppermute | solution.py:336
  43.4 4.4 %collective-permute-done.15.refs_3_ = bf16[256,256]{1,0:T(8,128)(2,1)S(1)} collective-permute-done((bf16[256,256]{1,0:T(8,128)(2,1)S(1)}, bf16[256,256]{1,0:T(8,128)(2,1)S(1)}, u32[]{:S(2)}, u32[]{:S(2)}) %collective-permute-start.15) | collective-permute-done | bytes 131104 | tf_op jit(solution)/shard_map/ppermute | solution.py:336
  48.8 3.9 %collective-permute-done.16.refs_2_ = bf16[256,256]{1,0:T(8,128)(2,1)S(1)} collective-permute-done((bf16[256,256]{1,0:T(8,128)(2,1)S(1)}, bf16[256,256]{1,0:T(8,128)(2,1)S(1)}, u32[]{:S(2)}, u32[]{:S(2)}) %collective-permute-start.16) | collective-permute-done | bytes 131104 | tf_op jit(solution)/shard_map/ppermute | solution.py:336
  52.7 2.5 %front1.1 = (bf16[256,1024]{1,0:T(8,128)(2,1)S(1)}, f32[256,128]{1,0:T(8,128)S(1)}, f32[256,128]{1,0:T(8,128)S(1)}, f32[64,128]{1,0:T(8,128)S(1)}, f32[256,1024]{1,0:T(8,128)S(1)}, /*index=5*/f32[256,128]{1,0:T(8,128)S(1)}) custom-call(s32[2,3]{1,0:T(2,128)S(1)} %copy-done.11, bf16[256,256]{1,0:T(8,128)(2,1)S(1)} %get-tuple-element.160.refs_4_.refs_1_, ...), custom_call_target="tpu_custom_call" | custom-call | flops 40000000000 | bytes 1 | tf_op jit(solution)/shard_map/front1/pallas_call | solution.py:108
  55.2 2.9 %collective-permute-start.18 = (f32[64,128]{1,0:T(8,128)S(1)}, f32[64,128]{1,0:T(8,128)S(1)}, u32[]{:S(2)}, u32[]{:S(2)}) collective-permute-start(f32[64,128]{1,0:T(8,128)S(1)} %get-tuple-element.164.refs_6_), channel_id=1, source_target_pairs={{0,3},{1,2},{2,1},{3,0},{4,7},{5,6},{6,5},{7,4},{8,11},{9,10},{10,... | collective-permute-start | bytes 98312 | tf_op jit(solution)/shard_map/ppermute | solution.py:336
  58.7 2.0 %wide1.1 = (f32[256,768]{1,0:T(8,128)S(1)}, bf16[256,768]{1,0:T(8,128)(2,1)S(1)}, f32[256,128]{1,0:T(8,128)S(1)}, bf16[256,128]{1,0:T(8,128)(2,1)S(1)}, bf16[256...) custom-call(s32[2,3]{1,0:T(2,128)S(1)} %copy-done.11, bf16[256,1024]{1,0:T(8,128)(2,1)S(1)} %get-tuple-element.165.refs_1_, ...), custom_call_target="tpu_custom_call" | custom-call | flops 40000000000 | bytes 1 | tf_op jit(solution)/shard_map/wide1/pallas_call | solution.py:108
  60.7 2.2 %collective-permute-start.24 = (bf16[256,128]{1,0:T(8,128)(2,1)S(1)}, bf16[256,128]{1,0:T(8,128)(2,1)S(1)}, u32[]{:S(2)}, u32[]{:S(2)}) collective-permute-start(bf16[256,128]{1,0:T(8,128)(2,1)S(1)} %get-tuple-element.172), channel_id=1, source_target_pairs={{0,12},{4,8},{8,4},{12,0},{1,13},{5,9},{9,5},{13,1},{2,14},{6,10},... | collective-permute-start | bytes 196616 | tf_op jit(solution)/shard_map/ppermute | solution.py:336
  62.9 2.3 %collective-permute-start.26 = (bf16[256,128]{1,0:T(8,128)(2,1)S(1)}, bf16[256,128]{1,0:T(8,128)(2,1)S(1)}, u32[]{:S(2)}, u32[]{:S(2)}) collective-permute-start(bf16[256,128]{1,0:T(8,128)(2,1)S(1)} %get-tuple-element.174), channel_id=1, source_target_pairs={{0,4},{4,0},{8,12},{12,8},{1,5},{5,1},{9,13},{13,9},{2,6},{6,2},{1... | collective-permute-start | bytes 196616 | tf_op jit(solution)/shard_map/ppermute | solution.py:336
  65.2 2.2 %carry1.1 = (f32[64,128]{1,0:T(8,128)S(1)}, bf16[256,128]{1,0:T(8,128)(2,1)S(1)}) custom-call(s32[2,3]{1,0:T(2,128)S(1)} %copy-done.11, f32[256,128]{1,0:T(8,128)S(1)} %get-tuple-element.163.refs_1_, f32[64,640]{1,0:T(8,128)S(1)} %get-tuple-element.161.refs_5_.refs_3_.refs_2_.refs_7_.refs_1_.refs_4_.refs_6_, f32[64,128]{1,0:T(8,128)S(1)} %collective-permute-done.18.refs_3_, ...), custom_call_target="tpu_custom_call" | custom-call | flops 40000000000 | bytes 1 | tf_op jit(solution)/shard_map/carry1/pallas_call | solution.py:108
  67.4 2.2 %collective-permute-start.21 = (bf16[256,128]{1,0:T(8,128)(2,1)S(1)}, bf16[256,128]{1,0:T(8,128)(2,1)S(1)}, u32[]{:S(2)}, u32[]{:S(2)}) collective-permute-start(bf16[256,128]{1,0:T(8,128)(2,1)S(1)} %get-tuple-element.169.refs_1_.refs_6_), channel_id=1, source_target_pairs={{0,12},{4,8},{8,4},{12,0},{1,13},{5,9},{9,5},{13,1},{2,14},{6,10},... | collective-permute-start | bytes 196616 | tf_op jit(solution)/shard_map/ppermute | solution.py:336
  70.5 1.3 collective-permute-start.23
  71.9 1.6 adjoint_local1.1
  73.5 2.7 %collective-permute-start.27 = (f32[64,128]{1,0:T(8,128)S(1)}, f32[64,128]{1,0:T(8,128)S(1)}, u32[]{:S(2)}, u32[]{:S(2)}) collective-permute-start(f32[64,128]{1,0:T(8,128)S(1)} %get-tuple-element.177), channel_id=1, source_target_pairs={{0,3},{1,2},{2,1},{3,0},{4,7},{5,6},{6,5},{7,4},{8,11},{9,10},{10,... | collective-permute-start | bytes 98312 | tf_op jit(solution)/shard_map/ppermute | solution.py:336
  77.1 1.5 middle1.1
  78.5 1.6 collective-permute-done.28.refs_5_
  80.2 2.4 %adjoint1.1 = (f32[64,128]{1,0:T(8,128)S(1)}, bf16[256,128]{1,0:T(8,128)(2,1)S(1)}) custom-call(s32[2,3]{1,0:T(2,128)S(1)} %copy-done.11, f32[256,128]{1,0:T(8,128)S(1)} %get-tuple-element.175.refs_1_.refs_3_, f32[256,128]{1,0:T(8,128)S(1)} %get-tuple-element.176.refs_2_, ...), custom_call_target="tpu_custom_call" | custom-call | flops 40000000000 | bytes 1 | tf_op jit(solution)/shard_map/adjoint1/pallas_call | solution.py:108
  82.6 1.9 %grad_normed1.1 = (f32[272,256]{1,0:T(8,128)S(1)}, bf16[272,256]{1,0:T(8,128)(2,1)S(1)}, bf16[272,256]{1,0:T(8,128)(2,1)S(1)}, bf16[272,256]{1,0:T(8,128)(2,1)S(1)}) custom-call(s32[2,3]{1,0:T(2,128)S(1)} %copy-done.11, bf16[256,768]{1,0:T(8,128)(2,1)S(1)} %get-tuple-element.171.refs_7_.refs_1_, bf16[256,128]{1,0:T(8,128)(2,1)S(1)} %get-tuple-element.178.refs_2_.refs_5_, ...), custom_call_target="tpu_custom_call" | custom-call | flops 40000000000 | bytes 1 | tf_op jit(solution)/shard_map/grad_normed1/pallas_call | solution.py:108
  84.4 2.1 %collective-permute-start.30 = (bf16[272,256]{1,0:T(8,128)(2,1)S(1)}, bf16[272,256]{1,0:T(8,128)(2,1)S(1)}, u32[]{:S(2)}, u32[]{:S(2)}) collective-permute-start(bf16[272,256]{1,0:T(8,128)(2,1)S(1)} %get-tuple-element.181), channel_id=1, source_target_pairs={{0,12},{4,8},{8,4},{12,0},{1,13},{5,9},{9,5},{13,1},{2,14},{6,10},... | collective-permute-start | bytes 417800 | tf_op jit(solution)/shard_map/ppermute | solution.py:336
  86.7 2.2 %collective-permute-start.32 = (bf16[272,256]{1,0:T(8,128)(2,1)S(1)}, bf16[272,256]{1,0:T(8,128)(2,1)S(1)}, u32[]{:S(2)}, u32[]{:S(2)}) collective-permute-start(bf16[272,256]{1,0:T(8,128)(2,1)S(1)} %get-tuple-element.183), channel_id=1, source_target_pairs={{0,4},{4,0},{8,12},{12,8},{1,5},{5,1},{9,13},{13,9},{2,6},{6,2},{1... | collective-permute-start | bytes 417800 | tf_op jit(solution)/shard_map/ppermute | solution.py:336
  91.1 3.8 %ssm_grads1.1.refs_9_.refs_7_ = f32[640,256]{1,0:T(8,128)S(1)} custom-call(s32[2,3]{1,0:T(2,128)S(1)} %copy-done.11, f32[256,128]{1,0:T(8,128)S(1)} %copy-done.14, f32[64,128]{1,0:T(8,128)S(1)} %get-tuple-element.185.refs_2_, f32[256,128]{1,0:T(8,128)S(1)} %get-tuple-element.175.refs_1_.refs_3_, f32[64,128]{1,0:T(8,128)S(1)} %get-tuple-element.186.refs_4_, ...), custom_call_target="tpu_custom_call" | custom-call | flops 1 | bytes 1 | tf_op jit(solution)/shard_map/ssm_grads1/pallas_call | solution.py:108
  94.9 1.4 layer_grad1.1
  96.3 2.1 %collective-permute-start.33 = (bf16[256,256]{1,0:T(8,128)(2,1)S(1)}, bf16[256,256]{1,0:T(8,128)(2,1)S(1)}, u32[]{:S(2)}, u32[]{:S(2)}) collective-permute-start(bf16[256,256]{1,0:T(8,128)(2,1)S(1)} %get-tuple-element.192.refs_5_.refs_1_), channel_id=1, source_target_pairs={{0,12},{4,8},{8,4},{12,0},{1,13},{5,9},{9,5},{13,1},{2,14},{6,10},... | collective-permute-start | bytes 393224 | tf_op jit(solution)/shard_map/ppermute | solution.py:336
  98.4 2.4 %collective-permute-start.35 = (bf16[256,256]{1,0:T(8,128)(2,1)S(1)}, bf16[256,256]{1,0:T(8,128)(2,1)S(1)}, u32[]{:S(2)}, u32[]{:S(2)}) collective-permute-start(bf16[256,256]{1,0:T(8,128)(2,1)S(1)} %get-tuple-element.192.refs_5_.refs_1_), channel_id=1, source_target_pairs={{0,4},{4,0},{8,12},{12,8},{1,5},{5,1},{9,13},{13,9},{2,6},{6,2},{1... | collective-permute-start | bytes 393224 | tf_op jit(solution)/shard_map/ppermute | solution.py:336
  100.8 2.0 %weight_grads1.1 = (bf16[2,1024,128]{2,1,0:T(8,128)(2,1)S(1)}, bf16[2,1024,128]{2,1,0:T(8,128)(2,1)S(1)}, bf16[2,912,128]{2,1,0:T(8,128)(2,1)S(1)}, bf16[2,912,128]{2,1,0:T(8,128)(2,1)S(1)}) custom-call(s32[2,3]{1,0:T(2,128)S(1)} %copy-done.11, bf16[2304,256]{1,0:T(8,128)(2,1)S(1)} %turn1.1.refs_4_.refs_7_.refs_1_, ...), custom_call_target="tpu_custom_call" | custom-call | flops 1 | bytes 1 | tf_op jit(solution)/shard_map/weight_grads1/pallas_call | solution.py:108
  102.9 1.1 top_parts.1
  104.6 1.4 collective-permute-start.43
  105.9 3.8 %collective-permute-done.34.refs_3_ = bf16[256,256]{1,0:T(8,128)(2,1)S(1)} collective-permute-done((bf16[256,256]{1,0:T(8,128)(2,1)S(1)}, bf16[256,256]{1,0:T(8,128)(2,1)S(1)}, u32[]{:S(2)}, u32[]{:S(2)}) %collective-permute-start.34) | collective-permute-done | bytes 131104 | tf_op jit(solution)/shard_map/ppermute | solution.py:336
  109.7 2.4 %grad_middle0.1 = (bf16[256,768]{1,0:T(8,128)(2,1)S(1)}, bf16[256,768]{1,0:T(8,128)(2,1)S(1)}, bf16[256,1024]{1,0:T(8,128)(2,1)S(1)}, f32[256,128]{1,0:T(8,128)S...) custom-call(s32[2,3]{1,0:T(2,128)S(1)} %copy-done.11, ...), custom_call_target="tpu_custom_call" | custom-call | flops 40000000000 | bytes 1 | tf_op jit(solution)/shard_map/grad_middle0/pallas_call | solution.py:108
  112.1 2.1 %collective-permute-start.39 = (bf16[256,128]{1,0:T(8,128)(2,1)S(1)}, bf16[256,128]{1,0:T(8,128)(2,1)S(1)}, u32[]{:S(2)}, u32[]{:S(2)}) collective-permute-start(bf16[256,128]{1,0:T(8,128)(2,1)S(1)} %get-tuple-element.203), channel_id=1, source_target_pairs={{0,12},{4,8},{8,4},{12,0},{1,13},{5,9},{9,5},{13,1},{2,14},{6,10},... | collective-permute-start | bytes 196616 | tf_op jit(solution)/shard_map/ppermute | solution.py:336
  114.2 2.4 %collective-permute-start.41 = (bf16[256,128]{1,0:T(8,128)(2,1)S(1)}, bf16[256,128]{1,0:T(8,128)(2,1)S(1)}, u32[]{:S(2)}, u32[]{:S(2)}) collective-permute-start(bf16[256,128]{1,0:T(8,128)(2,1)S(1)} %get-tuple-element.205), channel_id=1, source_target_pairs={{0,4},{4,0},{8,12},{12,8},{1,5},{5,1},{9,13},{13,9},{2,6},{6,2},{1... | collective-permute-start | bytes 196616 | tf_op jit(solution)/shard_map/ppermute | solution.py:336
  118.1 1.7 %collective-permute-start.49 = (bf16[1,1024,128]{2,1,0:T(8,128)(2,1)S(1)}, bf16[1,1024,128]{2,1,0:T(8,128)(2,1)S(1)}, u32[]{:S(2)}, u32[]{:S(2)}) collective-permute-start(bf16[1,1024,128]{2,1,0:T(8,128)(2,1)S(1)} %get-tuple-element.217), channel_id=1, source_target_pairs={{0,2},{1,3},{2,0},{3,1},{4,6},{5,7},{6,4},{7,5},{8,10},{9,11},{10,... | collective-permute-start | bytes 786440 | tf_op jit(solution)/shard_map/ppermute | solution.py:336
  120.6 1.6 adjoint_local0.1
  122.2 1.3 collective-permute-start.46
  123.5 1.4 collective-permute-start.47
  125.7 2.0 %weight_grads0.1 = (bf16[2,1024,128]{2,1,0:T(8,128)(2,1)S(1)}, bf16[2,1024,128]{2,1,0:T(8,128)(2,1)S(1)}, bf16[2,912,128]{2,1,0:T(8,128)(2,1)S(1)}, bf16[2,912,128]{2,1,0:T(8,128)(2,1)S(1)}) custom-call(s32[2,3]{1,0:T(2,128)S(1)} %copy-done.11, bf16[2304,256]{1,0:T(8,128)(2,1)S(1)} %copy-done.3, bf16[2304,256]{1,0:T(8,128)(2,1)S(1)} %copy-done.7, ...), custom_call_target="tpu_custom_call" | custom-call | flops 1 | bytes 1 | tf_op jit(solution)/shard_map/weight_grads0/pallas_call | solution.py:108
  129.2 1.7 collective-permute-start.45
  130.8 2.4 %adjoint0.1 = (f32[64,128]{1,0:T(8,128)S(1)}, bf16[256,128]{1,0:T(8,128)(2,1)S(1)}) custom-call(s32[2,3]{1,0:T(2,128)S(1)} %copy-done.11, f32[256,128]{1,0:T(8,128)S(1)} %get-tuple-element.215.refs_1_.refs_3_, f32[256,128]{1,0:T(8,128)S(1)} %get-tuple-element.216.refs_2_, f32[64,640]{1,0:T(8,128)S(1)} %get-tuple-element.146.refs_2_.refs_6_.refs_1_.refs_3_.refs_4_, ...), custom_call_target="tpu_custom_call" | custom-call | flops 40000000000 | bytes 1 | tf_op jit(solution)/shard_map/adjoint0/pallas_call | solution.py:108
  133.2 1.9 %grad_normed0.1 = (f32[272,256]{1,0:T(8,128)S(1)}, bf16[272,256]{1,0:T(8,128)(2,1)S(1)}, bf16[272,256]{1,0:T(8,128)(2,1)S(1)}, bf16[272,256]{1,0:T(8,128)(2,1)S(1)}) custom-call(s32[2,3]{1,0:T(2,128)S(1)} %copy-done.11, bf16[256,768]{1,0:T(8,128)(2,1)S(1)} %get-tuple-element.197.refs_1_, bf16[256,128]{1,0:T(8,128)(2,1)S(1)} %get-tuple-element.219.refs_2_.refs_5_, ...), custom_call_target="tpu_custom_call" | custom-call | flops 40000000000 | bytes 1 | tf_op jit(solution)/shard_map/grad_normed0/pallas_call | solution.py:108
  135.1 2.1 %collective-permute-start.55 = (bf16[272,256]{1,0:T(8,128)(2,1)S(1)}, bf16[272,256]{1,0:T(8,128)(2,1)S(1)}, u32[]{:S(2)}, u32[]{:S(2)}) collective-permute-start(bf16[272,256]{1,0:T(8,128)(2,1)S(1)} %get-tuple-element.233), channel_id=1, source_target_pairs={{0,12},{4,8},{8,4},{12,0},{1,13},{5,9},{9,5},{13,1},{2,14},{6,10},... | collective-permute-start | bytes 417800 | tf_op jit(solution)/shard_map/ppermute | solution.py:336
  137.2 1.2 collective-permute-start.56
  138.4 1.2 collective-permute-start.57
  139.5 1.5 collective-permute-done.45.refs_4_
  142.3 1.7 %collective-permute-start.52 = (bf16[1,1024,128]{2,1,0:T(8,128)(2,1)S(1)}, bf16[1,1024,128]{2,1,0:T(8,128)(2,1)S(1)}, u32[]{:S(2)}, u32[]{:S(2)}) collective-permute-start(bf16[1,1024,128]{2,1,0:T(8,128)(2,1)S(1)} %get-tuple-element.225), channel_id=1, source_target_pairs={{0,2},{1,3},{2,0},{3,1},{4,6},{5,7},{6,4},{7,5},{8,10},{9,11},{10,... | collective-permute-start | bytes 786440 | tf_op jit(solution)/shard_map/ppermute | solution.py:336
  144.5 3.8 %ssm_grads0.1 = (f32[640,256]{1,0:T(8,128)S(1)}, f32[640,256]{1,0:T(8,128)S(1)}) custom-call(s32[2,3]{1,0:T(2,128)S(1)} %copy-done.11, f32[256,128]{1,0:T(8,128)S(1)} %copy-done.22, f32[64,128]{1,0:T(8,128)S(1)} %get-tuple-element.229.refs_2_, f32[256,128]{1,0:T(8,128)S(1)} %get-tuple-element.215.refs_1_.refs_3_, f32[64,128]{1,0:T(8,128)S(1)} %get-tuple-element.230.refs_4_, ...), custom_call_target="tpu_custom_call" | custom-call | flops 40000000000 | bytes 1 | tf_op jit(solution)/shard_map/ssm_grads0/pallas_call | solution.py:108
  150.1 1.2 layer_grad0.1
  151.6 2.0 %collective-permute-start.63 = (bf16[1,256,256]{2,1,0:T(8,128)(2,1)S(1)}, bf16[1,256,256]{2,1,0:T(8,128)(2,1)S(1)}, u32[]{:S(2)}, u32[]{:S(2)}) collective-permute-start(bf16[1,256,256]{2,1,0:T(8,128)(2,1)S(1)} %get-tuple-element.250), channel_id=1, source_target_pairs={{0,8},{4,12},{8,0},{12,4},{1,9},{5,13},{9,1},{13,5},{2,10},{6,14},... | collective-permute-start | bytes 393224 | tf_op jit(solution)/shard_map/ppermute | solution.py:336
  155.2 1.8 %collective-permute-start.61 = (bf16[464,128]{1,0:T(8,128)(2,1)S(1)}, bf16[464,128]{1,0:T(8,128)(2,1)S(1)}, u32[]{:S(2)}, u32[]{:S(2)}) collective-permute-start(bf16[464,128]{1,0:T(8,128)(2,1)S(1)} %get-tuple-element.245), channel_id=1, source_target_pairs={{0,2},{1,3},{2,0},{3,1},{4,6},{5,7},{6,4},{7,5},{8,10},{9,11},{10,... | collective-permute-start | bytes 356360 | tf_op jit(solution)/shard_map/ppermute | solution.py:336
  158.6 1.8 %own_columns.1 = (f32[1,256,768]{2,1,0:T(8,128)}, f32[1,128,768]{2,1,0:T(8,128)}, f32[1,192,1024]{2,1,0:T(8,128)}, f32[1,2,256,256]{3,2,1,0:T(8,128)}) custom-call(s32[2,3]{1,0:T(2,128)S(1)} %copy-done.11, bf16[272,256]{1,0:T(8,128)(2,1)S(1)} %collective-permute-done.58.refs_4_.refs_1_, f32[1936,128]{1,0:T(8,128)S(1)} %get-tuple-element.242.refs_2_.refs_1_, ...), custom_call_target="tpu_custom_call" | custom-call | flops 1 | bytes 1 | tf_op jit(solution)/shard_map/own_columns/pallas_call | solution.py:108
  161.0 1.1 copy-done.5
  165.1 2.6 %finish.1 = (f32[1,256,768]{2,1,0:T(8,128)}, f32[1,128,768]{2,1,0:T(8,128)}, f32[1,192,1024]{2,1,0:T(8,128)}, f32[1,192]{1,0:T(1,128)}, f32[1,192]{1,0:T(1,128)}...) custom-call(s32[2,3]{1,0:T(2,128)S(1)} %copy-done.11, ...), custom_call_target="tpu_custom_call", output_to_operand_aliasing={{0}: (4, {}), {1}: (5, {}), {2}: (6, {})} | custom-call | flops 1 | bytes 1 | tf_op jit(solution)/shard_map/finish/pallas_call | solution.py:108
  (154 shorter events, 29.7 us)
Async XLA Ops:
  0.6 4.6 %collective-permute-start.1 = (bf16[1024,128]{1,0:T(8,128)(2,1)}, bf16[1024,128]{1,0:T(8,128)(2,1)S(1)}, u32[]{:S(2)}, u32[]{:S(2)}) collective-permute-start(bf16[1024,128]{1,0:T(8,128)(2,1)} %bitcast.22), channel_id=1, source_target_pairs={{0,16},{16,0},{1,17},{17,1},{2,18},{18,2},{3,19},{19,3},{4,20},{20... | collective-permute-start | bytes 786440 | tf_op jit(solution)/shard_map/ppermute | solution.py:279
  3.6 1.7 %collective-permute-start = (f32[64,640]{1,0:T(8,128)}, f32[64,640]{1,0:T(8,128)S(1)}, u32[]{:S(2)}, u32[]{:S(2)}) collective-permute-start(f32[64,640]{1,0:T(8,128)} %make_pack.1.refs_2_), channel_id=1, source_target_pairs={{0,16},{16,0},{1,17},{17,1},{2,18},{18,2},{3,19},{19,3},{4,20},{20... | collective-permute-start | bytes 491528 | tf_op jit(solution)/shard_map/ppermute | solution.py:279
  3.7 7.8 %collective-permute-start.5 = (bf16[1024,768]{1,0:T(8,128)(2,1)S(1)}, bf16[1024,768]{1,0:T(8,128)(2,1)S(1)}, u32[]{:S(2)}, u32[]{:S(2)}) collective-permute-start(bf16[1024,768]{1,0:T(8,128)(2,1)S(1)} %bitcast.13), channel_id=1, source_target_pairs={{0,16},{16,0},{1,17},{17,1},{2,18},{18,2},{3,19},{19,3},{4,20},{20... | collective-permute-start | bytes 4718600 | tf_op jit(solution)/shard_map/ppermute | solution.py:279
  7.4 6.0 %collective-permute-start.2 = (f32[64,128]{1,0:T(8,128)S(1)}, f32[64,128]{1,0:T(8,128)S(1)}, u32[]{:S(2)}, u32[]{:S(2)}) collective-permute-start(f32[64,128]{1,0:T(8,128)S(1)} %get-tuple-element.147), channel_id=1, source_target_pairs={{0,3},{1,2},{2,1},{3,0},{4,7},{5,6},{6,5},{7,4},{8,11},{9,10},{10,... | collective-permute-start | bytes 98312 | tf_op jit(solution)/shard_map/ppermute | solution.py:336
  10.9 3.9 %collective-permute-start.3 = (f32[64,128]{1,0:T(8,128)S(1)}, f32[64,128]{1,0:T(8,128)S(1)}, u32[]{:S(2)}, u32[]{:S(2)}) collective-permute-start(f32[64,128]{1,0:T(8,128)S(1)} %get-tuple-element.147), channel_id=1, source_target_pairs={{0,2},{1,3},{2,0},{3,1},{4,6},{5,7},{6,4},{7,5},{8,10},{9,11},{10,... | collective-permute-start | bytes 98312 | tf_op jit(solution)/shard_map/ppermute | solution.py:336
  11.3 3.9 %collective-permute-start.4 = (f32[64,128]{1,0:T(8,128)S(1)}, f32[64,128]{1,0:T(8,128)S(1)}, u32[]{:S(2)}, u32[]{:S(2)}) collective-permute-start(f32[64,128]{1,0:T(8,128)S(1)} %get-tuple-element.147), channel_id=1, source_target_pairs={{0,1},{1,0},{2,3},{3,2},{4,5},{5,4},{6,7},{7,6},{8,9},{9,8},{10,11... | collective-permute-start | bytes 98312 | tf_op jit(solution)/shard_map/ppermute | solution.py:336
  11.6 10.4 %collective-permute-start.10 = (bf16[768,1024]{1,0:T(8,128)(2,1)S(1)}, bf16[768,1024]{1,0:T(8,128)(2,1)S(1)}, u32[]{:S(2)}, u32[]{:S(2)}) collective-permute-start(bf16[768,1024]{1,0:T(8,128)(2,1)S(1)} %bitcast.16), channel_id=1, source_target_pairs={{0,16},{16,0},{1,17},{17,1},{2,18},{18,2},{3,19},{19,3},{4,20},{20... | collective-permute-start | bytes 4718600 | tf_op jit(solution)/shard_map/ppermute | solution.py:279
  11.6 10.4 %collective-permute-start.9 = (bf16[512,768]{1,0:T(8,128)(2,1)S(1)}, bf16[512,768]{1,0:T(8,128)(2,1)S(1)}, u32[]{:S(2)}, u32[]{:S(2)}) collective-permute-start(bf16[512,768]{1,0:T(8,128)(2,1)S(1)} %bitcast.19), channel_id=1, source_target_pairs={{0,16},{16,0},{1,17},{17,1},{2,18},{18,2},{3,19},{19,3},{4,20},{20... | collective-permute-start | bytes 2359304 | tf_op jit(solution)/shard_map/ppermute | solution.py:279
  17.5 6.2 %collective-permute-start.6 = (bf16[256,128]{1,0:T(8,128)(2,1)S(1)}, bf16[256,128]{1,0:T(8,128)(2,1)S(1)}, u32[]{:S(2)}, u32[]{:S(2)}) collective-permute-start(bf16[256,128]{1,0:T(8,128)(2,1)S(1)} %get-tuple-element.149.refs_5_.refs_1_), channel_id=1, source_target_pairs={{0,12},{4,8},{8,4},{12,0},{1,13},{5,9},{9,5},{13,1},{2,14},{6,10},... | collective-permute-start | bytes 196616 | tf_op jit(solution)/shard_map/ppermute | solution.py:336
  21.2 5.2 %collective-permute-start.7 = (bf16[256,128]{1,0:T(8,128)(2,1)S(1)}, bf16[256,128]{1,0:T(8,128)(2,1)S(1)}, u32[]{:S(2)}, u32[]{:S(2)}) collective-permute-start(bf16[256,128]{1,0:T(8,128)(2,1)S(1)} %get-tuple-element.149.refs_5_.refs_1_), channel_id=1, source_target_pairs={{0,8},{4,12},{8,0},{12,4},{1,9},{5,13},{9,1},{13,5},{2,10},{6,14},... | collective-permute-start | bytes 196616 | tf_op jit(solution)/shard_map/ppermute | solution.py:336
  21.2 5.2 %collective-permute-start.8 = (bf16[256,128]{1,0:T(8,128)(2,1)S(1)}, bf16[256,128]{1,0:T(8,128)(2,1)S(1)}, u32[]{:S(2)}, u32[]{:S(2)}) collective-permute-start(bf16[256,128]{1,0:T(8,128)(2,1)S(1)} %get-tuple-element.149.refs_5_.refs_1_), channel_id=1, source_target_pairs={{0,4},{4,0},{8,12},{12,8},{1,5},{5,1},{9,13},{13,9},{2,6},{6,2},{1... | collective-permute-start | bytes 196616 | tf_op jit(solution)/shard_map/ppermute | solution.py:336
  27.9 8.3 %collective-permute-start.11 = (bf16[256,256]{1,0:T(8,128)(2,1)S(1)}, bf16[256,256]{1,0:T(8,128)(2,1)S(1)}, u32[]{:S(2)}, u32[]{:S(2)}) collective-permute-start(bf16[256,256]{1,0:T(8,128)(2,1)S(1)} %get-tuple-element.155), channel_id=1, source_target_pairs={{0,12},{4,8},{8,4},{12,0},{1,13},{5,9},{9,5},{13,1},{2,14},{6,10},... | collective-permute-start | bytes 393224 | tf_op jit(solution)/shard_map/ppermute | solution.py:336
  30.1 10.1 %collective-permute-start.12 = (bf16[256,256]{1,0:T(8,128)(2,1)S(1)}, bf16[256,256]{1,0:T(8,128)(2,1)S(1)}, u32[]{:S(2)}, u32[]{:S(2)}) collective-permute-start(bf16[256,256]{1,0:T(8,128)(2,1)S(1)} %get-tuple-element.156), channel_id=1, source_target_pairs={{0,8},{4,12},{8,0},{12,4},{1,9},{5,13},{9,1},{13,5},{2,10},{6,14},... | collective-permute-start | bytes 393224 | tf_op jit(solution)/shard_map/ppermute | solution.py:336
  30.1 10.1 %collective-permute-start.13 = (bf16[256,256]{1,0:T(8,128)(2,1)S(1)}, bf16[256,256]{1,0:T(8,128)(2,1)S(1)}, u32[]{:S(2)}, u32[]{:S(2)}) collective-permute-start(bf16[256,256]{1,0:T(8,128)(2,1)S(1)} %get-tuple-element.157), channel_id=1, source_target_pairs={{0,4},{4,0},{8,12},{12,8},{1,5},{5,1},{9,13},{13,9},{2,6},{6,2},{1... | collective-permute-start | bytes 393224 | tf_op jit(solution)/shard_map/ppermute | solution.py:336
  40.8 6.9 %collective-permute-start.15 = (bf16[256,256]{1,0:T(8,128)(2,1)S(1)}, bf16[256,256]{1,0:T(8,128)(2,1)S(1)}, u32[]{:S(2)}, u32[]{:S(2)}) collective-permute-start(bf16[256,256]{1,0:T(8,128)(2,1)S(1)} %get-tuple-element.160.refs_4_.refs_1_), channel_id=1, source_target_pairs={{0,8},{4,12},{8,0},{12,4},{1,9},{5,13},{9,1},{13,5},{2,10},{6,14},... | collective-permute-start | bytes 393224 | tf_op jit(solution)/shard_map/ppermute | solution.py:336
  40.9 7.9 %collective-permute-start.17 = (bf16[256,256]{1,0:T(8,128)(2,1)S(1)}, bf16[256,256]{1,0:T(8,128)(2,1)S(1)}, u32[]{:S(2)}, u32[]{:S(2)}) collective-permute-start(bf16[256,256]{1,0:T(8,128)(2,1)S(1)} %get-tuple-element.160.refs_4_.refs_1_), channel_id=1, source_target_pairs={{0,4},{4,0},{8,12},{12,8},{1,5},{5,1},{9,13},{13,9},{2,6},{6,2},{1... | collective-permute-start | bytes 393224 | tf_op jit(solution)/shard_map/ppermute | solution.py:336
  47.7 5.0 %collective-permute-start.16 = (bf16[256,256]{1,0:T(8,128)(2,1)S(1)}, bf16[256,256]{1,0:T(8,128)(2,1)S(1)}, u32[]{:S(2)}, u32[]{:S(2)}) collective-permute-start(bf16[256,256]{1,0:T(8,128)(2,1)S(1)} %collective-permute-done.15.refs_3_), channel_id=1, source_target_pairs={{0,4},{4,0},{8,12},{12,8},{1,5},{5,1},{9,13},{13,9},{2,6},{6,2},{1... | collective-permute-start | bytes 393224 | tf_op jit(solution)/shard_map/ppermute | solution.py:336
  48.7 23.2 %collective-permute-start.14 = (bf16[2304,256]{1,0:T(8,128)(2,1)S(1)}, bf16[2304,256]{1,0:T(8,128)(2,1)S(1)}, u32[]{:S(2)}, u32[]{:S(2)}) collective-permute-start(bf16[2304,256]{1,0:T(8,128)(2,1)S(1)} %turn0.1.refs_7_.refs_1_.refs_8_), channel_id=1, source_target_pairs={{0,16},{16,0},{1,17},{17,1},{2,18},{18,2},{3,19},{19,3},{4,20},{20... | collective-permute-start | bytes 3538952 | tf_op jit(solution)/shard_map/ppermute | solution.py:279
  55.2 7.7 %collective-permute-start.18 = (f32[64,128]{1,0:T(8,128)S(1)}, f32[64,128]{1,0:T(8,128)S(1)}, u32[]{:S(2)}, u32[]{:S(2)}) collective-permute-start(f32[64,128]{1,0:T(8,128)S(1)} %get-tuple-element.164.refs_6_), channel_id=1, source_target_pairs={{0,3},{1,2},{2,1},{3,0},{4,7},{5,6},{6,5},{7,4},{8,11},{9,10},{10,... | collective-permute-start | bytes 98312 | tf_op jit(solution)/shard_map/ppermute | solution.py:336
  58.0 4.8 %collective-permute-start.19 = (f32[64,128]{1,0:T(8,128)S(1)}, f32[64,128]{1,0:T(8,128)S(1)}, u32[]{:S(2)}, u32[]{:S(2)}) collective-permute-start(f32[64,128]{1,0:T(8,128)S(1)} %get-tuple-element.164.refs_6_), channel_id=1, source_target_pairs={{0,2},{1,3},{2,0},{3,1},{4,6},{5,7},{6,4},{7,5},{8,10},{9,11},{10,... | collective-permute-start | bytes 98312 | tf_op jit(solution)/shard_map/ppermute | solution.py:336
  58.2 7.0 %collective-permute-start.20 = (f32[64,128]{1,0:T(8,128)S(1)}, f32[64,128]{1,0:T(8,128)S(1)}, u32[]{:S(2)}, u32[]{:S(2)}) collective-permute-start(f32[64,128]{1,0:T(8,128)S(1)} %get-tuple-element.164.refs_6_), channel_id=1, source_target_pairs={{0,1},{1,0},{2,3},{3,2},{4,5},{5,4},{6,7},{7,6},{8,9},{9,8},{10,11... | collective-permute-start | bytes 98312 | tf_op jit(solution)/shard_map/ppermute | solution.py:336
  60.7 8.8 %collective-permute-start.24 = (bf16[256,128]{1,0:T(8,128)(2,1)S(1)}, bf16[256,128]{1,0:T(8,128)(2,1)S(1)}, u32[]{:S(2)}, u32[]{:S(2)}) collective-permute-start(bf16[256,128]{1,0:T(8,128)(2,1)S(1)} %get-tuple-element.172), channel_id=1, source_target_pairs={{0,12},{4,8},{8,4},{12,0},{1,13},{5,9},{9,5},{13,1},{2,14},{6,10},... | collective-permute-start | bytes 196616 | tf_op jit(solution)/shard_map/ppermute | solution.py:336
  62.9 7.6 %collective-permute-start.25 = (bf16[256,128]{1,0:T(8,128)(2,1)S(1)}, bf16[256,128]{1,0:T(8,128)(2,1)S(1)}, u32[]{:S(2)}, u32[]{:S(2)}) collective-permute-start(bf16[256,128]{1,0:T(8,128)(2,1)S(1)} %get-tuple-element.173), channel_id=1, source_target_pairs={{0,8},{4,12},{8,0},{12,4},{1,9},{5,13},{9,1},{13,5},{2,10},{6,14},... | collective-permute-start | bytes 196616 | tf_op jit(solution)/shard_map/ppermute | solution.py:336
  62.9 9.0 %collective-permute-start.26 = (bf16[256,128]{1,0:T(8,128)(2,1)S(1)}, bf16[256,128]{1,0:T(8,128)(2,1)S(1)}, u32[]{:S(2)}, u32[]{:S(2)}) collective-permute-start(bf16[256,128]{1,0:T(8,128)(2,1)S(1)} %get-tuple-element.174), channel_id=1, source_target_pairs={{0,4},{4,0},{8,12},{12,8},{1,5},{5,1},{9,13},{13,9},{2,6},{6,2},{1... | collective-permute-start | bytes 196616 | tf_op jit(solution)/shard_map/ppermute | solution.py:336
  67.4 8.9 %collective-permute-start.21 = (bf16[256,128]{1,0:T(8,128)(2,1)S(1)}, bf16[256,128]{1,0:T(8,128)(2,1)S(1)}, u32[]{:S(2)}, u32[]{:S(2)}) collective-permute-start(bf16[256,128]{1,0:T(8,128)(2,1)S(1)} %get-tuple-element.169.refs_1_.refs_6_), channel_id=1, source_target_pairs={{0,12},{4,8},{8,4},{12,0},{1,13},{5,9},{9,5},{13,1},{2,14},{6,10},... | collective-permute-start | bytes 196616 | tf_op jit(solution)/shard_map/ppermute | solution.py:336
  69.6 7.5 %collective-permute-start.22 = (bf16[256,128]{1,0:T(8,128)(2,1)S(1)}, bf16[256,128]{1,0:T(8,128)(2,1)S(1)}, u32[]{:S(2)}, u32[]{:S(2)}) collective-permute-start(bf16[256,128]{1,0:T(8,128)(2,1)S(1)} %get-tuple-element.169.refs_1_.refs_6_), channel_id=1, source_target_pairs={{0,8},{4,12},{8,0},{12,4},{1,9},{5,13},{9,1},{13,5},{2,10},{6,14},... | collective-permute-start | bytes 196616 | tf_op jit(solution)/shard_map/ppermute | solution.py:336
  70.5 6.5 %collective-permute-start.23 = (bf16[256,128]{1,0:T(8,128)(2,1)S(1)}, bf16[256,128]{1,0:T(8,128)(2,1)S(1)}, u32[]{:S(2)}, u32[]{:S(2)}) collective-permute-start(bf16[256,128]{1,0:T(8,128)(2,1)S(1)} %get-tuple-element.169.refs_1_.refs_6_), channel_id=1, source_target_pairs={{0,4},{4,0},{8,12},{12,8},{1,5},{5,1},{9,13},{13,9},{2,6},{6,2},{1... | collective-permute-start | bytes 196616 | tf_op jit(solution)/shard_map/ppermute | solution.py:336
  73.5 5.0 %collective-permute-start.27 = (f32[64,128]{1,0:T(8,128)S(1)}, f32[64,128]{1,0:T(8,128)S(1)}, u32[]{:S(2)}, u32[]{:S(2)}) collective-permute-start(f32[64,128]{1,0:T(8,128)S(1)} %get-tuple-element.177), channel_id=1, source_target_pairs={{0,3},{1,2},{2,1},{3,0},{4,7},{5,6},{6,5},{7,4},{8,11},{9,10},{10,... | collective-permute-start | bytes 98312 | tf_op jit(solution)/shard_map/ppermute | solution.py:336
  76.2 3.9 %collective-permute-start.28 = (f32[64,128]{1,0:T(8,128)S(1)}, f32[64,128]{1,0:T(8,128)S(1)}, u32[]{:S(2)}, u32[]{:S(2)}) collective-permute-start(f32[64,128]{1,0:T(8,128)S(1)} %get-tuple-element.177), channel_id=1, source_target_pairs={{0,2},{1,3},{2,0},{3,1},{4,6},{5,7},{6,4},{7,5},{8,10},{9,11},{10,... | collective-permute-start | bytes 98312 | tf_op jit(solution)/shard_map/ppermute | solution.py:336
  76.3 3.9 %collective-permute-start.29 = (f32[64,128]{1,0:T(8,128)S(1)}, f32[64,128]{1,0:T(8,128)S(1)}, u32[]{:S(2)}, u32[]{:S(2)}) collective-permute-start(f32[64,128]{1,0:T(8,128)S(1)} %get-tuple-element.177), channel_id=1, source_target_pairs={{0,1},{1,0},{2,3},{3,2},{4,5},{5,4},{6,7},{7,6},{8,9},{9,8},{10,11... | collective-permute-start | bytes 98312 | tf_op jit(solution)/shard_map/ppermute | solution.py:336
  84.4 10.5 %collective-permute-start.30 = (bf16[272,256]{1,0:T(8,128)(2,1)S(1)}, bf16[272,256]{1,0:T(8,128)(2,1)S(1)}, u32[]{:S(2)}, u32[]{:S(2)}) collective-permute-start(bf16[272,256]{1,0:T(8,128)(2,1)S(1)} %get-tuple-element.181), channel_id=1, source_target_pairs={{0,12},{4,8},{8,4},{12,0},{1,13},{5,9},{9,5},{13,1},{2,14},{6,10},... | collective-permute-start | bytes 417800 | tf_op jit(solution)/shard_map/ppermute | solution.py:336
  86.5 8.4 %collective-permute-start.31 = (bf16[272,256]{1,0:T(8,128)(2,1)S(1)}, bf16[272,256]{1,0:T(8,128)(2,1)S(1)}, u32[]{:S(2)}, u32[]{:S(2)}) collective-permute-start(bf16[272,256]{1,0:T(8,128)(2,1)S(1)} %get-tuple-element.182), channel_id=1, source_target_pairs={{0,8},{4,12},{8,0},{12,4},{1,9},{5,13},{9,1},{13,5},{2,10},{6,14},... | collective-permute-start | bytes 417800 | tf_op jit(solution)/shard_map/ppermute | solution.py:336
  86.7 8.3 %collective-permute-start.32 = (bf16[272,256]{1,0:T(8,128)(2,1)S(1)}, bf16[272,256]{1,0:T(8,128)(2,1)S(1)}, u32[]{:S(2)}, u32[]{:S(2)}) collective-permute-start(bf16[272,256]{1,0:T(8,128)(2,1)S(1)} %get-tuple-element.183), channel_id=1, source_target_pairs={{0,4},{4,0},{8,12},{12,8},{1,5},{5,1},{9,13},{13,9},{2,6},{6,2},{1... | collective-permute-start | bytes 417800 | tf_op jit(solution)/shard_map/ppermute | solution.py:336
  89.8 11.0 %collective-permute-start.36 = (bf16[2304,256]{1,0:T(8,128)(2,1)S(1)}, bf16[2304,256]{1,0:T(8,128)(2,1)S(1)}, u32[]{:S(2)}, u32[]{:S(2)}) collective-permute-start(bf16[2304,256]{1,0:T(8,128)(2,1)S(1)} %turn1.1.refs_4_.refs_7_.refs_1_), channel_id=1, source_target_pairs={{0,16},{16,0},{1,17},{17,1},{2,18},{18,2},{3,19},{19,3},{4,20},{20... | collective-permute-start | bytes 3538952 | tf_op jit(solution)/shard_map/ppermute | solution.py:279
  90.6 10.2 %collective-permute-start.37 = (bf16[256,1280]{1,0:T(8,128)(2,1)S(1)}, bf16[256,1280]{1,0:T(8,128)(2,1)S(1)}, u32[]{:S(2)}, u32[]{:S(2)}) collective-permute-start(bf16[256,1280]{1,0:T(8,128)(2,1)S(1)} %get-tuple-element.194), channel_id=1, source_target_pairs={{0,16},{16,0},{1,17},{17,1},{2,18},{18,2},{3,19},{19,3},{4,20},{20... | collective-permute-start | bytes 1966088 | tf_op jit(solution)/shard_map/ppermute | solution.py:279
  96.3 9.6 %collective-permute-start.33 = (bf16[256,256]{1,0:T(8,128)(2,1)S(1)}, bf16[256,256]{1,0:T(8,128)(2,1)S(1)}, u32[]{:S(2)}, u32[]{:S(2)}) collective-permute-start(bf16[256,256]{1,0:T(8,128)(2,1)S(1)} %get-tuple-element.192.refs_5_.refs_1_), channel_id=1, source_target_pairs={{0,12},{4,8},{8,4},{12,0},{1,13},{5,9},{9,5},{13,1},{2,14},{6,10},... | collective-permute-start | bytes 393224 | tf_op jit(solution)/shard_map/ppermute | solution.py:336
  98.4 11.3 %collective-permute-start.34 = (bf16[256,256]{1,0:T(8,128)(2,1)S(1)}, bf16[256,256]{1,0:T(8,128)(2,1)S(1)}, u32[]{:S(2)}, u32[]{:S(2)}) collective-permute-start(bf16[256,256]{1,0:T(8,128)(2,1)S(1)} %get-tuple-element.192.refs_5_.refs_1_), channel_id=1, source_target_pairs={{0,8},{4,12},{8,0},{12,4},{1,9},{5,13},{9,1},{13,5},{2,10},{6,14},... | collective-permute-start | bytes 393224 | tf_op jit(solution)/shard_map/ppermute | solution.py:336
  98.4 11.3 %collective-permute-start.35 = (bf16[256,256]{1,0:T(8,128)(2,1)S(1)}, bf16[256,256]{1,0:T(8,128)(2,1)S(1)}, u32[]{:S(2)}, u32[]{:S(2)}) collective-permute-start(bf16[256,256]{1,0:T(8,128)(2,1)S(1)} %get-tuple-element.192.refs_5_.refs_1_), channel_id=1, source_target_pairs={{0,4},{4,0},{8,12},{12,8},{1,5},{5,1},{9,13},{13,9},{2,6},{6,2},{1... | collective-permute-start | bytes 393224 | tf_op jit(solution)/shard_map/ppermute | solution.py:336
  104.0 13.3 %collective-permute-start.42 = (bf16[2,1024,128]{2,1,0:T(8,128)(2,1)S(1)}, bf16[2,1024,128]{2,1,0:T(8,128)(2,1)S(1)}, u32[]{:S(2)}, u32[]{:S(2)}) collective-permute-start(bf16[2,1024,128]{2,1,0:T(8,128)(2,1)S(1)} %get-tuple-element.206), channel_id=1, source_target_pairs={{0,1},{1,0},{2,3},{3,2},{4,5},{5,4},{6,7},{7,6},{8,9},{9,8},{10,11... | collective-permute-start | bytes 1572872 | tf_op jit(solution)/shard_map/ppermute | solution.py:336
  104.6 12.6 %collective-permute-start.43 = (bf16[2,912,128]{2,1,0:T(8,128)(2,1)S(1)}, bf16[2,912,128]{2,1,0:T(8,128)(2,1)S(1)}, u32[]{:S(2)}, u32[]{:S(2)}) collective-permute-start(bf16[2,912,128]{2,1,0:T(8,128)(2,1)S(1)} %get-tuple-element.208), channel_id=1, source_target_pairs={{0,2},{1,3},{2,0},{3,1},{4,6},{5,7},{6,4},{7,5},{8,10},{9,11},{10,... | collective-permute-start | bytes 1400840 | tf_op jit(solution)/shard_map/ppermute | solution.py:336
  112.1 7.8 %collective-permute-start.39 = (bf16[256,128]{1,0:T(8,128)(2,1)S(1)}, bf16[256,128]{1,0:T(8,128)(2,1)S(1)}, u32[]{:S(2)}, u32[]{:S(2)}) collective-permute-start(bf16[256,128]{1,0:T(8,128)(2,1)S(1)} %get-tuple-element.203), channel_id=1, source_target_pairs={{0,12},{4,8},{8,4},{12,0},{1,13},{5,9},{9,5},{13,1},{2,14},{6,10},... | collective-permute-start | bytes 196616 | tf_op jit(solution)/shard_map/ppermute | solution.py:336
  114.2 6.4 %collective-permute-start.40 = (bf16[256,128]{1,0:T(8,128)(2,1)S(1)}, bf16[256,128]{1,0:T(8,128)(2,1)S(1)}, u32[]{:S(2)}, u32[]{:S(2)}) collective-permute-start(bf16[256,128]{1,0:T(8,128)(2,1)S(1)} %get-tuple-element.204), channel_id=1, source_target_pairs={{0,8},{4,12},{8,0},{12,4},{1,9},{5,13},{9,1},{13,5},{2,10},{6,14},... | collective-permute-start | bytes 196616 | tf_op jit(solution)/shard_map/ppermute | solution.py:336
  114.2 6.4 %collective-permute-start.41 = (bf16[256,128]{1,0:T(8,128)(2,1)S(1)}, bf16[256,128]{1,0:T(8,128)(2,1)S(1)}, u32[]{:S(2)}, u32[]{:S(2)}) collective-permute-start(bf16[256,128]{1,0:T(8,128)(2,1)S(1)} %get-tuple-element.205), channel_id=1, source_target_pairs={{0,4},{4,0},{8,12},{12,8},{1,5},{5,1},{9,13},{13,9},{2,6},{6,2},{1... | collective-permute-start | bytes 196616 | tf_op jit(solution)/shard_map/ppermute | solution.py:336
  117.2 7.7 %collective-permute-start.38 = (bf16[256,1280]{1,0:T(8,128)(2,1)S(1)}, bf16[256,1280]{1,0:T(8,128)(2,1)S(1)}, u32[]{:S(2)}, u32[]{:S(2)}) collective-permute-start(bf16[256,1280]{1,0:T(8,128)(2,1)S(1)} %get-tuple-element.201), channel_id=1, source_target_pairs={{0,16},{16,0},{1,17},{17,1},{2,18},{18,2},{3,19},{19,3},{4,20},{20... | collective-permute-start | bytes 1966088 | tf_op jit(solution)/shard_map/ppermute | solution.py:279
  118.1 12.7 %collective-permute-start.49 = (bf16[1,1024,128]{2,1,0:T(8,128)(2,1)S(1)}, bf16[1,1024,128]{2,1,0:T(8,128)(2,1)S(1)}, u32[]{:S(2)}, u32[]{:S(2)}) collective-permute-start(bf16[1,1024,128]{2,1,0:T(8,128)(2,1)S(1)} %get-tuple-element.217), channel_id=1, source_target_pairs={{0,2},{1,3},{2,0},{3,1},{4,6},{5,7},{6,4},{7,5},{8,10},{9,11},{10,... | collective-permute-start | bytes 786440 | tf_op jit(solution)/shard_map/ppermute | solution.py:336
  119.9 11.0 %collective-permute-start.50 = (bf16[1,912,128]{2,1,0:T(8,128)(2,1)S(1)}, bf16[1,912,128]{2,1,0:T(8,128)(2,1)S(1)}, u32[]{:S(2)}, u32[]{:S(2)}) collective-permute-start(bf16[1,912,128]{2,1,0:T(8,128)(2,1)S(1)} %get-tuple-element.218), channel_id=1, source_target_pairs={{0,1},{1,0},{2,3},{3,2},{4,5},{5,4},{6,7},{7,6},{8,9},{9,8},{10,11... | collective-permute-start | bytes 700424 | tf_op jit(solution)/shard_map/ppermute | solution.py:336
  122.2 6.3 %collective-permute-start.46 = (f32[64,128]{1,0:T(8,128)S(1)}, f32[64,128]{1,0:T(8,128)S(1)}, u32[]{:S(2)}, u32[]{:S(2)}) collective-permute-start(f32[64,128]{1,0:T(8,128)S(1)} %get-tuple-element.210.refs_5_), channel_id=1, source_target_pairs={{0,3},{1,2},{2,1},{3,0},{4,7},{5,6},{6,5},{7,4},{8,11},{9,10},{10,... | collective-permute-start | bytes 98312 | tf_op jit(solution)/shard_map/ppermute | solution.py:336
  123.5 5.1 %collective-permute-start.47 = (f32[64,128]{1,0:T(8,128)S(1)}, f32[64,128]{1,0:T(8,128)S(1)}, u32[]{:S(2)}, u32[]{:S(2)}) collective-permute-start(f32[64,128]{1,0:T(8,128)S(1)} %get-tuple-element.210.refs_5_), channel_id=1, source_target_pairs={{0,2},{1,3},{2,0},{3,1},{4,6},{5,7},{6,4},{7,5},{8,10},{9,11},{10,... | collective-permute-start | bytes 98312 | tf_op jit(solution)/shard_map/ppermute | solution.py:336
  124.9 4.3 %collective-permute-start.48 = (f32[64,128]{1,0:T(8,128)S(1)}, f32[64,128]{1,0:T(8,128)S(1)}, u32[]{:S(2)}, u32[]{:S(2)}) collective-permute-start(f32[64,128]{1,0:T(8,128)S(1)} %get-tuple-element.210.refs_5_), channel_id=1, source_target_pairs={{0,1},{1,0},{2,3},{3,2},{4,5},{5,4},{6,7},{7,6},{8,9},{9,8},{10,11... | collective-permute-start | bytes 98312 | tf_op jit(solution)/shard_map/ppermute | solution.py:336
  128.5 9.9 %collective-permute-start.51 = (bf16[2,256,256]{2,1,0:T(8,128)(2,1)S(1)}, bf16[2,256,256]{2,1,0:T(8,128)(2,1)S(1)}, u32[]{:S(2)}, u32[]{:S(2)}) collective-permute-start(bf16[2,256,256]{2,1,0:T(8,128)(2,1)S(1)} %get-tuple-element.223), channel_id=1, source_target_pairs={{0,4},{4,0},{8,12},{12,8},{1,5},{5,1},{9,13},{13,9},{2,6},{6,2},{1... | collective-permute-start | bytes 786440 | tf_op jit(solution)/shard_map/ppermute | solution.py:336
  128.5 12.9 %collective-permute-start.44 = (bf16[2,1024,128]{2,1,0:T(8,128)(2,1)S(1)}, bf16[2,1024,128]{2,1,0:T(8,128)(2,1)S(1)}, u32[]{:S(2)}, u32[]{:S(2)}) collective-permute-start(bf16[2,1024,128]{2,1,0:T(8,128)(2,1)S(1)} %get-tuple-element.212), channel_id=1, source_target_pairs={{0,1},{1,0},{2,3},{3,2},{4,5},{5,4},{6,7},{7,6},{8,9},{9,8},{10,11... | collective-permute-start | bytes 1572872 | tf_op jit(solution)/shard_map/ppermute | solution.py:336
  129.2 11.9 %collective-permute-start.45 = (bf16[2,912,128]{2,1,0:T(8,128)(2,1)S(1)}, bf16[2,912,128]{2,1,0:T(8,128)(2,1)S(1)}, u32[]{:S(2)}, u32[]{:S(2)}) collective-permute-start(bf16[2,912,128]{2,1,0:T(8,128)(2,1)S(1)} %get-tuple-element.214), channel_id=1, source_target_pairs={{0,2},{1,3},{2,0},{3,1},{4,6},{5,7},{6,4},{7,5},{8,10},{9,11},{10,... | collective-permute-start | bytes 1400840 | tf_op jit(solution)/shard_map/ppermute | solution.py:336
  135.1 14.6 %collective-permute-start.55 = (bf16[272,256]{1,0:T(8,128)(2,1)S(1)}, bf16[272,256]{1,0:T(8,128)(2,1)S(1)}, u32[]{:S(2)}, u32[]{:S(2)}) collective-permute-start(bf16[272,256]{1,0:T(8,128)(2,1)S(1)} %get-tuple-element.233), channel_id=1, source_target_pairs={{0,12},{4,8},{8,4},{12,0},{1,13},{5,9},{9,5},{13,1},{2,14},{6,10},... | collective-permute-start | bytes 417800 | tf_op jit(solution)/shard_map/ppermute | solution.py:336
  137.2 12.6 %collective-permute-start.56 = (bf16[272,256]{1,0:T(8,128)(2,1)S(1)}, bf16[272,256]{1,0:T(8,128)(2,1)S(1)}, u32[]{:S(2)}, u32[]{:S(2)}) collective-permute-start(bf16[272,256]{1,0:T(8,128)(2,1)S(1)} %get-tuple-element.234), channel_id=1, source_target_pairs={{0,8},{4,12},{8,0},{12,4},{1,9},{5,13},{9,1},{13,5},{2,10},{6,14},... | collective-permute-start | bytes 417800 | tf_op jit(solution)/shard_map/ppermute | solution.py:336
  138.4 11.4 %collective-permute-start.57 = (bf16[272,256]{1,0:T(8,128)(2,1)S(1)}, bf16[272,256]{1,0:T(8,128)(2,1)S(1)}, u32[]{:S(2)}, u32[]{:S(2)}) collective-permute-start(bf16[272,256]{1,0:T(8,128)(2,1)S(1)} %get-tuple-element.235), channel_id=1, source_target_pairs={{0,4},{4,0},{8,12},{12,8},{1,5},{5,1},{9,13},{13,9},{2,6},{6,2},{1... | collective-permute-start | bytes 417800 | tf_op jit(solution)/shard_map/ppermute | solution.py:336
  142.3 7.8 %collective-permute-start.52 = (bf16[1,1024,128]{2,1,0:T(8,128)(2,1)S(1)}, bf16[1,1024,128]{2,1,0:T(8,128)(2,1)S(1)}, u32[]{:S(2)}, u32[]{:S(2)}) collective-permute-start(bf16[1,1024,128]{2,1,0:T(8,128)(2,1)S(1)} %get-tuple-element.225), channel_id=1, source_target_pairs={{0,2},{1,3},{2,0},{3,1},{4,6},{5,7},{6,4},{7,5},{8,10},{9,11},{10,... | collective-permute-start | bytes 786440 | tf_op jit(solution)/shard_map/ppermute | solution.py:336
  144.0 6.1 %collective-permute-start.53 = (bf16[1,912,128]{2,1,0:T(8,128)(2,1)S(1)}, bf16[1,912,128]{2,1,0:T(8,128)(2,1)S(1)}, u32[]{:S(2)}, u32[]{:S(2)}) collective-permute-start(bf16[1,912,128]{2,1,0:T(8,128)(2,1)S(1)} %get-tuple-element.227), channel_id=1, source_target_pairs={{0,1},{1,0},{2,3},{3,2},{4,5},{5,4},{6,7},{7,6},{8,9},{9,8},{10,11... | collective-permute-start | bytes 700424 | tf_op jit(solution)/shard_map/ppermute | solution.py:336
  149.7 3.9 %collective-permute-start.54 = (f32[640,256]{1,0:T(8,128)S(1)}, f32[640,256]{1,0:T(8,128)S(1)}, u32[]{:S(2)}, u32[]{:S(2)}) collective-permute-start(f32[640,256]{1,0:T(8,128)S(1)} %get-tuple-element.232), channel_id=1, source_target_pairs={{0,16},{16,0},{1,17},{17,1},{2,18},{18,2},{3,19},{19,3},{4,20},{20... | collective-permute-start | bytes 1966088 | tf_op jit(solution)/shard_map/ppermute | solution.py:279
  151.3 2.2 %collective-permute-start.58 = (bf16[272,256]{1,0:T(8,128)(2,1)S(1)}, bf16[272,256]{1,0:T(8,128)(2,1)S(1)}, u32[]{:S(2)}, u32[]{:S(2)}) collective-permute-start(bf16[272,256]{1,0:T(8,128)(2,1)S(1)} %get-tuple-element.240), channel_id=1, source_target_pairs={{0,16},{16,0},{1,17},{17,1},{2,18},{18,2},{3,19},{19,3},{4,20},{20... | collective-permute-start | bytes 417800 | tf_op jit(solution)/shard_map/ppermute | solution.py:279
  151.6 9.4 %collective-permute-start.63 = (bf16[1,256,256]{2,1,0:T(8,128)(2,1)S(1)}, bf16[1,256,256]{2,1,0:T(8,128)(2,1)S(1)}, u32[]{:S(2)}, u32[]{:S(2)}) collective-permute-start(bf16[1,256,256]{2,1,0:T(8,128)(2,1)S(1)} %get-tuple-element.250), channel_id=1, source_target_pairs={{0,8},{4,12},{8,0},{12,4},{1,9},{5,13},{9,1},{13,5},{2,10},{6,14},... | collective-permute-start | bytes 393224 | tf_op jit(solution)/shard_map/ppermute | solution.py:336
  154.3 9.1 %collective-permute-start.60 = (bf16[464,128]{1,0:T(8,128)(2,1)S(1)}, bf16[464,128]{1,0:T(8,128)(2,1)S(1)}, u32[]{:S(2)}, u32[]{:S(2)}) collective-permute-start(bf16[464,128]{1,0:T(8,128)(2,1)S(1)} %get-tuple-element.244), channel_id=1, source_target_pairs={{0,3},{1,2},{2,1},{3,0},{4,7},{5,6},{6,5},{7,4},{8,11},{9,10},{10,... | collective-permute-start | bytes 356360 | tf_op jit(solution)/shard_map/ppermute | solution.py:336
  155.2 8.1 %collective-permute-start.61 = (bf16[464,128]{1,0:T(8,128)(2,1)S(1)}, bf16[464,128]{1,0:T(8,128)(2,1)S(1)}, u32[]{:S(2)}, u32[]{:S(2)}) collective-permute-start(bf16[464,128]{1,0:T(8,128)(2,1)S(1)} %get-tuple-element.245), channel_id=1, source_target_pairs={{0,2},{1,3},{2,0},{3,1},{4,6},{5,7},{6,4},{7,5},{8,10},{9,11},{10,... | collective-permute-start | bytes 356360 | tf_op jit(solution)/shard_map/ppermute | solution.py:336
  157.1 6.2 %collective-permute-start.62 = (bf16[464,128]{1,0:T(8,128)(2,1)S(1)}, bf16[464,128]{1,0:T(8,128)(2,1)S(1)}, u32[]{:S(2)}, u32[]{:S(2)}) collective-permute-start(bf16[464,128]{1,0:T(8,128)(2,1)S(1)} %get-tuple-element.246), channel_id=1, source_target_pairs={{0,1},{1,0},{2,3},{3,2},{4,5},{5,4},{6,7},{7,6},{8,9},{9,8},{10,11... | collective-permute-start | bytes 356360 | tf_op jit(solution)/shard_map/ppermute | solution.py:336
  162.8 2.2 %collective-permute-start.59 = (bf16[1936,128]{1,0:T(8,128)(2,1)S(1)}, bf16[1936,128]{1,0:T(8,128)(2,1)S(1)}, u32[]{:S(2)}, u32[]{:S(2)}) collective-permute-start(bf16[1936,128]{1,0:T(8,128)(2,1)S(1)} %get-tuple-element.243), channel_id=1, source_target_pairs={{0,16},{16,0},{1,17},{17,1},{2,18},{18,2},{3,19},{19,3},{4,20},{20... | collective-permute-start | bytes 1486856 | tf_op jit(solution)/shard_map/ppermute | solution.py:279
  (24 other events, 111.5 us)

commit v2 on v1

--- a/solution.py
+++ b/solution.py
@@ -236,7 +236,7 @@
 def crossing(meta, arrived, decay, length, direction):
     total = jnp.zeros_like(decay)
     for s, part in enumerate(arrived):
-        apart = direction * (meta[2] - jnp.bitwise_xor(meta[2], len(arrived) - s)) - 1
+        apart = direction * (meta[2] - jnp.bitwise_xor(meta[2], s + 1)) - 1
         first = -apart * length if direction == 1 else length
         open_way = jnp.logical_and(apart >= 0, jnp.logical_not(start_in(meta, first, apart * length)))
         reach = jnp.exp(decay * (-float(length)) * jnp.maximum(apart, 0).astype(F32))
@@ -343,8 +343,8 @@
         if forward and nt == 4:
             across = paired(part, "tensor", 2)
             beside = paired(part, "tensor", 1)
-            return (part, paired(across, "tensor", 1), across, beside)
-        return (part, *(paired(part, "tensor", nt - s) for s in range(1, nt)))
+            return (part, beside, across, paired(across, "tensor", 1))
+        return (part, *(paired(part, "tensor", s) for s in range(1, nt)))
 
     def paired_parts(meta, keep, give, part):
         for i in range(nt // 2):
@@ -354,32 +354,35 @@
     def paired_outs(width):
         return [((nt // 2, T, width), F32), ((nt // 2, T, width), BF16)]
 
-    def parts_join(layer, keep, arrived, after):
+    def parts_join(layer, keep, arrived, base, after):
         half, width = keep.shape[0] // 2, keep.shape[2]
 
         def body(k):
             for i in range(2 * half):
+                part = k.vin[0][i] + k.vin[1][i].astype(F32)
+                if base and i == 0:
+                    part = part + k.vin[2][...] + column_rows(k.vin[3], DOWN_B, k.meta[1])
                 out = k.outs[i % 2]
-                out[i // 2] = (k.vin[0][i] + k.vin[1][i].astype(F32)).astype(out.dtype)
+                out[i // 2] = part.astype(out.dtype)
 
         return kernels[layer](
             f"parts_join{layer}",
             body,
             [((half, T, width), F32), ((half, T, width), BF16)],
-            vin=(keep, arrived),
-            after=after,
-        )
-
-    def paired_sum(layer, keep, give, arrived, after):
+            vin=(keep, arrived, *base),
+            after=after,
+        )
+
+    def paired_sum(layer, keep, give, arrived, base, after):
         step = 2
         while step < nt:
-            keep, give = parts_join(layer, keep, arrived, after)
+            keep, give = parts_join(layer, keep, arrived, base if step == 2 else (), after)
             arrived = paired(give, "tensor", step)
             step *= 2
         return keep, arrived
 
     def line(value):
-        return tuple(paired(value, "dp", nd - 1 - s) for s in range(nd - 1))
+        return tuple(paired(value, "dp", s + 1) for s in range(nd - 1))
 
     def target(mine, s, n):
         return jnp.bitwise_xor(mine, (n - s) % n)
@@ -591,7 +594,7 @@
     def assemble(meta, parts, whole):
         width = parts[0].shape[1]
         for s in range(nt):
-            at = target(meta[1], s, nt) * width
+            at = jnp.bitwise_xor(meta[1], s) * width
             whole[:, pl.ds(pl.multiple_of(at, width), width)] = parts[s][...]
 
     def down_parts(meta, gated, down, sends):
@@ -676,22 +679,22 @@
                 copy.start()
                 copy.wait()
                 total = rows[...].astype(F32)
+                for part in k.vin[1:]:
+                    total = total + part[...].astype(F32)
+                total = total + column_rows(k.vin[0], DOWN_B, meta[1])
             else:
-                total = k.vin[-1][...] + k.vin[1][0] + k.vin[2][0].astype(F32)
-            for part in k.vin[1 : 1 + nt] if layer == 0 else ():
-                total = total + part[...].astype(F32)
-            total = total + column_rows(k.vin[0], DOWN_B, meta[1])
+                total = k.vin[1][0] + k.vin[2][0].astype(F32)
             if layer == 0:
                 k.outs[0][...] = total
                 k.outs[1][...] = total.astype(BF16)
             else:
-                keep_or_give(meta, k.outs[0], k.outs[1], k.vin[-1][...], total)
+                k.outs[0][...] = total
 
         return kernels[layer](
             f"layer_output{layer}",
             body,
-            [((T, DC), F32), ((T, DC), BF16 if layer == 0 else F32)],
-            vin=(pack, *parts) if layer == 0 else (pack, *parts, before),
+            [((T, DC), F32)] + ([((T, DC), BF16)] if layer == 0 else []),
+            vin=(pack, *parts),
             after=after,
             places=(before,) if layer == 0 else (),
             scratch=[pltpu.VMEM((T, DC), BF16), pltpu.SemaphoreType.DMA((1,))] if layer == 0 else [],
@@ -798,27 +801,40 @@
 
     LATE = D // 2 + 2 * N
 
-    def ssm_grads(layer, act, entering, d_scanned, incoming, turned, narrow_low, pack, upper, after):
+    def states_before(layer, act, entering, pack, after):
+        def body(k):
+            u, enter, pk = k.vin
+            a = jnp.exp(-tables(pk)[0])
+
+            def ahead(t0, state, masked):
+                for j, row in row_groups(u, t0, BLOCK):
+                    if masked:
+                        state = state * keep_at(k.meta, t0 + j)
+                    k.outs[0][t0 + j] = state
+                    state = a * state + row
+                return state
+
+            scan_blocks(k.meta, T, enter[...], ahead)
+
+        return kernels[layer](
+            f"states_before{layer}",
+            body,
+            [((T, N, HC), F32)],
+            vin=(act, entering, pack),
+            after=after,
+        )[0]
+
+    def ssm_grads(layer, act, states, d_scanned, incoming, turned, narrow_low, pack, upper, after):
         def body(k):
             meta = k.meta
-            u, enter, grads, incoming, low, pk = k.vin[:6]
-            states, lefts, sems = k.scratch[:3]
-            late = k.outs[0] if layer == 1 else k.scratch[3]
+            u, states, grads, incoming, low, pk = k.vin[:6]
+            lefts, sems = k.scratch[:2]
+            late = k.outs[0] if layer == 1 else k.scratch[2]
             copy = pltpu.make_async_copy(k.places[0].at[0:D, :], lefts, sems.at[0])
             copy.start()
             decay, grown, rate_in, read_out = tables(pk)
             a = jnp.exp(-decay)
             zero = jnp.zeros((N, HC), F32)
-
-            def ahead(t0, state, masked):
-                for j, row in row_groups(u, t0, BLOCK):
-                    if masked:
-                        state = state * keep_at(meta, t0 + j)
-                    states[t0 + j] = state
-                    state = a * state + row
-                return state
-
-            scan_blocks(meta, T, enter[...], ahead)
 
             def back(t0, carried, masked):
                 z, with_rows, with_states = carried
@@ -856,12 +872,11 @@
             f"ssm_grads{layer}",
             body,
             [((LATE, 2 * LANES), F32)] * (2 - layer),
-            vin=(act, entering, d_scanned, incoming, narrow_low, pack, *upper),
+            vin=(act, states, d_scanned, incoming, narrow_low, pack, *upper),
             places=(turned,),
             span=1 if layer else SPAN,
             after=after,
             scratch=[
-                pltpu.VMEM((T, N, HC), F32),
                 pltpu.VMEM((D, T), BF16),
                 pltpu.SemaphoreType.DMA((1,)),
             ]
@@ -1137,7 +1152,8 @@
     def own_columns(keep, grad, grad_other, after):
         def body(k):
             meta = k.meta
-            *outs, grads = k.outs
+            *outs, grads, token = k.outs
+            token[...] = jnp.zeros((8, LANES), F32)
             rows, sems = k.scratch
             rows[...] = k.vin[0][0:T, :].astype(F32)
             moves = [(k.places[1].at[0:T, :], grads.at[0, meta[0]]), (rows, grads.at[0, 1 - meta[0]])]
@@ -1162,7 +1178,13 @@
         return kernels[0](
             "own_columns",
             body,
-            [((1, RW, FW), F32), ((1, RL, FW), F32), ((1, RD, D), F32), ((1, 2, T, DC), F32)],
+            [
+                ((1, RW, FW), F32),
+                ((1, RL, FW), F32),
+                ((1, RD, D), F32),
+                ((1, 2, T, DC), F32),
+                ((8, LANES), F32),
+            ],
             vin=(grad_other,),
             places=(keep, grad),
             after=after,
@@ -1170,7 +1192,7 @@
             scratch=[pltpu.VMEM((T, DC), F32), pltpu.SemaphoreType.DMA((2 + 2 * CW + CD,))],
         )
 
-    def finish(own, big, small, output, output_other):
+    def finish(own, big, small, lower, upper):
         def body(k):
             meta = k.meta
             wide, lift, down, rows, turned, sems = k.scratch
@@ -1178,17 +1200,25 @@
             wide_b, lift_b, down_b = k.outs[3:6]
             by_narrow, narrow_b, *by_ssm, by_skip, gain, shift, outputs = k.outs[6:]
             keep, give, late = k.vin
+
+            def output(layer, i):
+                return pltpu.make_async_copy(
+                    k.places[3 + 2 * layer + i],
+                    outputs.at[0, meta[0] if i == 0 else 1 - meta[0]],
+                    sems.at[3 + i],
+                )
+
+            def send(layer):
+                for i in range(2):
+                    output(layer, i).start()
+
+            pl.when(meta[0] == 0)(partial(send, 0))
+            pl.when(meta[0] != 0)(partial(send, 1))
             moves = [
-                (k.places[3], outputs.at[0, meta[0]]),
-                (k.places[4], outputs.at[0, 1 - meta[0]]),
-                (k.places[5].at[0:RW, :], by_narrow.at[0]),
+                pltpu.make_async_copy(k.places[7].at[0:RW, :], by_narrow.at[0], sems.at[5])
             ]
-            moves = [
-                pltpu.make_async_copy(source, out, sems.at[3 + i])
-                for i, (source, out) in enumerate(moves)
-            ]
-            for move in moves:
-                move.start()
+            moves[0].start()
+            moves += [output(0, i) for i in range(2)]
             for q, (buffer, out, (first, height, columns)) in enumerate(
                 zip((wide, lift, down), (by_wide, by_lift, by_down), big_places())
             ):
@@ -1241,7 +1271,7 @@
                 ((1, 2, T, DC), F32),
             ],
             vin=(*big, small),
-            places=(*own, output, output_other, small),
+            places=(*own, *lower, *upper, small),
             direct=(0, 1, 2, 6, 14),
             onto=3,
             scratch=[
@@ -1272,7 +1302,7 @@
     hidden, hidden_low = layer_output(0, layer_input, parts, pack0, after=(d_gated1,))
     pieces = gather(hidden_low, forward=True)
     lefts0 = turn(0, (normed0, scanned_all0, gated0), after=(hidden_low,))
-    lefts0_other = swap(lefts0)
+    lefts0_other, hidden_other = swap(lefts0), swap(hidden)
 
     normed1, narrow_pre1, act1, final1, xhat1, rstd1 = front(
         1, pieces, pack1, narrow_w1, after=(lefts0,)
@@ -1282,10 +1312,11 @@
     parts = scatter(sends)
     enter1, scanned1 = carry(1, act1, arrived, pack1, after=(sends[0],))
     pieces = gather(scanned1)
-    d_scanned1, first1 = adjoint_local(1, parts, pack1, after=(scanned1, lefts0_other))
+    d_scanned1, first1 = adjoint_local(1, parts, pack1, after=(scanned1, lefts0_other, hidden_other))
     scanned_all1, gated1, wide_low1 = middle1(pieces, wide_pre1, d_gated1, pack1, lift_w1)
     arrived = line(first1)
-    incoming1, narrow_low1 = adjoint(1, d_scanned1, narrow_pre1, arrived, pack1, after=(wide_low1,))
+    states1 = states_before(1, act1, enter1, pack1, after=(wide_low1,))
+    incoming1, narrow_low1 = adjoint(1, d_scanned1, narrow_pre1, arrived, pack1, after=(states1,))
     sends = grad_normed(1, wide_low1, narrow_low1, xhat1, pack1, wide_w1, narrow_w1)
     parts = scatter(sends)
     lefts1 = turn(1, (normed1, scanned_all1, gated1), after=(sends[0],))
@@ -1294,7 +1325,7 @@
     (late1,) = ssm_grads(
         1,
         act1,
-        enter1,
+        states1,
         d_scanned1,
         incoming1,
         lefts1,
@@ -1335,13 +1366,16 @@
         0, wide_low0, narrow_low0, xhat0, pack0, wide_w0, narrow_w0
     )
     parts = scatter(sends)
+    states0 = states_before(0, act0, enter0, pack0, after=(sends[0],))
+    (sum1,) = big_sum(1, weights1, big1, (), after=(sends[0],))
+    top = paired_sum(1, top_keep, top_give, top_arrived, (hidden, pack1), (sends[0],))
     for step in range(1, STEPS):
-        weights0 = blocks_join(0, weights0, big0, (sends[0], top_arrived))
+        weights0 = blocks_join(0, weights0, big0, (sum1, top[0], states0))
         big0 = to_pairs(weights0, step)
     late, late_give = ssm_grads(
         0,
         act0,
-        enter0,
+        states0,
         d_scanned0,
         incoming0,
         lefts0,
@@ -1350,18 +1384,16 @@
         (late1,),
         after=(weights0[0],),
     )
-    (sum1,) = big_sum(1, weights1, big1, (), after=(late,))
-    top = paired_sum(1, top_keep, top_give, top_arrived, (late,))
     grad, grad_give = layer_grad(
-        0, parts, rstd0, xhat0, grad_mid, pack0, after=(late, sum1, top[0], *big0)
+        0, parts, rstd0, xhat0, grad_mid, pack0, after=(late, sum1, top[0])
     )
     grad_other = swap(grad_give)
     small_parts = late_join(late, swap(late_give), grad, grad_other, after=())
     small_parts_in = scatter(small_parts, "dp")
     keep, give = big_sum(0, weights0, big0, (sum1,), after=(small_parts[0],))
     big_other = swap(give)
-    *own, input_grad = own_columns(keep, grad, grad_other, after=())
-    output, output_give = layer_output(1, hidden, top, pack1, after=(own[0],))
+    *own, input_grad, token = own_columns(keep, grad, grad_other, after=())
+    (output,) = layer_output(1, None, top, pack1, after=(token,))
     (
         by_wide,
         by_lift,
@@ -1378,7 +1410,13 @@
         gain,
         shift,
         section_output,
-    ) = finish(own, (keep, big_other), late_sum(small_parts_in), output, swap(output_give))
+    ) = finish(
+        own,
+        (keep, big_other),
+        late_sum(small_parts_in),
+        (hidden, hidden_other),
+        (output, swap(output)),
+    )
     return (
         section_output,
         input_grad,

time: 168 us -> 165 us (0.982)
  waiting for transfers between devices: 30.6 us -> 28.2 us
    ppermute x52, waiting for transfers between devices: 29.5 us -> 27.7 us  [paired(): return lax.ppermute(part, axis, [(i, i ^ s) for i in range(n)])]
    pallas_call x42 -> x44, Pallas kernels: 65 us -> 66 us  [__call__(): pl.pallas_call(run, out_shape=[jax.ShapeDtypeStruct(s, d) for s, d in out...]
  transfers between devices with their start and end apart: 65 -> 66, of which waited for: 19 -> 20; matrix products, arithmetic and copies ran while one was open for 0% -> 0% of each run, Pallas kernels for 33% -> 33%
where the time goes in v2:
time: 165 us
  starting transfers between devices  68.7 us (42%)
  Pallas kernels  66 us (40%)
  waiting for transfers between devices  28.2 us (17%)
    pallas_call x44, Pallas kernels, __call__(): pl.pallas_call(run, out_shape=[jax.ShapeDtypeStruct(s, d) for s, d in out...  66 us
    ppermute x52, starting transfers between devices, paired(): return lax.ppermute(part, axis, [(i, i ^ s) for i in range(n)])  65.6 us
    ppermute x52, waiting for transfers between devices, paired(): return lax.ppermute(part, axis, [(i, i ^ s) for i in range(n)])  27.7 us
  transfers between devices with their start and end apart: 66, of which 20 were waited for; matrix products, arithmetic and copies ran while one was open for 0% of the time, Pallas kernels for 33%

profile of v2, /device:TPU:0, one launch (start us, length us, event | category | flops | bytes accessed | tf_op | source)
XLA Modules:
  0.0 164.7 jit_solution(1870321713046434002)
XLA Ops:
  0.7 2.4 %make_pack.1.refs_2_ = f32[64,640]{1,0:T(8,128)} custom-call(s32[2,3]{1,0:T(2,128)} %refs_0_.87, f32[64,128]{1,0:T(8,128)} %bitcast.25, f32[64,128]{1,0:T(8,128)} %bitcast.26, f32[64,128]{1,0:T(8,128)} %bitcast.27, f32[1,1024]{1,0:T(1,128)} %refs_4_.1, f32[1,1024]{1,0:T(1,128)} %refs_5_.1, f32[1,1024]{1,0:T(1,128)} %refs_6_.2, f32[1,768]{1,0:T(1,128)} %refs_7_.1, ...), custom_call_target="tpu_custom_call" | custom-call | flops 40000000000 | bytes 1 | tf_op jit(solution)/shard_map/make_pack/pallas_call | solution.py:108
  4.2 1.1 norm0.1
  5.3 2.0 %front0.1 = (bf16[256,1024]{1,0:T(8,128)(2,1)S(1)}, f32[256,128]{1,0:T(8,128)S(1)}, f32[256,128]{1,0:T(8,128)S(1)}, f32[64,128]{1,0:T(8,128)S(1)}, f32[64,640]{1...) custom-call(s32[2,3]{1,0:T(2,128)S(1)} %copy-done.8, ...), custom_call_target="tpu_custom_call" | custom-call | flops 40000000000 | bytes 1 | tf_op jit(solution)/shard_map/front0/pallas_call | solution.py:108
  7.4 3.5 %collective-permute-start.4 = (f32[64,128]{1,0:T(8,128)S(1)}, f32[64,128]{1,0:T(8,128)S(1)}, u32[]{:S(2)}, u32[]{:S(2)}) collective-permute-start(f32[64,128]{1,0:T(8,128)S(1)} %get-tuple-element.146), channel_id=1, source_target_pairs={{0,3},{1,2},{2,1},{3,0},{4,7},{5,6},{6,5},{7,4},{8,11},{9,10},{10,... | collective-permute-start | bytes 98312 | tf_op jit(solution)/shard_map/ppermute | solution.py:336
  12.1 1.3 wide0.1
  13.4 1.5 collective-permute-done.3.refs_4_
  15.3 2.2 %carry0.1 = (f32[64,128]{1,0:T(8,128)S(1)}, bf16[256,128]{1,0:T(8,128)(2,1)S(1)}) custom-call(s32[2,3]{1,0:T(2,128)S(1)} %copy-done.8, f32[256,128]{1,0:T(8,128)S(1)} %get-tuple-element.144.refs_1_, f32[64,640]{1,0:T(8,128)S(1)} %get-tuple-element.145.refs_2_.refs_6_.refs_1_.refs_3_.refs_4_, f32[64,128]{1,0:T(8,128)S(1)} %collective-permute-done.2.refs_3_, ...), custom_call_target="tpu_custom_call" | custom-call | flops 40000000000 | bytes 1 | tf_op jit(solution)/shard_map/carry0/pallas_call | solution.py:108
  17.5 3.7 %collective-permute-start.8 = (bf16[256,128]{1,0:T(8,128)(2,1)S(1)}, bf16[256,128]{1,0:T(8,128)(2,1)S(1)}, u32[]{:S(2)}, u32[]{:S(2)}) collective-permute-start(bf16[256,128]{1,0:T(8,128)(2,1)S(1)} %get-tuple-element.148.refs_5_.refs_1_), channel_id=1, source_target_pairs={{0,12},{4,8},{8,4},{12,0},{1,13},{5,9},{9,5},{13,1},{2,14},{6,10},... | collective-permute-start | bytes 196616 | tf_op jit(solution)/shard_map/ppermute | solution.py:336
  23.6 2.7 %collective-permute-done.7.refs_3_ = bf16[256,128]{1,0:T(8,128)(2,1)S(1)} collective-permute-done((bf16[256,128]{1,0:T(8,128)(2,1)S(1)}, bf16[256,128]{1,0:T(8,128)(2,1)S(1)}, u32[]{:S(2)}, u32[]{:S(2)}) %collective-permute-start.7) | collective-permute-done | bytes 65568 | tf_op jit(solution)/shard_map/ppermute | solution.py:336
  26.4 1.5 middle0.1
  27.9 2.2 %collective-permute-start.11 = (bf16[256,256]{1,0:T(8,128)(2,1)S(1)}, bf16[256,256]{1,0:T(8,128)(2,1)S(1)}, u32[]{:S(2)}, u32[]{:S(2)}) collective-permute-start(bf16[256,256]{1,0:T(8,128)(2,1)S(1)} %get-tuple-element.154), channel_id=1, source_target_pairs={{0,12},{4,8},{8,4},{12,0},{1,13},{5,9},{9,5},{13,1},{2,14},{6,10},... | collective-permute-start | bytes 393224 | tf_op jit(solution)/shard_map/ppermute | solution.py:336
  30.1 2.3 %collective-permute-start.13 = (bf16[256,256]{1,0:T(8,128)(2,1)S(1)}, bf16[256,256]{1,0:T(8,128)(2,1)S(1)}, u32[]{:S(2)}, u32[]{:S(2)}) collective-permute-start(bf16[256,256]{1,0:T(8,128)(2,1)S(1)} %get-tuple-element.156), channel_id=1, source_target_pairs={{0,4},{4,0},{8,12},{12,8},{1,5},{5,1},{9,13},{13,9},{2,6},{6,2},{1... | collective-permute-start | bytes 393224 | tf_op jit(solution)/shard_map/ppermute | solution.py:336
  33.6 1.2 grad_gated1.1
  34.8 1.4 collective-permute-done.11.refs_3_
  36.2 3.9 %collective-permute-done.12.refs_4_ = bf16[256,256]{1,0:T(8,128)(2,1)S(1)} collective-permute-done((bf16[256,256]{1,0:T(8,128)(2,1)S(1)}, bf16[256,256]{1,0:T(8,128)(2,1)S(1)}, u32[]{:S(2)}, u32[]{:S(2)}) %collective-permute-start.12) | collective-permute-done | bytes 131104 | tf_op jit(solution)/shard_map/ppermute | solution.py:336
  40.9 2.5 %collective-permute-start.15 = (bf16[256,256]{1,0:T(8,128)(2,1)S(1)}, bf16[256,256]{1,0:T(8,128)(2,1)S(1)}, u32[]{:S(2)}, u32[]{:S(2)}) collective-permute-start(bf16[256,256]{1,0:T(8,128)(2,1)S(1)} %get-tuple-element.159.refs_4_.refs_1_), channel_id=1, source_target_pairs={{0,4},{4,0},{8,12},{12,8},{1,5},{5,1},{9,13},{13,9},{2,6},{6,2},{1... | collective-permute-start | bytes 393224 | tf_op jit(solution)/shard_map/ppermute | solution.py:336
  43.4 4.4 %collective-permute-done.16.refs_3_ = bf16[256,256]{1,0:T(8,128)(2,1)S(1)} collective-permute-done((bf16[256,256]{1,0:T(8,128)(2,1)S(1)}, bf16[256,256]{1,0:T(8,128)(2,1)S(1)}, u32[]{:S(2)}, u32[]{:S(2)}) %collective-permute-start.16) | collective-permute-done | bytes 131104 | tf_op jit(solution)/shard_map/ppermute | solution.py:336
  49.3 3.4 %collective-permute-done.17.refs_4_ = bf16[256,256]{1,0:T(8,128)(2,1)S(1)} collective-permute-done((bf16[256,256]{1,0:T(8,128)(2,1)S(1)}, bf16[256,256]{1,0:T(8,128)(2,1)S(1)}, u32[]{:S(2)}, u32[]{:S(2)}) %collective-permute-start.17) | collective-permute-done | bytes 131104 | tf_op jit(solution)/shard_map/ppermute | solution.py:336
  52.7 2.4 %front1.1 = (bf16[256,1024]{1,0:T(8,128)(2,1)S(1)}, f32[256,128]{1,0:T(8,128)S(1)}, f32[256,128]{1,0:T(8,128)S(1)}, f32[64,128]{1,0:T(8,128)S(1)}, f32[256,1024]{1,0:T(8,128)S(1)}, /*index=5*/f32[256,128]{1,0:T(8,128)S(1)}) custom-call(s32[2,3]{1,0:T(2,128)S(1)} %copy-done.8, bf16[256,256]{1,0:T(8,128)(2,1)S(1)} %get-tuple-element.159.refs_4_.refs_1_, ...), custom_call_target="tpu_custom_call" | custom-call | flops 40000000000 | bytes 1 | tf_op jit(solution)/shard_map/front1/pallas_call | solution.py:108
  55.2 2.9 %collective-permute-start.20 = (f32[64,128]{1,0:T(8,128)S(1)}, f32[64,128]{1,0:T(8,128)S(1)}, u32[]{:S(2)}, u32[]{:S(2)}) collective-permute-start(f32[64,128]{1,0:T(8,128)S(1)} %get-tuple-element.163.refs_6_), channel_id=1, source_target_pairs={{0,3},{1,2},{2,1},{3,0},{4,7},{5,6},{6,5},{7,4},{8,11},{9,10},{10,... | collective-permute-start | bytes 98312 | tf_op jit(solution)/shard_map/ppermute | solution.py:336
  58.7 2.0 %wide1.1 = (f32[256,768]{1,0:T(8,128)S(1)}, bf16[256,768]{1,0:T(8,128)(2,1)S(1)}, f32[256,128]{1,0:T(8,128)S(1)}, bf16[256,128]{1,0:T(8,128)(2,1)S(1)}, bf16[256...) custom-call(s32[2,3]{1,0:T(2,128)S(1)} %copy-done.8, bf16[256,1024]{1,0:T(8,128)(2,1)S(1)} %get-tuple-element.164.refs_1_, ...), custom_call_target="tpu_custom_call" | custom-call | flops 40000000000 | bytes 1 | tf_op jit(solution)/shard_map/wide1/pallas_call | solution.py:108
  60.7 2.2 %collective-permute-start.24 = (bf16[256,128]{1,0:T(8,128)(2,1)S(1)}, bf16[256,128]{1,0:T(8,128)(2,1)S(1)}, u32[]{:S(2)}, u32[]{:S(2)}) collective-permute-start(bf16[256,128]{1,0:T(8,128)(2,1)S(1)} %get-tuple-element.171), channel_id=1, source_target_pairs={{0,12},{4,8},{8,4},{12,0},{1,13},{5,9},{9,5},{13,1},{2,14},{6,10},... | collective-permute-start | bytes 196616 | tf_op jit(solution)/shard_map/ppermute | solution.py:336
  62.9 2.3 %collective-permute-start.26 = (bf16[256,128]{1,0:T(8,128)(2,1)S(1)}, bf16[256,128]{1,0:T(8,128)(2,1)S(1)}, u32[]{:S(2)}, u32[]{:S(2)}) collective-permute-start(bf16[256,128]{1,0:T(8,128)(2,1)S(1)} %get-tuple-element.173), channel_id=1, source_target_pairs={{0,4},{4,0},{8,12},{12,8},{1,5},{5,1},{9,13},{13,9},{2,6},{6,2},{1... | collective-permute-start | bytes 196616 | tf_op jit(solution)/shard_map/ppermute | solution.py:336
  65.2 2.2 %carry1.1 = (f32[64,128]{1,0:T(8,128)S(1)}, bf16[256,128]{1,0:T(8,128)(2,1)S(1)}) custom-call(s32[2,3]{1,0:T(2,128)S(1)} %copy-done.8, f32[256,128]{1,0:T(8,128)S(1)} %get-tuple-element.162.refs_1_, f32[64,640]{1,0:T(8,128)S(1)} %get-tuple-element.160.refs_5_.refs_3_.refs_2_.refs_7_.refs_1_.refs_4_.refs_6_, f32[64,128]{1,0:T(8,128)S(1)} %collective-permute-done.18.refs_3_, ...), custom_call_target="tpu_custom_call" | custom-call | flops 40000000000 | bytes 1 | tf_op jit(solution)/shard_map/carry1/pallas_call | solution.py:108
  67.4 2.2 %collective-permute-start.23 = (bf16[256,128]{1,0:T(8,128)(2,1)S(1)}, bf16[256,128]{1,0:T(8,128)(2,1)S(1)}, u32[]{:S(2)}, u32[]{:S(2)}) collective-permute-start(bf16[256,128]{1,0:T(8,128)(2,1)S(1)} %get-tuple-element.168.refs_1_.refs_6_), channel_id=1, source_target_pairs={{0,12},{4,8},{8,4},{12,0},{1,13},{5,9},{9,5},{13,1},{2,14},{6,10},... | collective-permute-start | bytes 196616 | tf_op jit(solution)/shard_map/ppermute | solution.py:336
  70.5 1.4 collective-permute-start.21
  71.9 1.6 adjoint_local1.1
  73.5 2.7 %collective-permute-start.30 = (f32[64,128]{1,0:T(8,128)S(1)}, f32[64,128]{1,0:T(8,128)S(1)}, u32[]{:S(2)}, u32[]{:S(2)}) collective-permute-start(f32[64,128]{1,0:T(8,128)S(1)} %get-tuple-element.177), channel_id=1, source_target_pairs={{0,3},{1,2},{2,1},{3,0},{4,7},{5,6},{6,5},{7,4},{8,11},{9,10},{10,... | collective-permute-start | bytes 98312 | tf_op jit(solution)/shard_map/ppermute | solution.py:336
  77.1 1.5 middle1.1
  78.5 1.5 states_before1.1.refs_7_.refs_2_
  80.2 2.4 %adjoint1.1 = (f32[64,128]{1,0:T(8,128)S(1)}, bf16[256,128]{1,0:T(8,128)(2,1)S(1)}) custom-call(s32[2,3]{1,0:T(2,128)S(1)} %copy-done.8, f32[256,128]{1,0:T(8,128)S(1)} %get-tuple-element.175.refs_1_.refs_3_, f32[256,128]{1,0:T(8,128)S(1)} %get-tuple-element.176.refs_2_, ...), custom_call_target="tpu_custom_call" | custom-call | flops 40000000000 | bytes 1 | tf_op jit(solution)/shard_map/adjoint1/pallas_call | solution.py:108
  82.6 1.9 %grad_normed1.1 = (f32[272,256]{1,0:T(8,128)S(1)}, bf16[272,256]{1,0:T(8,128)(2,1)S(1)}, bf16[272,256]{1,0:T(8,128)(2,1)S(1)}, bf16[272,256]{1,0:T(8,128)(2,1)S(1)}) custom-call(s32[2,3]{1,0:T(2,128)S(1)} %copy-done.8, bf16[256,768]{1,0:T(8,128)(2,1)S(1)} %get-tuple-element.170.refs_4_.refs_1_, bf16[256,128]{1,0:T(8,128)(2,1)S(1)} %get-tuple-element.179.refs_2_.refs_5_, ...), custom_call_target="tpu_custom_call" | custom-call | flops 40000000000 | bytes 1 | tf_op jit(solution)/shard_map/grad_normed1/pallas_call | solution.py:108
  84.4 2.1 %collective-permute-start.31 = (bf16[272,256]{1,0:T(8,128)(2,1)S(1)}, bf16[272,256]{1,0:T(8,128)(2,1)S(1)}, u32[]{:S(2)}, u32[]{:S(2)}) collective-permute-start(bf16[272,256]{1,0:T(8,128)(2,1)S(1)} %get-tuple-element.182), channel_id=1, source_target_pairs={{0,12},{4,8},{8,4},{12,0},{1,13},{5,9},{9,5},{13,1},{2,14},{6,10},... | collective-permute-start | bytes 417800 | tf_op jit(solution)/shard_map/ppermute | solution.py:336
  86.7 2.2 %collective-permute-start.33 = (bf16[272,256]{1,0:T(8,128)(2,1)S(1)}, bf16[272,256]{1,0:T(8,128)(2,1)S(1)}, u32[]{:S(2)}, u32[]{:S(2)}) collective-permute-start(bf16[272,256]{1,0:T(8,128)(2,1)S(1)} %get-tuple-element.184), channel_id=1, source_target_pairs={{0,4},{4,0},{8,12},{12,8},{1,5},{5,1},{9,13},{13,9},{2,6},{6,2},{1... | collective-permute-start | bytes 417800 | tf_op jit(solution)/shard_map/ppermute | solution.py:336
  91.1 2.8 %ssm_grads1.1.refs_9_.refs_7_ = f32[640,256]{1,0:T(8,128)S(1)} custom-call(s32[2,3]{1,0:T(2,128)S(1)} %copy-done.8, f32[256,128]{1,0:T(8,128)S(1)} %get-tuple-element.162.refs_1_, f32[256,64,128]{2,1,0:T(8,128)S(1)} %states_before1.1.refs_7_.refs_2_, f32[256,128]{1,0:T(8,128)S(1)} %get-tuple-element.175.refs_1_.refs_3_, ...), custom_call_target="tpu_custom_call" | custom-call | flops 1 | bytes 1 | tf_op jit(solution)/shard_map/ssm_grads1/pallas_call | solution.py:108
  94.3 1.4 layer_grad1.1
  95.7 2.1 %collective-permute-start.36 = (bf16[256,256]{1,0:T(8,128)(2,1)S(1)}, bf16[256,256]{1,0:T(8,128)(2,1)S(1)}, u32[]{:S(2)}, u32[]{:S(2)}) collective-permute-start(bf16[256,256]{1,0:T(8,128)(2,1)S(1)} %get-tuple-element.192.refs_5_.refs_1_), channel_id=1, source_target_pairs={{0,12},{4,8},{8,4},{12,0},{1,13},{5,9},{9,5},{13,1},{2,14},{6,10},... | collective-permute-start | bytes 393224 | tf_op jit(solution)/shard_map/ppermute | solution.py:336
  97.8 2.3 %collective-permute-start.34 = (bf16[256,256]{1,0:T(8,128)(2,1)S(1)}, bf16[256,256]{1,0:T(8,128)(2,1)S(1)}, u32[]{:S(2)}, u32[]{:S(2)}) collective-permute-start(bf16[256,256]{1,0:T(8,128)(2,1)S(1)} %get-tuple-element.192.refs_5_.refs_1_), channel_id=1, source_target_pairs={{0,4},{4,0},{8,12},{12,8},{1,5},{5,1},{9,13},{13,9},{2,6},{6,2},{1... | collective-permute-start | bytes 393224 | tf_op jit(solution)/shard_map/ppermute | solution.py:336
  100.2 2.0 %weight_grads1.1 = (bf16[2,1024,128]{2,1,0:T(8,128)(2,1)S(1)}, bf16[2,1024,128]{2,1,0:T(8,128)(2,1)S(1)}, bf16[2,912,128]{2,1,0:T(8,128)(2,1)S(1)}, bf16[2,912,128]{2,1,0:T(8,128)(2,1)S(1)}) custom-call(s32[2,3]{1,0:T(2,128)S(1)} %copy-done.8, bf16[2304,256]{1,0:T(8,128)(2,1)S(1)} %turn1.1.refs_4_.refs_7_.refs_1_, ...), custom_call_target="tpu_custom_call" | custom-call | flops 1 | bytes 1 | tf_op jit(solution)/shard_map/weight_grads1/pallas_call | solution.py:108
  102.3 1.2 top_parts.1
  103.4 2.0 %collective-permute-start.44 = (bf16[2,912,128]{2,1,0:T(8,128)(2,1)S(1)}, bf16[2,912,128]{2,1,0:T(8,128)(2,1)S(1)}, u32[]{:S(2)}, u32[]{:S(2)}) collective-permute-start(bf16[2,912,128]{2,1,0:T(8,128)(2,1)S(1)} %get-tuple-element.208), channel_id=1, source_target_pairs={{0,2},{1,3},{2,0},{3,1},{4,6},{5,7},{6,4},{7,5},{8,10},{9,11},{10,... | collective-permute-start | bytes 1400840 | tf_op jit(solution)/shard_map/ppermute | solution.py:336
  105.4 1.1 collective-permute-start.43
  106.5 2.4 %collective-permute-done.35.refs_3_ = bf16[256,256]{1,0:T(8,128)(2,1)S(1)} collective-permute-done((bf16[256,256]{1,0:T(8,128)(2,1)S(1)}, bf16[256,256]{1,0:T(8,128)(2,1)S(1)}, u32[]{:S(2)}, u32[]{:S(2)}) %collective-permute-start.35) | collective-permute-done | bytes 131104 | tf_op jit(solution)/shard_map/ppermute | solution.py:336
  108.9 2.4 %grad_middle0.1 = (bf16[256,768]{1,0:T(8,128)(2,1)S(1)}, bf16[256,768]{1,0:T(8,128)(2,1)S(1)}, bf16[256,1024]{1,0:T(8,128)(2,1)S(1)}, f32[256,128]{1,0:T(8,128)S...) custom-call(s32[2,3]{1,0:T(2,128)S(1)} %copy-done.8, ...), custom_call_target="tpu_custom_call" | custom-call | flops 40000000000 | bytes 1 | tf_op jit(solution)/shard_map/grad_middle0/pallas_call | solution.py:108
  111.3 1.9 %collective-permute-start.40 = (bf16[256,128]{1,0:T(8,128)(2,1)S(1)}, bf16[256,128]{1,0:T(8,128)(2,1)S(1)}, u32[]{:S(2)}, u32[]{:S(2)}) collective-permute-start(bf16[256,128]{1,0:T(8,128)(2,1)S(1)} %get-tuple-element.203), channel_id=1, source_target_pairs={{0,12},{4,8},{8,4},{12,0},{1,13},{5,9},{9,5},{13,1},{2,14},{6,10},... | collective-permute-start | bytes 196616 | tf_op jit(solution)/shard_map/ppermute | solution.py:336
  113.2 2.5 %collective-permute-start.42 = (bf16[256,128]{1,0:T(8,128)(2,1)S(1)}, bf16[256,128]{1,0:T(8,128)(2,1)S(1)}, u32[]{:S(2)}, u32[]{:S(2)}) collective-permute-start(bf16[256,128]{1,0:T(8,128)(2,1)S(1)} %get-tuple-element.205), channel_id=1, source_target_pairs={{0,4},{4,0},{8,12},{12,8},{1,5},{5,1},{9,13},{13,9},{2,6},{6,2},{1... | collective-permute-start | bytes 196616 | tf_op jit(solution)/shard_map/ppermute | solution.py:336
  116.5 1.2 collective-permute-done.43.refs_2_
  118.5 1.2 collective-permute-start.48
  120.4 1.6 adjoint_local0.1
  122.0 1.6 collective-permute-start.51
  124.3 1.3 collective-permute-start.49
  125.6 2.1 %weight_grads0.1 = (bf16[2,1024,128]{2,1,0:T(8,128)(2,1)S(1)}, bf16[2,1024,128]{2,1,0:T(8,128)(2,1)S(1)}, bf16[2,912,128]{2,1,0:T(8,128)(2,1)S(1)}, bf16[2,912,128]{2,1,0:T(8,128)(2,1)S(1)}) custom-call(s32[2,3]{1,0:T(2,128)S(1)} %copy-done.8, bf16[2304,256]{1,0:T(8,128)(2,1)S(1)} %copy-done.3, ...), custom_call_target="tpu_custom_call" | custom-call | flops 1 | bytes 1 | tf_op jit(solution)/shard_map/weight_grads0/pallas_call | solution.py:108
  128.5 1.7 %collective-permute-start.46 = (bf16[2,912,128]{2,1,0:T(8,128)(2,1)S(1)}, bf16[2,912,128]{2,1,0:T(8,128)(2,1)S(1)}, u32[]{:S(2)}, u32[]{:S(2)}) collective-permute-start(bf16[2,912,128]{2,1,0:T(8,128)(2,1)S(1)} %get-tuple-element.214), channel_id=1, source_target_pairs={{0,2},{1,3},{2,0},{3,1},{4,6},{5,7},{6,4},{7,5},{8,10},{9,11},{10,... | collective-permute-start | bytes 1400840 | tf_op jit(solution)/shard_map/ppermute | solution.py:336
  131.1 2.4 %adjoint0.1 = (f32[64,128]{1,0:T(8,128)S(1)}, bf16[256,128]{1,0:T(8,128)(2,1)S(1)}) custom-call(s32[2,3]{1,0:T(2,128)S(1)} %copy-done.8, f32[256,128]{1,0:T(8,128)S(1)} %get-tuple-element.218.refs_1_.refs_3_, f32[256,128]{1,0:T(8,128)S(1)} %get-tuple-element.219.refs_2_, f32[64,640]{1,0:T(8,128)S(1)} %get-tuple-element.145.refs_2_.refs_6_.refs_1_.refs_3_.refs_4_, ...), custom_call_target="tpu_custom_call" | custom-call | flops 40000000000 | bytes 1 | tf_op jit(solution)/shard_map/adjoint0/pallas_call | solution.py:108
  133.6 1.9 %grad_normed0.1 = (f32[272,256]{1,0:T(8,128)S(1)}, bf16[272,256]{1,0:T(8,128)(2,1)S(1)}, bf16[272,256]{1,0:T(8,128)(2,1)S(1)}, bf16[272,256]{1,0:T(8,128)(2,1)S(1)}) custom-call(s32[2,3]{1,0:T(2,128)S(1)} %copy-done.8, bf16[256,768]{1,0:T(8,128)(2,1)S(1)} %get-tuple-element.197.refs_1_, bf16[256,128]{1,0:T(8,128)(2,1)S(1)} %get-tuple-element.220.refs_2_.refs_5_, ...), custom_call_target="tpu_custom_call" | custom-call | flops 40000000000 | bytes 1 | tf_op jit(solution)/shard_map/grad_normed0/pallas_call | solution.py:108
  135.4 1.8 %collective-permute-start.56 = (bf16[272,256]{1,0:T(8,128)(2,1)S(1)}, bf16[272,256]{1,0:T(8,128)(2,1)S(1)}, u32[]{:S(2)}, u32[]{:S(2)}) collective-permute-start(bf16[272,256]{1,0:T(8,128)(2,1)S(1)} %get-tuple-element.234), channel_id=1, source_target_pairs={{0,12},{4,8},{8,4},{12,0},{1,13},{5,9},{9,5},{13,1},{2,14},{6,10},... | collective-permute-start | bytes 417800 | tf_op jit(solution)/shard_map/ppermute | solution.py:336
  137.7 1.5 states_before0.1.refs_7_.refs_2_
  139.2 2.3 %collective-permute-start.58 = (bf16[272,256]{1,0:T(8,128)(2,1)S(1)}, bf16[272,256]{1,0:T(8,128)(2,1)S(1)}, u32[]{:S(2)}, u32[]{:S(2)}) collective-permute-start(bf16[272,256]{1,0:T(8,128)(2,1)S(1)} %get-tuple-element.236), channel_id=1, source_target_pairs={{0,4},{4,0},{8,12},{12,8},{1,5},{5,1},{9,13},{13,9},{2,6},{6,2},{1... | collective-permute-start | bytes 417800 | tf_op jit(solution)/shard_map/ppermute | solution.py:336
  145.2 2.8 %ssm_grads0.1 = (f32[640,256]{1,0:T(8,128)S(1)}, f32[640,256]{1,0:T(8,128)S(1)}) custom-call(s32[2,3]{1,0:T(2,128)S(1)} %copy-done.8, f32[256,128]{1,0:T(8,128)S(1)} %copy-done.13, f32[256,64,128]{2,1,0:T(8,128)S(1)} %states_before0.1.refs_7_.refs_2_, f32[256,128]{1,0:T(8,128)S(1)} %get-tuple-element.218.refs_1_.refs_3_, ...), custom_call_target="tpu_custom_call" | custom-call | flops 40000000000 | bytes 1 | tf_op jit(solution)/shard_map/ssm_grads0/pallas_call | solution.py:108
  149.1 1.2 layer_grad0.1
  152.5 1.5 collective-permute-start.61
  154.0 1.1 collective-permute-start.62
  156.9 1.8 %own_columns.1 = (f32[1,256,768]{2,1,0:T(8,128)}, f32[1,128,768]{2,1,0:T(8,128)}, f32[1,192,1024]{2,1,0:T(8,128)}, f32[1,2,256,256]{3,2,1,0:T(8,128)}, f32[8,128]{1,0:T(8,128)S(1)}) custom-call(s32[2,3]{1,0:T(2,128)S(1)} %copy-done.8, bf16[272,256]{1,0:T(8,128)(2,1)S(1)} %collective-permute-done.59.refs_4_.refs_1_, ...), custom_call_target="tpu_custom_call" | custom-call | flops 1 | bytes 1 | tf_op jit(solution)/shard_map/own_columns/pallas_call | solution.py:108
  162.0 2.6 %finish.1 = (f32[1,256,768]{2,1,0:T(8,128)}, f32[1,128,768]{2,1,0:T(8,128)}, f32[1,192,1024]{2,1,0:T(8,128)}, f32[1,192]{1,0:T(1,128)}, f32[1,192]{1,0:T(1,128)}...) custom-call(s32[2,3]{1,0:T(2,128)S(1)} %copy-done.8, ...), custom_call_target="tpu_custom_call", output_to_operand_aliasing={{0}: (4, {}), {1}: (5, {}), {2}: (6, {})} | custom-call | flops 1 | bytes 1 | tf_op jit(solution)/shard_map/finish/pallas_call | solution.py:108
  (156 shorter events, 31.0 us)
Async XLA Ops:
  3.1 2.1 %collective-permute-start = (f32[64,640]{1,0:T(8,128)}, f32[64,640]{1,0:T(8,128)S(1)}, u32[]{:S(2)}, u32[]{:S(2)}) collective-permute-start(f32[64,640]{1,0:T(8,128)} %make_pack.1.refs_2_), channel_id=1, source_target_pairs={{0,16},{16,0},{1,17},{17,1},{2,18},{18,2},{3,19},{19,3},{4,20},{20... | collective-permute-start | bytes 491528 | tf_op jit(solution)/shard_map/ppermute | solution.py:279
  3.8 7.8 %collective-permute-start.5 = (bf16[1024,768]{1,0:T(8,128)(2,1)S(1)}, bf16[1024,768]{1,0:T(8,128)(2,1)S(1)}, u32[]{:S(2)}, u32[]{:S(2)}) collective-permute-start(bf16[1024,768]{1,0:T(8,128)(2,1)S(1)} %bitcast.13), channel_id=1, source_target_pairs={{0,16},{16,0},{1,17},{17,1},{2,18},{18,2},{3,19},{19,3},{4,20},{20... | collective-permute-start | bytes 4718600 | tf_op jit(solution)/shard_map/ppermute | solution.py:279
  7.4 6.0 %collective-permute-start.4 = (f32[64,128]{1,0:T(8,128)S(1)}, f32[64,128]{1,0:T(8,128)S(1)}, u32[]{:S(2)}, u32[]{:S(2)}) collective-permute-start(f32[64,128]{1,0:T(8,128)S(1)} %get-tuple-element.146), channel_id=1, source_target_pairs={{0,3},{1,2},{2,1},{3,0},{4,7},{5,6},{6,5},{7,4},{8,11},{9,10},{10,... | collective-permute-start | bytes 98312 | tf_op jit(solution)/shard_map/ppermute | solution.py:336
  10.9 3.9 %collective-permute-start.3 = (f32[64,128]{1,0:T(8,128)S(1)}, f32[64,128]{1,0:T(8,128)S(1)}, u32[]{:S(2)}, u32[]{:S(2)}) collective-permute-start(f32[64,128]{1,0:T(8,128)S(1)} %get-tuple-element.146), channel_id=1, source_target_pairs={{0,2},{1,3},{2,0},{3,1},{4,6},{5,7},{6,4},{7,5},{8,10},{9,11},{10,... | collective-permute-start | bytes 98312 | tf_op jit(solution)/shard_map/ppermute | solution.py:336
  11.3 3.9 %collective-permute-start.2 = (f32[64,128]{1,0:T(8,128)S(1)}, f32[64,128]{1,0:T(8,128)S(1)}, u32[]{:S(2)}, u32[]{:S(2)}) collective-permute-start(f32[64,128]{1,0:T(8,128)S(1)} %get-tuple-element.146), channel_id=1, source_target_pairs={{0,1},{1,0},{2,3},{3,2},{4,5},{5,4},{6,7},{7,6},{8,9},{9,8},{10,11... | collective-permute-start | bytes 98312 | tf_op jit(solution)/shard_map/ppermute | solution.py:336
  11.6 10.4 %collective-permute-start.9 = (bf16[512,768]{1,0:T(8,128)(2,1)S(1)}, bf16[512,768]{1,0:T(8,128)(2,1)S(1)}, u32[]{:S(2)}, u32[]{:S(2)}) collective-permute-start(bf16[512,768]{1,0:T(8,128)(2,1)S(1)} %bitcast.19), channel_id=1, source_target_pairs={{0,16},{16,0},{1,17},{17,1},{2,18},{18,2},{3,19},{19,3},{4,20},{20... | collective-permute-start | bytes 2359304 | tf_op jit(solution)/shard_map/ppermute | solution.py:279
  11.6 10.4 %collective-permute-start.10 = (bf16[768,1024]{1,0:T(8,128)(2,1)S(1)}, bf16[768,1024]{1,0:T(8,128)(2,1)S(1)}, u32[]{:S(2)}, u32[]{:S(2)}) collective-permute-start(bf16[768,1024]{1,0:T(8,128)(2,1)S(1)} %bitcast.16), channel_id=1, source_target_pairs={{0,16},{16,0},{1,17},{17,1},{2,18},{18,2},{3,19},{19,3},{4,20},{20... | collective-permute-start | bytes 4718600 | tf_op jit(solution)/shard_map/ppermute | solution.py:279
  17.5 6.1 %collective-permute-start.8 = (bf16[256,128]{1,0:T(8,128)(2,1)S(1)}, bf16[256,128]{1,0:T(8,128)(2,1)S(1)}, u32[]{:S(2)}, u32[]{:S(2)}) collective-permute-start(bf16[256,128]{1,0:T(8,128)(2,1)S(1)} %get-tuple-element.148.refs_5_.refs_1_), channel_id=1, source_target_pairs={{0,12},{4,8},{8,4},{12,0},{1,13},{5,9},{9,5},{13,1},{2,14},{6,10},... | collective-permute-start | bytes 196616 | tf_op jit(solution)/shard_map/ppermute | solution.py:336
  21.1 5.2 %collective-permute-start.7 = (bf16[256,128]{1,0:T(8,128)(2,1)S(1)}, bf16[256,128]{1,0:T(8,128)(2,1)S(1)}, u32[]{:S(2)}, u32[]{:S(2)}) collective-permute-start(bf16[256,128]{1,0:T(8,128)(2,1)S(1)} %get-tuple-element.148.refs_5_.refs_1_), channel_id=1, source_target_pairs={{0,8},{4,12},{8,0},{12,4},{1,9},{5,13},{9,1},{13,5},{2,10},{6,14},... | collective-permute-start | bytes 196616 | tf_op jit(solution)/shard_map/ppermute | solution.py:336
  21.1 5.2 %collective-permute-start.6 = (bf16[256,128]{1,0:T(8,128)(2,1)S(1)}, bf16[256,128]{1,0:T(8,128)(2,1)S(1)}, u32[]{:S(2)}, u32[]{:S(2)}) collective-permute-start(bf16[256,128]{1,0:T(8,128)(2,1)S(1)} %get-tuple-element.148.refs_5_.refs_1_), channel_id=1, source_target_pairs={{0,4},{4,0},{8,12},{12,8},{1,5},{5,1},{9,13},{13,9},{2,6},{6,2},{1... | collective-permute-start | bytes 196616 | tf_op jit(solution)/shard_map/ppermute | solution.py:336
  27.9 8.3 %collective-permute-start.11 = (bf16[256,256]{1,0:T(8,128)(2,1)S(1)}, bf16[256,256]{1,0:T(8,128)(2,1)S(1)}, u32[]{:S(2)}, u32[]{:S(2)}) collective-permute-start(bf16[256,256]{1,0:T(8,128)(2,1)S(1)} %get-tuple-element.154), channel_id=1, source_target_pairs={{0,12},{4,8},{8,4},{12,0},{1,13},{5,9},{9,5},{13,1},{2,14},{6,10},... | collective-permute-start | bytes 393224 | tf_op jit(solution)/shard_map/ppermute | solution.py:336
  30.1 10.1 %collective-permute-start.12 = (bf16[256,256]{1,0:T(8,128)(2,1)S(1)}, bf16[256,256]{1,0:T(8,128)(2,1)S(1)}, u32[]{:S(2)}, u32[]{:S(2)}) collective-permute-start(bf16[256,256]{1,0:T(8,128)(2,1)S(1)} %get-tuple-element.155), channel_id=1, source_target_pairs={{0,8},{4,12},{8,0},{12,4},{1,9},{5,13},{9,1},{13,5},{2,10},{6,14},... | collective-permute-start | bytes 393224 | tf_op jit(solution)/shard_map/ppermute | solution.py:336
  30.1 10.1 %collective-permute-start.13 = (bf16[256,256]{1,0:T(8,128)(2,1)S(1)}, bf16[256,256]{1,0:T(8,128)(2,1)S(1)}, u32[]{:S(2)}, u32[]{:S(2)}) collective-permute-start(bf16[256,256]{1,0:T(8,128)(2,1)S(1)} %get-tuple-element.156), channel_id=1, source_target_pairs={{0,4},{4,0},{8,12},{12,8},{1,5},{5,1},{9,13},{13,9},{2,6},{6,2},{1... | collective-permute-start | bytes 393224 | tf_op jit(solution)/shard_map/ppermute | solution.py:336
  40.8 6.9 %collective-permute-start.16 = (bf16[256,256]{1,0:T(8,128)(2,1)S(1)}, bf16[256,256]{1,0:T(8,128)(2,1)S(1)}, u32[]{:S(2)}, u32[]{:S(2)}) collective-permute-start(bf16[256,256]{1,0:T(8,128)(2,1)S(1)} %get-tuple-element.159.refs_4_.refs_1_), channel_id=1, source_target_pairs={{0,8},{4,12},{8,0},{12,4},{1,9},{5,13},{9,1},{13,5},{2,10},{6,14},... | collective-permute-start | bytes 393224 | tf_op jit(solution)/shard_map/ppermute | solution.py:336
  40.9 8.4 %collective-permute-start.15 = (bf16[256,256]{1,0:T(8,128)(2,1)S(1)}, bf16[256,256]{1,0:T(8,128)(2,1)S(1)}, u32[]{:S(2)}, u32[]{:S(2)}) collective-permute-start(bf16[256,256]{1,0:T(8,128)(2,1)S(1)} %get-tuple-element.159.refs_4_.refs_1_), channel_id=1, source_target_pairs={{0,4},{4,0},{8,12},{12,8},{1,5},{5,1},{9,13},{13,9},{2,6},{6,2},{1... | collective-permute-start | bytes 393224 | tf_op jit(solution)/shard_map/ppermute | solution.py:336
  47.7 5.0 %collective-permute-start.17 = (bf16[256,256]{1,0:T(8,128)(2,1)S(1)}, bf16[256,256]{1,0:T(8,128)(2,1)S(1)}, u32[]{:S(2)}, u32[]{:S(2)}) collective-permute-start(bf16[256,256]{1,0:T(8,128)(2,1)S(1)} %collective-permute-done.16.refs_3_), channel_id=1, source_target_pairs={{0,4},{4,0},{8,12},{12,8},{1,5},{5,1},{9,13},{13,9},{2,6},{6,2},{1... | collective-permute-start | bytes 393224 | tf_op jit(solution)/shard_map/ppermute | solution.py:336
  47.8 19.6 %collective-permute-start.27 = (f32[256,256]{1,0:T(8,128)S(1)}, f32[256,256]{1,0:T(8,128)S(1)}, u32[]{:S(2)}, u32[]{:S(2)}) collective-permute-start(f32[256,256]{1,0:T(8,128)S(1)} %get-tuple-element.174.refs_3_.refs_7_), channel_id=1, source_target_pairs={{0,16},{16,0},{1,17},{17,1},{2,18},{18,2},{3,19},{19,3},{4,20},{20... | collective-permute-start | bytes 786440 | tf_op jit(solution)/shard_map/ppermute | solution.py:279
  48.7 23.2 %collective-permute-start.14 = (bf16[2304,256]{1,0:T(8,128)(2,1)S(1)}, bf16[2304,256]{1,0:T(8,128)(2,1)S(1)}, u32[]{:S(2)}, u32[]{:S(2)}) collective-permute-start(bf16[2304,256]{1,0:T(8,128)(2,1)S(1)} %turn0.1.refs_7_.refs_1_.refs_8_), channel_id=1, source_target_pairs={{0,16},{16,0},{1,17},{17,1},{2,18},{18,2},{3,19},{19,3},{4,20},{20... | collective-permute-start | bytes 3538952 | tf_op jit(solution)/shard_map/ppermute | solution.py:279
  55.2 5.5 %collective-permute-start.20 = (f32[64,128]{1,0:T(8,128)S(1)}, f32[64,128]{1,0:T(8,128)S(1)}, u32[]{:S(2)}, u32[]{:S(2)}) collective-permute-start(f32[64,128]{1,0:T(8,128)S(1)} %get-tuple-element.163.refs_6_), channel_id=1, source_target_pairs={{0,3},{1,2},{2,1},{3,0},{4,7},{5,6},{6,5},{7,4},{8,11},{9,10},{10,... | collective-permute-start | bytes 98312 | tf_op jit(solution)/shard_map/ppermute | solution.py:336
  58.0 4.8 %collective-permute-start.19 = (f32[64,128]{1,0:T(8,128)S(1)}, f32[64,128]{1,0:T(8,128)S(1)}, u32[]{:S(2)}, u32[]{:S(2)}) collective-permute-start(f32[64,128]{1,0:T(8,128)S(1)} %get-tuple-element.163.refs_6_), channel_id=1, source_target_pairs={{0,2},{1,3},{2,0},{3,1},{4,6},{5,7},{6,4},{7,5},{8,10},{9,11},{10,... | collective-permute-start | bytes 98312 | tf_op jit(solution)/shard_map/ppermute | solution.py:336
  58.1 4.8 %collective-permute-start.18 = (f32[64,128]{1,0:T(8,128)S(1)}, f32[64,128]{1,0:T(8,128)S(1)}, u32[]{:S(2)}, u32[]{:S(2)}) collective-permute-start(f32[64,128]{1,0:T(8,128)S(1)} %get-tuple-element.163.refs_6_), channel_id=1, source_target_pairs={{0,1},{1,0},{2,3},{3,2},{4,5},{5,4},{6,7},{7,6},{8,9},{9,8},{10,11... | collective-permute-start | bytes 98312 | tf_op jit(solution)/shard_map/ppermute | solution.py:336
  60.7 8.9 %collective-permute-start.24 = (bf16[256,128]{1,0:T(8,128)(2,1)S(1)}, bf16[256,128]{1,0:T(8,128)(2,1)S(1)}, u32[]{:S(2)}, u32[]{:S(2)}) collective-permute-start(bf16[256,128]{1,0:T(8,128)(2,1)S(1)} %get-tuple-element.171), channel_id=1, source_target_pairs={{0,12},{4,8},{8,4},{12,0},{1,13},{5,9},{9,5},{13,1},{2,14},{6,10},... | collective-permute-start | bytes 196616 | tf_op jit(solution)/shard_map/ppermute | solution.py:336
  62.9 7.6 %collective-permute-start.25 = (bf16[256,128]{1,0:T(8,128)(2,1)S(1)}, bf16[256,128]{1,0:T(8,128)(2,1)S(1)}, u32[]{:S(2)}, u32[]{:S(2)}) collective-permute-start(bf16[256,128]{1,0:T(8,128)(2,1)S(1)} %get-tuple-element.172), channel_id=1, source_target_pairs={{0,8},{4,12},{8,0},{12,4},{1,9},{5,13},{9,1},{13,5},{2,10},{6,14},... | collective-permute-start | bytes 196616 | tf_op jit(solution)/shard_map/ppermute | solution.py:336
  62.9 9.0 %collective-permute-start.26 = (bf16[256,128]{1,0:T(8,128)(2,1)S(1)}, bf16[256,128]{1,0:T(8,128)(2,1)S(1)}, u32[]{:S(2)}, u32[]{:S(2)}) collective-permute-start(bf16[256,128]{1,0:T(8,128)(2,1)S(1)} %get-tuple-element.173), channel_id=1, source_target_pairs={{0,4},{4,0},{8,12},{12,8},{1,5},{5,1},{9,13},{13,9},{2,6},{6,2},{1... | collective-permute-start | bytes 196616 | tf_op jit(solution)/shard_map/ppermute | solution.py:336
  67.4 8.8 %collective-permute-start.23 = (bf16[256,128]{1,0:T(8,128)(2,1)S(1)}, bf16[256,128]{1,0:T(8,128)(2,1)S(1)}, u32[]{:S(2)}, u32[]{:S(2)}) collective-permute-start(bf16[256,128]{1,0:T(8,128)(2,1)S(1)} %get-tuple-element.168.refs_1_.refs_6_), channel_id=1, source_target_pairs={{0,12},{4,8},{8,4},{12,0},{1,13},{5,9},{9,5},{13,1},{2,14},{6,10},... | collective-permute-start | bytes 196616 | tf_op jit(solution)/shard_map/ppermute | solution.py:336
  69.6 7.5 %collective-permute-start.22 = (bf16[256,128]{1,0:T(8,128)(2,1)S(1)}, bf16[256,128]{1,0:T(8,128)(2,1)S(1)}, u32[]{:S(2)}, u32[]{:S(2)}) collective-permute-start(bf16[256,128]{1,0:T(8,128)(2,1)S(1)} %get-tuple-element.168.refs_1_.refs_6_), channel_id=1, source_target_pairs={{0,8},{4,12},{8,0},{12,4},{1,9},{5,13},{9,1},{13,5},{2,10},{6,14},... | collective-permute-start | bytes 196616 | tf_op jit(solution)/shard_map/ppermute | solution.py:336
  70.5 6.5 %collective-permute-start.21 = (bf16[256,128]{1,0:T(8,128)(2,1)S(1)}, bf16[256,128]{1,0:T(8,128)(2,1)S(1)}, u32[]{:S(2)}, u32[]{:S(2)}) collective-permute-start(bf16[256,128]{1,0:T(8,128)(2,1)S(1)} %get-tuple-element.168.refs_1_.refs_6_), channel_id=1, source_target_pairs={{0,4},{4,0},{8,12},{12,8},{1,5},{5,1},{9,13},{13,9},{2,6},{6,2},{1... | collective-permute-start | bytes 196616 | tf_op jit(solution)/shard_map/ppermute | solution.py:336
  73.5 6.6 %collective-permute-start.30 = (f32[64,128]{1,0:T(8,128)S(1)}, f32[64,128]{1,0:T(8,128)S(1)}, u32[]{:S(2)}, u32[]{:S(2)}) collective-permute-start(f32[64,128]{1,0:T(8,128)S(1)} %get-tuple-element.177), channel_id=1, source_target_pairs={{0,3},{1,2},{2,1},{3,0},{4,7},{5,6},{6,5},{7,4},{8,11},{9,10},{10,... | collective-permute-start | bytes 98312 | tf_op jit(solution)/shard_map/ppermute | solution.py:336
  76.2 3.9 %collective-permute-start.29 = (f32[64,128]{1,0:T(8,128)S(1)}, f32[64,128]{1,0:T(8,128)S(1)}, u32[]{:S(2)}, u32[]{:S(2)}) collective-permute-start(f32[64,128]{1,0:T(8,128)S(1)} %get-tuple-element.177), channel_id=1, source_target_pairs={{0,2},{1,3},{2,0},{3,1},{4,6},{5,7},{6,4},{7,5},{8,10},{9,11},{10,... | collective-permute-start | bytes 98312 | tf_op jit(solution)/shard_map/ppermute | solution.py:336
  76.2 3.9 %collective-permute-start.28 = (f32[64,128]{1,0:T(8,128)S(1)}, f32[64,128]{1,0:T(8,128)S(1)}, u32[]{:S(2)}, u32[]{:S(2)}) collective-permute-start(f32[64,128]{1,0:T(8,128)S(1)} %get-tuple-element.177), channel_id=1, source_target_pairs={{0,1},{1,0},{2,3},{3,2},{4,5},{5,4},{6,7},{7,6},{8,9},{9,8},{10,11... | collective-permute-start | bytes 98312 | tf_op jit(solution)/shard_map/ppermute | solution.py:336
  84.4 9.5 %collective-permute-start.31 = (bf16[272,256]{1,0:T(8,128)(2,1)S(1)}, bf16[272,256]{1,0:T(8,128)(2,1)S(1)}, u32[]{:S(2)}, u32[]{:S(2)}) collective-permute-start(bf16[272,256]{1,0:T(8,128)(2,1)S(1)} %get-tuple-element.182), channel_id=1, source_target_pairs={{0,12},{4,8},{8,4},{12,0},{1,13},{5,9},{9,5},{13,1},{2,14},{6,10},... | collective-permute-start | bytes 417800 | tf_op jit(solution)/shard_map/ppermute | solution.py:336
  86.5 7.8 %collective-permute-start.32 = (bf16[272,256]{1,0:T(8,128)(2,1)S(1)}, bf16[272,256]{1,0:T(8,128)(2,1)S(1)}, u32[]{:S(2)}, u32[]{:S(2)}) collective-permute-start(bf16[272,256]{1,0:T(8,128)(2,1)S(1)} %get-tuple-element.183), channel_id=1, source_target_pairs={{0,8},{4,12},{8,0},{12,4},{1,9},{5,13},{9,1},{13,5},{2,10},{6,14},... | collective-permute-start | bytes 417800 | tf_op jit(solution)/shard_map/ppermute | solution.py:336
  86.7 7.6 %collective-permute-start.33 = (bf16[272,256]{1,0:T(8,128)(2,1)S(1)}, bf16[272,256]{1,0:T(8,128)(2,1)S(1)}, u32[]{:S(2)}, u32[]{:S(2)}) collective-permute-start(bf16[272,256]{1,0:T(8,128)(2,1)S(1)} %get-tuple-element.184), channel_id=1, source_target_pairs={{0,4},{4,0},{8,12},{12,8},{1,5},{5,1},{9,13},{13,9},{2,6},{6,2},{1... | collective-permute-start | bytes 417800 | tf_op jit(solution)/shard_map/ppermute | solution.py:336
  89.8 10.4 %collective-permute-start.37 = (bf16[2304,256]{1,0:T(8,128)(2,1)S(1)}, bf16[2304,256]{1,0:T(8,128)(2,1)S(1)}, u32[]{:S(2)}, u32[]{:S(2)}) collective-permute-start(bf16[2304,256]{1,0:T(8,128)(2,1)S(1)} %turn1.1.refs_4_.refs_7_.refs_1_), channel_id=1, source_target_pairs={{0,16},{16,0},{1,17},{17,1},{2,18},{18,2},{3,19},{19,3},{4,20},{20... | collective-permute-start | bytes 3538952 | tf_op jit(solution)/shard_map/ppermute | solution.py:279
  90.5 9.7 %collective-permute-start.38 = (bf16[256,1280]{1,0:T(8,128)(2,1)S(1)}, bf16[256,1280]{1,0:T(8,128)(2,1)S(1)}, u32[]{:S(2)}, u32[]{:S(2)}) collective-permute-start(bf16[256,1280]{1,0:T(8,128)(2,1)S(1)} %get-tuple-element.194), channel_id=1, source_target_pairs={{0,16},{16,0},{1,17},{17,1},{2,18},{18,2},{3,19},{19,3},{4,20},{20... | collective-permute-start | bytes 1966088 | tf_op jit(solution)/shard_map/ppermute | solution.py:279
  95.7 10.8 %collective-permute-start.36 = (bf16[256,256]{1,0:T(8,128)(2,1)S(1)}, bf16[256,256]{1,0:T(8,128)(2,1)S(1)}, u32[]{:S(2)}, u32[]{:S(2)}) collective-permute-start(bf16[256,256]{1,0:T(8,128)(2,1)S(1)} %get-tuple-element.192.refs_5_.refs_1_), channel_id=1, source_target_pairs={{0,12},{4,8},{8,4},{12,0},{1,13},{5,9},{9,5},{13,1},{2,14},{6,10},... | collective-permute-start | bytes 393224 | tf_op jit(solution)/shard_map/ppermute | solution.py:336
  97.8 11.1 %collective-permute-start.35 = (bf16[256,256]{1,0:T(8,128)(2,1)S(1)}, bf16[256,256]{1,0:T(8,128)(2,1)S(1)}, u32[]{:S(2)}, u32[]{:S(2)}) collective-permute-start(bf16[256,256]{1,0:T(8,128)(2,1)S(1)} %get-tuple-element.192.refs_5_.refs_1_), channel_id=1, source_target_pairs={{0,8},{4,12},{8,0},{12,4},{1,9},{5,13},{9,1},{13,5},{2,10},{6,14},... | collective-permute-start | bytes 393224 | tf_op jit(solution)/shard_map/ppermute | solution.py:336
  97.8 11.1 %collective-permute-start.34 = (bf16[256,256]{1,0:T(8,128)(2,1)S(1)}, bf16[256,256]{1,0:T(8,128)(2,1)S(1)}, u32[]{:S(2)}, u32[]{:S(2)}) collective-permute-start(bf16[256,256]{1,0:T(8,128)(2,1)S(1)} %get-tuple-element.192.refs_5_.refs_1_), channel_id=1, source_target_pairs={{0,4},{4,0},{8,12},{12,8},{1,5},{5,1},{9,13},{13,9},{2,6},{6,2},{1... | collective-permute-start | bytes 393224 | tf_op jit(solution)/shard_map/ppermute | solution.py:336
  103.4 13.0 %collective-permute-start.44 = (bf16[2,912,128]{2,1,0:T(8,128)(2,1)S(1)}, bf16[2,912,128]{2,1,0:T(8,128)(2,1)S(1)}, u32[]{:S(2)}, u32[]{:S(2)}) collective-permute-start(bf16[2,912,128]{2,1,0:T(8,128)(2,1)S(1)} %get-tuple-element.208), channel_id=1, source_target_pairs={{0,2},{1,3},{2,0},{3,1},{4,6},{5,7},{6,4},{7,5},{8,10},{9,11},{10,... | collective-permute-start | bytes 1400840 | tf_op jit(solution)/shard_map/ppermute | solution.py:336
  105.4 12.3 %collective-permute-start.43 = (bf16[2,1024,128]{2,1,0:T(8,128)(2,1)S(1)}, bf16[2,1024,128]{2,1,0:T(8,128)(2,1)S(1)}, u32[]{:S(2)}, u32[]{:S(2)}) collective-permute-start(bf16[2,1024,128]{2,1,0:T(8,128)(2,1)S(1)} %get-tuple-element.206), channel_id=1, source_target_pairs={{0,1},{1,0},{2,3},{3,2},{4,5},{5,4},{6,7},{7,6},{8,9},{9,8},{10,11... | collective-permute-start | bytes 1572872 | tf_op jit(solution)/shard_map/ppermute | solution.py:336
  111.3 8.4 %collective-permute-start.40 = (bf16[256,128]{1,0:T(8,128)(2,1)S(1)}, bf16[256,128]{1,0:T(8,128)(2,1)S(1)}, u32[]{:S(2)}, u32[]{:S(2)}) collective-permute-start(bf16[256,128]{1,0:T(8,128)(2,1)S(1)} %get-tuple-element.203), channel_id=1, source_target_pairs={{0,12},{4,8},{8,4},{12,0},{1,13},{5,9},{9,5},{13,1},{2,14},{6,10},... | collective-permute-start | bytes 196616 | tf_op jit(solution)/shard_map/ppermute | solution.py:336
  113.2 7.2 %collective-permute-start.41 = (bf16[256,128]{1,0:T(8,128)(2,1)S(1)}, bf16[256,128]{1,0:T(8,128)(2,1)S(1)}, u32[]{:S(2)}, u32[]{:S(2)}) collective-permute-start(bf16[256,128]{1,0:T(8,128)(2,1)S(1)} %get-tuple-element.204), channel_id=1, source_target_pairs={{0,8},{4,12},{8,0},{12,4},{1,9},{5,13},{9,1},{13,5},{2,10},{6,14},... | collective-permute-start | bytes 196616 | tf_op jit(solution)/shard_map/ppermute | solution.py:336
  113.2 7.2 %collective-permute-start.42 = (bf16[256,128]{1,0:T(8,128)(2,1)S(1)}, bf16[256,128]{1,0:T(8,128)(2,1)S(1)}, u32[]{:S(2)}, u32[]{:S(2)}) collective-permute-start(bf16[256,128]{1,0:T(8,128)(2,1)S(1)} %get-tuple-element.205), channel_id=1, source_target_pairs={{0,4},{4,0},{8,12},{12,8},{1,5},{5,1},{9,13},{13,9},{2,6},{6,2},{1... | collective-permute-start | bytes 196616 | tf_op jit(solution)/shard_map/ppermute | solution.py:336
  116.4 7.9 %collective-permute-start.39 = (bf16[256,1280]{1,0:T(8,128)(2,1)S(1)}, bf16[256,1280]{1,0:T(8,128)(2,1)S(1)}, u32[]{:S(2)}, u32[]{:S(2)}) collective-permute-start(bf16[256,1280]{1,0:T(8,128)(2,1)S(1)} %get-tuple-element.201), channel_id=1, source_target_pairs={{0,16},{16,0},{1,17},{17,1},{2,18},{18,2},{3,19},{19,3},{4,20},{20... | collective-permute-start | bytes 1966088 | tf_op jit(solution)/shard_map/ppermute | solution.py:279
  118.5 12.7 %collective-permute-start.48 = (bf16[1,912,128]{2,1,0:T(8,128)(2,1)S(1)}, bf16[1,912,128]{2,1,0:T(8,128)(2,1)S(1)}, u32[]{:S(2)}, u32[]{:S(2)}) collective-permute-start(bf16[1,912,128]{2,1,0:T(8,128)(2,1)S(1)} %get-tuple-element.217), channel_id=1, source_target_pairs={{0,1},{1,0},{2,3},{3,2},{4,5},{5,4},{6,7},{7,6},{8,9},{9,8},{10,11... | collective-permute-start | bytes 700424 | tf_op jit(solution)/shard_map/ppermute | solution.py:336
  119.7 11.4 %collective-permute-start.47 = (bf16[1,1024,128]{2,1,0:T(8,128)(2,1)S(1)}, bf16[1,1024,128]{2,1,0:T(8,128)(2,1)S(1)}, u32[]{:S(2)}, u32[]{:S(2)}) collective-permute-start(bf16[1,1024,128]{2,1,0:T(8,128)(2,1)S(1)} %get-tuple-element.215), channel_id=1, source_target_pairs={{0,2},{1,3},{2,0},{3,1},{4,6},{5,7},{6,4},{7,5},{8,10},{9,11},{10,... | collective-permute-start | bytes 786440 | tf_op jit(solution)/shard_map/ppermute | solution.py:336
  122.0 5.8 %collective-permute-start.51 = (f32[64,128]{1,0:T(8,128)S(1)}, f32[64,128]{1,0:T(8,128)S(1)}, u32[]{:S(2)}, u32[]{:S(2)}) collective-permute-start(f32[64,128]{1,0:T(8,128)S(1)} %get-tuple-element.210.refs_5_), channel_id=1, source_target_pairs={{0,3},{1,2},{2,1},{3,0},{4,7},{5,6},{6,5},{7,4},{8,11},{9,10},{10,... | collective-permute-start | bytes 98312 | tf_op jit(solution)/shard_map/ppermute | solution.py:336
  123.6 4.8 %collective-permute-start.50 = (f32[64,128]{1,0:T(8,128)S(1)}, f32[64,128]{1,0:T(8,128)S(1)}, u32[]{:S(2)}, u32[]{:S(2)}) collective-permute-start(f32[64,128]{1,0:T(8,128)S(1)} %get-tuple-element.210.refs_5_), channel_id=1, source_target_pairs={{0,2},{1,3},{2,0},{3,1},{4,6},{5,7},{6,4},{7,5},{8,10},{9,11},{10,... | collective-permute-start | bytes 98312 | tf_op jit(solution)/shard_map/ppermute | solution.py:336
  124.3 5.9 %collective-permute-start.49 = (f32[64,128]{1,0:T(8,128)S(1)}, f32[64,128]{1,0:T(8,128)S(1)}, u32[]{:S(2)}, u32[]{:S(2)}) collective-permute-start(f32[64,128]{1,0:T(8,128)S(1)} %get-tuple-element.210.refs_5_), channel_id=1, source_target_pairs={{0,1},{1,0},{2,3},{3,2},{4,5},{5,4},{6,7},{7,6},{8,9},{9,8},{10,11... | collective-permute-start | bytes 98312 | tf_op jit(solution)/shard_map/ppermute | solution.py:336
  127.8 11.4 %collective-permute-start.52 = (bf16[2,256,256]{2,1,0:T(8,128)(2,1)S(1)}, bf16[2,256,256]{2,1,0:T(8,128)(2,1)S(1)}, u32[]{:S(2)}, u32[]{:S(2)}) collective-permute-start(bf16[2,256,256]{2,1,0:T(8,128)(2,1)S(1)} %get-tuple-element.224), channel_id=1, source_target_pairs={{0,4},{4,0},{8,12},{12,8},{1,5},{5,1},{9,13},{13,9},{2,6},{6,2},{1... | collective-permute-start | bytes 786440 | tf_op jit(solution)/shard_map/ppermute | solution.py:336
  128.5 14.3 %collective-permute-start.46 = (bf16[2,912,128]{2,1,0:T(8,128)(2,1)S(1)}, bf16[2,912,128]{2,1,0:T(8,128)(2,1)S(1)}, u32[]{:S(2)}, u32[]{:S(2)}) collective-permute-start(bf16[2,912,128]{2,1,0:T(8,128)(2,1)S(1)} %get-tuple-element.214), channel_id=1, source_target_pairs={{0,2},{1,3},{2,0},{3,1},{4,6},{5,7},{6,4},{7,5},{8,10},{9,11},{10,... | collective-permute-start | bytes 1400840 | tf_op jit(solution)/shard_map/ppermute | solution.py:336
  130.2 12.9 %collective-permute-start.45 = (bf16[2,1024,128]{2,1,0:T(8,128)(2,1)S(1)}, bf16[2,1024,128]{2,1,0:T(8,128)(2,1)S(1)}, u32[]{:S(2)}, u32[]{:S(2)}) collective-permute-start(bf16[2,1024,128]{2,1,0:T(8,128)(2,1)S(1)} %get-tuple-element.212), channel_id=1, source_target_pairs={{0,1},{1,0},{2,3},{3,2},{4,5},{5,4},{6,7},{7,6},{8,9},{9,8},{10,11... | collective-permute-start | bytes 1572872 | tf_op jit(solution)/shard_map/ppermute | solution.py:336
  135.4 12.6 %collective-permute-start.56 = (bf16[272,256]{1,0:T(8,128)(2,1)S(1)}, bf16[272,256]{1,0:T(8,128)(2,1)S(1)}, u32[]{:S(2)}, u32[]{:S(2)}) collective-permute-start(bf16[272,256]{1,0:T(8,128)(2,1)S(1)} %get-tuple-element.234), channel_id=1, source_target_pairs={{0,12},{4,8},{8,4},{12,0},{1,13},{5,9},{9,5},{13,1},{2,14},{6,10},... | collective-permute-start | bytes 417800 | tf_op jit(solution)/shard_map/ppermute | solution.py:336
  137.3 11.9 %collective-permute-start.57 = (bf16[272,256]{1,0:T(8,128)(2,1)S(1)}, bf16[272,256]{1,0:T(8,128)(2,1)S(1)}, u32[]{:S(2)}, u32[]{:S(2)}) collective-permute-start(bf16[272,256]{1,0:T(8,128)(2,1)S(1)} %get-tuple-element.235), channel_id=1, source_target_pairs={{0,8},{4,12},{8,0},{12,4},{1,9},{5,13},{9,1},{13,5},{2,10},{6,14},... | collective-permute-start | bytes 417800 | tf_op jit(solution)/shard_map/ppermute | solution.py:336
  139.2 10.0 %collective-permute-start.58 = (bf16[272,256]{1,0:T(8,128)(2,1)S(1)}, bf16[272,256]{1,0:T(8,128)(2,1)S(1)}, u32[]{:S(2)}, u32[]{:S(2)}) collective-permute-start(bf16[272,256]{1,0:T(8,128)(2,1)S(1)} %get-tuple-element.236), channel_id=1, source_target_pairs={{0,4},{4,0},{8,12},{12,8},{1,5},{5,1},{9,13},{13,9},{2,6},{6,2},{1... | collective-permute-start | bytes 417800 | tf_op jit(solution)/shard_map/ppermute | solution.py:336
  143.9 11.1 %collective-permute-start.54 = (bf16[1,912,128]{2,1,0:T(8,128)(2,1)S(1)}, bf16[1,912,128]{2,1,0:T(8,128)(2,1)S(1)}, u32[]{:S(2)}, u32[]{:S(2)}) collective-permute-start(bf16[1,912,128]{2,1,0:T(8,128)(2,1)S(1)} %get-tuple-element.230), channel_id=1, source_target_pairs={{0,1},{1,0},{2,3},{3,2},{4,5},{5,4},{6,7},{7,6},{8,9},{9,8},{10,11... | collective-permute-start | bytes 700424 | tf_op jit(solution)/shard_map/ppermute | solution.py:336
  144.9 11.2 %collective-permute-start.53 = (bf16[1,1024,128]{2,1,0:T(8,128)(2,1)S(1)}, bf16[1,1024,128]{2,1,0:T(8,128)(2,1)S(1)}, u32[]{:S(2)}, u32[]{:S(2)}) collective-permute-start(bf16[1,1024,128]{2,1,0:T(8,128)(2,1)S(1)} %get-tuple-element.228), channel_id=1, source_target_pairs={{0,2},{1,3},{2,0},{3,1},{4,6},{5,7},{6,4},{7,5},{8,10},{9,11},{10,... | collective-permute-start | bytes 786440 | tf_op jit(solution)/shard_map/ppermute | solution.py:336
  148.1 3.8 %collective-permute-start.55 = (f32[640,256]{1,0:T(8,128)S(1)}, f32[640,256]{1,0:T(8,128)S(1)}, u32[]{:S(2)}, u32[]{:S(2)}) collective-permute-start(f32[640,256]{1,0:T(8,128)S(1)} %get-tuple-element.233), channel_id=1, source_target_pairs={{0,16},{16,0},{1,17},{17,1},{2,18},{18,2},{3,19},{19,3},{4,20},{20... | collective-permute-start | bytes 1966088 | tf_op jit(solution)/shard_map/ppermute | solution.py:279
  150.5 9.1 %collective-permute-start.64 = (bf16[1,256,256]{2,1,0:T(8,128)(2,1)S(1)}, bf16[1,256,256]{2,1,0:T(8,128)(2,1)S(1)}, u32[]{:S(2)}, u32[]{:S(2)}) collective-permute-start(bf16[1,256,256]{2,1,0:T(8,128)(2,1)S(1)} %get-tuple-element.250), channel_id=1, source_target_pairs={{0,8},{4,12},{8,0},{12,4},{1,9},{5,13},{9,1},{13,5},{2,10},{6,14},... | collective-permute-start | bytes 393224 | tf_op jit(solution)/shard_map/ppermute | solution.py:336
  152.5 7.8 %collective-permute-start.61 = (bf16[464,128]{1,0:T(8,128)(2,1)S(1)}, bf16[464,128]{1,0:T(8,128)(2,1)S(1)}, u32[]{:S(2)}, u32[]{:S(2)}) collective-permute-start(bf16[464,128]{1,0:T(8,128)(2,1)S(1)} %get-tuple-element.244), channel_id=1, source_target_pairs={{0,3},{1,2},{2,1},{3,0},{4,7},{5,6},{6,5},{7,4},{8,11},{9,10},{10,... | collective-permute-start | bytes 356360 | tf_op jit(solution)/shard_map/ppermute | solution.py:336
  154.0 7.3 %collective-permute-start.62 = (bf16[464,128]{1,0:T(8,128)(2,1)S(1)}, bf16[464,128]{1,0:T(8,128)(2,1)S(1)}, u32[]{:S(2)}, u32[]{:S(2)}) collective-permute-start(bf16[464,128]{1,0:T(8,128)(2,1)S(1)} %get-tuple-element.245), channel_id=1, source_target_pairs={{0,2},{1,3},{2,0},{3,1},{4,6},{5,7},{6,4},{7,5},{8,10},{9,11},{10,... | collective-permute-start | bytes 356360 | tf_op jit(solution)/shard_map/ppermute | solution.py:336
  155.1 6.2 %collective-permute-start.63 = (bf16[464,128]{1,0:T(8,128)(2,1)S(1)}, bf16[464,128]{1,0:T(8,128)(2,1)S(1)}, u32[]{:S(2)}, u32[]{:S(2)}) collective-permute-start(bf16[464,128]{1,0:T(8,128)(2,1)S(1)} %get-tuple-element.246), channel_id=1, source_target_pairs={{0,1},{1,0},{2,3},{3,2},{4,5},{5,4},{6,7},{7,6},{8,9},{9,8},{10,11... | collective-permute-start | bytes 356360 | tf_op jit(solution)/shard_map/ppermute | solution.py:336
  156.8 5.1 %collective-permute-start.60 = (bf16[1936,128]{1,0:T(8,128)(2,1)S(1)}, bf16[1936,128]{1,0:T(8,128)(2,1)S(1)}, u32[]{:S(2)}, u32[]{:S(2)}) collective-permute-start(bf16[1936,128]{1,0:T(8,128)(2,1)S(1)} %get-tuple-element.243), channel_id=1, source_target_pairs={{0,16},{16,0},{1,17},{17,1},{2,18},{18,2},{3,19},{19,3},{4,20},{20... | collective-permute-start | bytes 1486856 | tf_op jit(solution)/shard_map/ppermute | solution.py:279
  160.2 1.8 %collective-permute-start.65 = (f32[256,256]{1,0:T(8,128)S(1)}, f32[256,256]{1,0:T(8,128)S(1)}, u32[]{:S(2)}, u32[]{:S(2)}) collective-permute-start(f32[256,256]{1,0:T(8,128)S(1)} %layer_output1.1.refs_9_), channel_id=1, source_target_pairs={{0,16},{16,0},{1,17},{17,1},{2,18},{18,2},{3,19},{19,3},{4,20},{20... | collective-permute-start | bytes 786440 | tf_op jit(solution)/shard_map/ppermute | solution.py:279
  (24 other events, 102.8 us)

commit v3 on v2

--- a/solution.py
+++ b/solution.py
@@ -664,7 +664,7 @@
     def keep_or_give(meta, keep, give, first, second, by_layer=True):
         lower = meta[0] == 0
         keep[...] = jnp.where(lower, first, second)
-        give[0 : keep.shape[0], :] = jnp.where(lower, second, first).astype(give.dtype)
+        give[...] = jnp.where(lower, second, first)
 
     def layer_output(layer, before, parts, pack, after=()):
         def body(k):
@@ -957,8 +957,12 @@
             result[T : T + 1, :] = jnp.sum(total * standard[...], axis=0, keepdims=True)
             result[T + 1 : T + 2, :] = jnp.sum(total, axis=0, keepdims=True)
             if layer == 0:
-                keep_or_give(meta, keep, give, result[...], upper[...])
-                give[T + 8 :, :] = jnp.zeros((8, DC), BF16)
+                lower = meta[0] == 0
+                keep[...] = jnp.where(lower, result[...], upper[...])
+                give[0:T, :] = jnp.where(lower, upper[0:T, :], result[0:T, :]).astype(BF16)
+                sums = jnp.where(lower, upper[T:, :], result[T:, :])
+                sums = jnp.concatenate([sums, jnp.zeros((8, DC), F32)], axis=0)
+                give[T:, :] = sums.astype(BF16)
 
         return kernels[layer](
             f"layer_grad{layer}",

time: 165 us -> 165 us (level)
  no operation moved by 1% of the time
where the time goes in v3:
time: 165 us
  starting transfers between devices  68.7 us (42%)
  Pallas kernels  66 us (40%)
  waiting for transfers between devices  28.2 us (17%)
    pallas_call x44, Pallas kernels, __call__(): pl.pallas_call(run, out_shape=[jax.ShapeDtypeStruct(s, d) for s, d in out...  66 us
    ppermute x52, starting transfers between devices, paired(): return lax.ppermute(part, axis, [(i, i ^ s) for i in range(n)])  65.6 us
    ppermute x52, waiting for transfers between devices, paired(): return lax.ppermute(part, axis, [(i, i ^ s) for i in range(n)])  27.7 us
  transfers between devices with their start and end apart: 66, of which 20 were waited for; matrix products, arithmetic and copies ran while one was open for 0% of the time, Pallas kernels for 33%

profile of v3, /device:TPU:0, one launch (start us, length us, event | category | flops | bytes accessed | tf_op | source)
XLA Modules:
  0.0 164.7 jit_solution(14792601801099010365)
XLA Ops:
  0.7 2.4 %make_pack.1.refs_2_ = f32[64,640]{1,0:T(8,128)} custom-call(s32[2,3]{1,0:T(2,128)} %refs_0_.87, f32[64,128]{1,0:T(8,128)} %bitcast.25, f32[64,128]{1,0:T(8,128)} %bitcast.26, f32[64,128]{1,0:T(8,128)} %bitcast.27, f32[1,1024]{1,0:T(1,128)} %refs_4_.1, f32[1,1024]{1,0:T(1,128)} %refs_5_.1, f32[1,1024]{1,0:T(1,128)} %refs_6_.2, f32[1,768]{1,0:T(1,128)} %refs_7_.1, ...), custom_call_target="tpu_custom_call" | custom-call | flops 40000000000 | bytes 1 | tf_op jit(solution)/shard_map/make_pack/pallas_call | solution.py:108
  4.2 1.1 norm0.1
  5.3 2.0 %front0.1 = (bf16[256,1024]{1,0:T(8,128)(2,1)S(1)}, f32[256,128]{1,0:T(8,128)S(1)}, f32[256,128]{1,0:T(8,128)S(1)}, f32[64,128]{1,0:T(8,128)S(1)}, f32[64,640]{1...) custom-call(s32[2,3]{1,0:T(2,128)S(1)} %copy-done.8, ...), custom_call_target="tpu_custom_call" | custom-call | flops 40000000000 | bytes 1 | tf_op jit(solution)/shard_map/front0/pallas_call | solution.py:108
  7.4 3.5 %collective-permute-start.4 = (f32[64,128]{1,0:T(8,128)S(1)}, f32[64,128]{1,0:T(8,128)S(1)}, u32[]{:S(2)}, u32[]{:S(2)}) collective-permute-start(f32[64,128]{1,0:T(8,128)S(1)} %get-tuple-element.146), channel_id=1, source_target_pairs={{0,3},{1,2},{2,1},{3,0},{4,7},{5,6},{6,5},{7,4},{8,11},{9,10},{10,... | collective-permute-start | bytes 98312 | tf_op jit(solution)/shard_map/ppermute | solution.py:336
  12.1 1.3 wide0.1
  13.4 1.5 collective-permute-done.3.refs_4_
  15.3 2.2 %carry0.1 = (f32[64,128]{1,0:T(8,128)S(1)}, bf16[256,128]{1,0:T(8,128)(2,1)S(1)}) custom-call(s32[2,3]{1,0:T(2,128)S(1)} %copy-done.8, f32[256,128]{1,0:T(8,128)S(1)} %get-tuple-element.144.refs_1_, f32[64,640]{1,0:T(8,128)S(1)} %get-tuple-element.145.refs_2_.refs_6_.refs_1_.refs_3_.refs_4_, f32[64,128]{1,0:T(8,128)S(1)} %collective-permute-done.2.refs_3_, ...), custom_call_target="tpu_custom_call" | custom-call | flops 40000000000 | bytes 1 | tf_op jit(solution)/shard_map/carry0/pallas_call | solution.py:108
  17.5 3.7 %collective-permute-start.8 = (bf16[256,128]{1,0:T(8,128)(2,1)S(1)}, bf16[256,128]{1,0:T(8,128)(2,1)S(1)}, u32[]{:S(2)}, u32[]{:S(2)}) collective-permute-start(bf16[256,128]{1,0:T(8,128)(2,1)S(1)} %get-tuple-element.148.refs_5_.refs_1_), channel_id=1, source_target_pairs={{0,12},{4,8},{8,4},{12,0},{1,13},{5,9},{9,5},{13,1},{2,14},{6,10},... | collective-permute-start | bytes 196616 | tf_op jit(solution)/shard_map/ppermute | solution.py:336
  23.6 2.7 %collective-permute-done.7.refs_3_ = bf16[256,128]{1,0:T(8,128)(2,1)S(1)} collective-permute-done((bf16[256,128]{1,0:T(8,128)(2,1)S(1)}, bf16[256,128]{1,0:T(8,128)(2,1)S(1)}, u32[]{:S(2)}, u32[]{:S(2)}) %collective-permute-start.7) | collective-permute-done | bytes 65568 | tf_op jit(solution)/shard_map/ppermute | solution.py:336
  26.4 1.5 middle0.1
  27.9 2.2 %collective-permute-start.11 = (bf16[256,256]{1,0:T(8,128)(2,1)S(1)}, bf16[256,256]{1,0:T(8,128)(2,1)S(1)}, u32[]{:S(2)}, u32[]{:S(2)}) collective-permute-start(bf16[256,256]{1,0:T(8,128)(2,1)S(1)} %get-tuple-element.154), channel_id=1, source_target_pairs={{0,12},{4,8},{8,4},{12,0},{1,13},{5,9},{9,5},{13,1},{2,14},{6,10},... | collective-permute-start | bytes 393224 | tf_op jit(solution)/shard_map/ppermute | solution.py:336
  30.1 2.3 %collective-permute-start.13 = (bf16[256,256]{1,0:T(8,128)(2,1)S(1)}, bf16[256,256]{1,0:T(8,128)(2,1)S(1)}, u32[]{:S(2)}, u32[]{:S(2)}) collective-permute-start(bf16[256,256]{1,0:T(8,128)(2,1)S(1)} %get-tuple-element.156), channel_id=1, source_target_pairs={{0,4},{4,0},{8,12},{12,8},{1,5},{5,1},{9,13},{13,9},{2,6},{6,2},{1... | collective-permute-start | bytes 393224 | tf_op jit(solution)/shard_map/ppermute | solution.py:336
  33.6 1.2 grad_gated1.1
  34.8 1.4 collective-permute-done.11.refs_3_
  36.2 3.9 %collective-permute-done.12.refs_4_ = bf16[256,256]{1,0:T(8,128)(2,1)S(1)} collective-permute-done((bf16[256,256]{1,0:T(8,128)(2,1)S(1)}, bf16[256,256]{1,0:T(8,128)(2,1)S(1)}, u32[]{:S(2)}, u32[]{:S(2)}) %collective-permute-start.12) | collective-permute-done | bytes 131104 | tf_op jit(solution)/shard_map/ppermute | solution.py:336
  40.9 2.5 %collective-permute-start.15 = (bf16[256,256]{1,0:T(8,128)(2,1)S(1)}, bf16[256,256]{1,0:T(8,128)(2,1)S(1)}, u32[]{:S(2)}, u32[]{:S(2)}) collective-permute-start(bf16[256,256]{1,0:T(8,128)(2,1)S(1)} %get-tuple-element.159.refs_4_.refs_1_), channel_id=1, source_target_pairs={{0,4},{4,0},{8,12},{12,8},{1,5},{5,1},{9,13},{13,9},{2,6},{6,2},{1... | collective-permute-start | bytes 393224 | tf_op jit(solution)/shard_map/ppermute | solution.py:336
  43.4 4.4 %collective-permute-done.16.refs_3_ = bf16[256,256]{1,0:T(8,128)(2,1)S(1)} collective-permute-done((bf16[256,256]{1,0:T(8,128)(2,1)S(1)}, bf16[256,256]{1,0:T(8,128)(2,1)S(1)}, u32[]{:S(2)}, u32[]{:S(2)}) %collective-permute-start.16) | collective-permute-done | bytes 131104 | tf_op jit(solution)/shard_map/ppermute | solution.py:336
  49.3 3.4 %collective-permute-done.17.refs_4_ = bf16[256,256]{1,0:T(8,128)(2,1)S(1)} collective-permute-done((bf16[256,256]{1,0:T(8,128)(2,1)S(1)}, bf16[256,256]{1,0:T(8,128)(2,1)S(1)}, u32[]{:S(2)}, u32[]{:S(2)}) %collective-permute-start.17) | collective-permute-done | bytes 131104 | tf_op jit(solution)/shard_map/ppermute | solution.py:336
  52.7 2.4 %front1.1 = (bf16[256,1024]{1,0:T(8,128)(2,1)S(1)}, f32[256,128]{1,0:T(8,128)S(1)}, f32[256,128]{1,0:T(8,128)S(1)}, f32[64,128]{1,0:T(8,128)S(1)}, f32[256,1024]{1,0:T(8,128)S(1)}, /*index=5*/f32[256,128]{1,0:T(8,128)S(1)}) custom-call(s32[2,3]{1,0:T(2,128)S(1)} %copy-done.8, bf16[256,256]{1,0:T(8,128)(2,1)S(1)} %get-tuple-element.159.refs_4_.refs_1_, ...), custom_call_target="tpu_custom_call" | custom-call | flops 40000000000 | bytes 1 | tf_op jit(solution)/shard_map/front1/pallas_call | solution.py:108
  55.2 2.9 %collective-permute-start.20 = (f32[64,128]{1,0:T(8,128)S(1)}, f32[64,128]{1,0:T(8,128)S(1)}, u32[]{:S(2)}, u32[]{:S(2)}) collective-permute-start(f32[64,128]{1,0:T(8,128)S(1)} %get-tuple-element.163.refs_6_), channel_id=1, source_target_pairs={{0,3},{1,2},{2,1},{3,0},{4,7},{5,6},{6,5},{7,4},{8,11},{9,10},{10,... | collective-permute-start | bytes 98312 | tf_op jit(solution)/shard_map/ppermute | solution.py:336
  58.7 2.0 %wide1.1 = (f32[256,768]{1,0:T(8,128)S(1)}, bf16[256,768]{1,0:T(8,128)(2,1)S(1)}, f32[256,128]{1,0:T(8,128)S(1)}, bf16[256,128]{1,0:T(8,128)(2,1)S(1)}, bf16[256...) custom-call(s32[2,3]{1,0:T(2,128)S(1)} %copy-done.8, bf16[256,1024]{1,0:T(8,128)(2,1)S(1)} %get-tuple-element.164.refs_1_, ...), custom_call_target="tpu_custom_call" | custom-call | flops 40000000000 | bytes 1 | tf_op jit(solution)/shard_map/wide1/pallas_call | solution.py:108
  60.7 2.2 %collective-permute-start.24 = (bf16[256,128]{1,0:T(8,128)(2,1)S(1)}, bf16[256,128]{1,0:T(8,128)(2,1)S(1)}, u32[]{:S(2)}, u32[]{:S(2)}) collective-permute-start(bf16[256,128]{1,0:T(8,128)(2,1)S(1)} %get-tuple-element.171), channel_id=1, source_target_pairs={{0,12},{4,8},{8,4},{12,0},{1,13},{5,9},{9,5},{13,1},{2,14},{6,10},... | collective-permute-start | bytes 196616 | tf_op jit(solution)/shard_map/ppermute | solution.py:336
  62.9 2.3 %collective-permute-start.26 = (bf16[256,128]{1,0:T(8,128)(2,1)S(1)}, bf16[256,128]{1,0:T(8,128)(2,1)S(1)}, u32[]{:S(2)}, u32[]{:S(2)}) collective-permute-start(bf16[256,128]{1,0:T(8,128)(2,1)S(1)} %get-tuple-element.173), channel_id=1, source_target_pairs={{0,4},{4,0},{8,12},{12,8},{1,5},{5,1},{9,13},{13,9},{2,6},{6,2},{1... | collective-permute-start | bytes 196616 | tf_op jit(solution)/shard_map/ppermute | solution.py:336
  65.2 2.2 %carry1.1 = (f32[64,128]{1,0:T(8,128)S(1)}, bf16[256,128]{1,0:T(8,128)(2,1)S(1)}) custom-call(s32[2,3]{1,0:T(2,128)S(1)} %copy-done.8, f32[256,128]{1,0:T(8,128)S(1)} %get-tuple-element.162.refs_1_, f32[64,640]{1,0:T(8,128)S(1)} %get-tuple-element.160.refs_5_.refs_3_.refs_2_.refs_7_.refs_1_.refs_4_.refs_6_, f32[64,128]{1,0:T(8,128)S(1)} %collective-permute-done.18.refs_3_, ...), custom_call_target="tpu_custom_call" | custom-call | flops 40000000000 | bytes 1 | tf_op jit(solution)/shard_map/carry1/pallas_call | solution.py:108
  67.4 2.2 %collective-permute-start.23 = (bf16[256,128]{1,0:T(8,128)(2,1)S(1)}, bf16[256,128]{1,0:T(8,128)(2,1)S(1)}, u32[]{:S(2)}, u32[]{:S(2)}) collective-permute-start(bf16[256,128]{1,0:T(8,128)(2,1)S(1)} %get-tuple-element.168.refs_1_.refs_6_), channel_id=1, source_target_pairs={{0,12},{4,8},{8,4},{12,0},{1,13},{5,9},{9,5},{13,1},{2,14},{6,10},... | collective-permute-start | bytes 196616 | tf_op jit(solution)/shard_map/ppermute | solution.py:336
  70.5 1.4 collective-permute-start.21
  71.9 1.6 adjoint_local1.1
  73.5 2.7 %collective-permute-start.30 = (f32[64,128]{1,0:T(8,128)S(1)}, f32[64,128]{1,0:T(8,128)S(1)}, u32[]{:S(2)}, u32[]{:S(2)}) collective-permute-start(f32[64,128]{1,0:T(8,128)S(1)} %get-tuple-element.177), channel_id=1, source_target_pairs={{0,3},{1,2},{2,1},{3,0},{4,7},{5,6},{6,5},{7,4},{8,11},{9,10},{10,... | collective-permute-start | bytes 98312 | tf_op jit(solution)/shard_map/ppermute | solution.py:336
  77.1 1.5 middle1.1
  78.5 1.5 states_before1.1.refs_7_.refs_2_
  80.2 2.4 %adjoint1.1 = (f32[64,128]{1,0:T(8,128)S(1)}, bf16[256,128]{1,0:T(8,128)(2,1)S(1)}) custom-call(s32[2,3]{1,0:T(2,128)S(1)} %copy-done.8, f32[256,128]{1,0:T(8,128)S(1)} %get-tuple-element.175.refs_1_.refs_3_, f32[256,128]{1,0:T(8,128)S(1)} %get-tuple-element.176.refs_2_, ...), custom_call_target="tpu_custom_call" | custom-call | flops 40000000000 | bytes 1 | tf_op jit(solution)/shard_map/adjoint1/pallas_call | solution.py:108
  82.6 1.9 %grad_normed1.1 = (f32[272,256]{1,0:T(8,128)S(1)}, bf16[272,256]{1,0:T(8,128)(2,1)S(1)}, bf16[272,256]{1,0:T(8,128)(2,1)S(1)}, bf16[272,256]{1,0:T(8,128)(2,1)S(1)}) custom-call(s32[2,3]{1,0:T(2,128)S(1)} %copy-done.8, bf16[256,768]{1,0:T(8,128)(2,1)S(1)} %get-tuple-element.170.refs_4_.refs_1_, bf16[256,128]{1,0:T(8,128)(2,1)S(1)} %get-tuple-element.179.refs_2_.refs_5_, ...), custom_call_target="tpu_custom_call" | custom-call | flops 40000000000 | bytes 1 | tf_op jit(solution)/shard_map/grad_normed1/pallas_call | solution.py:108
  84.5 2.1 %collective-permute-start.31 = (bf16[272,256]{1,0:T(8,128)(2,1)S(1)}, bf16[272,256]{1,0:T(8,128)(2,1)S(1)}, u32[]{:S(2)}, u32[]{:S(2)}) collective-permute-start(bf16[272,256]{1,0:T(8,128)(2,1)S(1)} %get-tuple-element.182), channel_id=1, source_target_pairs={{0,12},{4,8},{8,4},{12,0},{1,13},{5,9},{9,5},{13,1},{2,14},{6,10},... | collective-permute-start | bytes 417800 | tf_op jit(solution)/shard_map/ppermute | solution.py:336
  86.7 2.2 %collective-permute-start.33 = (bf16[272,256]{1,0:T(8,128)(2,1)S(1)}, bf16[272,256]{1,0:T(8,128)(2,1)S(1)}, u32[]{:S(2)}, u32[]{:S(2)}) collective-permute-start(bf16[272,256]{1,0:T(8,128)(2,1)S(1)} %get-tuple-element.184), channel_id=1, source_target_pairs={{0,4},{4,0},{8,12},{12,8},{1,5},{5,1},{9,13},{13,9},{2,6},{6,2},{1... | collective-permute-start | bytes 417800 | tf_op jit(solution)/shard_map/ppermute | solution.py:336
  91.1 2.8 %ssm_grads1.1.refs_9_.refs_7_ = f32[640,256]{1,0:T(8,128)S(1)} custom-call(s32[2,3]{1,0:T(2,128)S(1)} %copy-done.8, f32[256,128]{1,0:T(8,128)S(1)} %get-tuple-element.162.refs_1_, f32[256,64,128]{2,1,0:T(8,128)S(1)} %states_before1.1.refs_7_.refs_2_, f32[256,128]{1,0:T(8,128)S(1)} %get-tuple-element.175.refs_1_.refs_3_, ...), custom_call_target="tpu_custom_call" | custom-call | flops 1 | bytes 1 | tf_op jit(solution)/shard_map/ssm_grads1/pallas_call | solution.py:108
  94.3 1.4 layer_grad1.1
  95.8 2.1 %collective-permute-start.36 = (bf16[256,256]{1,0:T(8,128)(2,1)S(1)}, bf16[256,256]{1,0:T(8,128)(2,1)S(1)}, u32[]{:S(2)}, u32[]{:S(2)}) collective-permute-start(bf16[256,256]{1,0:T(8,128)(2,1)S(1)} %get-tuple-element.192.refs_5_.refs_1_), channel_id=1, source_target_pairs={{0,12},{4,8},{8,4},{12,0},{1,13},{5,9},{9,5},{13,1},{2,14},{6,10},... | collective-permute-start | bytes 393224 | tf_op jit(solution)/shard_map/ppermute | solution.py:336
  97.8 2.4 %collective-permute-start.34 = (bf16[256,256]{1,0:T(8,128)(2,1)S(1)}, bf16[256,256]{1,0:T(8,128)(2,1)S(1)}, u32[]{:S(2)}, u32[]{:S(2)}) collective-permute-start(bf16[256,256]{1,0:T(8,128)(2,1)S(1)} %get-tuple-element.192.refs_5_.refs_1_), channel_id=1, source_target_pairs={{0,4},{4,0},{8,12},{12,8},{1,5},{5,1},{9,13},{13,9},{2,6},{6,2},{1... | collective-permute-start | bytes 393224 | tf_op jit(solution)/shard_map/ppermute | solution.py:336
  100.2 2.0 %weight_grads1.1 = (bf16[2,1024,128]{2,1,0:T(8,128)(2,1)S(1)}, bf16[2,1024,128]{2,1,0:T(8,128)(2,1)S(1)}, bf16[2,912,128]{2,1,0:T(8,128)(2,1)S(1)}, bf16[2,912,128]{2,1,0:T(8,128)(2,1)S(1)}) custom-call(s32[2,3]{1,0:T(2,128)S(1)} %copy-done.8, bf16[2304,256]{1,0:T(8,128)(2,1)S(1)} %turn1.1.refs_4_.refs_7_.refs_1_, ...), custom_call_target="tpu_custom_call" | custom-call | flops 1 | bytes 1 | tf_op jit(solution)/shard_map/weight_grads1/pallas_call | solution.py:108
  102.3 1.2 top_parts.1
  103.4 1.9 %collective-permute-start.44 = (bf16[2,912,128]{2,1,0:T(8,128)(2,1)S(1)}, bf16[2,912,128]{2,1,0:T(8,128)(2,1)S(1)}, u32[]{:S(2)}, u32[]{:S(2)}) collective-permute-start(bf16[2,912,128]{2,1,0:T(8,128)(2,1)S(1)} %get-tuple-element.208), channel_id=1, source_target_pairs={{0,2},{1,3},{2,0},{3,1},{4,6},{5,7},{6,4},{7,5},{8,10},{9,11},{10,... | collective-permute-start | bytes 1400840 | tf_op jit(solution)/shard_map/ppermute | solution.py:336
  105.4 1.1 collective-permute-start.43
  106.5 2.4 %collective-permute-done.35.refs_3_ = bf16[256,256]{1,0:T(8,128)(2,1)S(1)} collective-permute-done((bf16[256,256]{1,0:T(8,128)(2,1)S(1)}, bf16[256,256]{1,0:T(8,128)(2,1)S(1)}, u32[]{:S(2)}, u32[]{:S(2)}) %collective-permute-start.35) | collective-permute-done | bytes 131104 | tf_op jit(solution)/shard_map/ppermute | solution.py:336
  108.9 2.4 %grad_middle0.1 = (bf16[256,768]{1,0:T(8,128)(2,1)S(1)}, bf16[256,768]{1,0:T(8,128)(2,1)S(1)}, bf16[256,1024]{1,0:T(8,128)(2,1)S(1)}, f32[256,128]{1,0:T(8,128)S...) custom-call(s32[2,3]{1,0:T(2,128)S(1)} %copy-done.8, ...), custom_call_target="tpu_custom_call" | custom-call | flops 40000000000 | bytes 1 | tf_op jit(solution)/shard_map/grad_middle0/pallas_call | solution.py:108
  111.3 1.9 %collective-permute-start.40 = (bf16[256,128]{1,0:T(8,128)(2,1)S(1)}, bf16[256,128]{1,0:T(8,128)(2,1)S(1)}, u32[]{:S(2)}, u32[]{:S(2)}) collective-permute-start(bf16[256,128]{1,0:T(8,128)(2,1)S(1)} %get-tuple-element.203), channel_id=1, source_target_pairs={{0,12},{4,8},{8,4},{12,0},{1,13},{5,9},{9,5},{13,1},{2,14},{6,10},... | collective-permute-start | bytes 196616 | tf_op jit(solution)/shard_map/ppermute | solution.py:336
  113.2 2.5 %collective-permute-start.42 = (bf16[256,128]{1,0:T(8,128)(2,1)S(1)}, bf16[256,128]{1,0:T(8,128)(2,1)S(1)}, u32[]{:S(2)}, u32[]{:S(2)}) collective-permute-start(bf16[256,128]{1,0:T(8,128)(2,1)S(1)} %get-tuple-element.205), channel_id=1, source_target_pairs={{0,4},{4,0},{8,12},{12,8},{1,5},{5,1},{9,13},{13,9},{2,6},{6,2},{1... | collective-permute-start | bytes 196616 | tf_op jit(solution)/shard_map/ppermute | solution.py:336
  116.5 1.2 collective-permute-done.43.refs_2_
  118.5 1.2 collective-permute-start.48
  120.4 1.6 adjoint_local0.1
  122.0 1.6 collective-permute-start.51
  124.3 1.3 collective-permute-start.49
  125.6 2.1 %weight_grads0.1 = (bf16[2,1024,128]{2,1,0:T(8,128)(2,1)S(1)}, bf16[2,1024,128]{2,1,0:T(8,128)(2,1)S(1)}, bf16[2,912,128]{2,1,0:T(8,128)(2,1)S(1)}, bf16[2,912,128]{2,1,0:T(8,128)(2,1)S(1)}) custom-call(s32[2,3]{1,0:T(2,128)S(1)} %copy-done.8, bf16[2304,256]{1,0:T(8,128)(2,1)S(1)} %copy-done.3, ...), custom_call_target="tpu_custom_call" | custom-call | flops 1 | bytes 1 | tf_op jit(solution)/shard_map/weight_grads0/pallas_call | solution.py:108
  128.5 1.7 %collective-permute-start.46 = (bf16[2,912,128]{2,1,0:T(8,128)(2,1)S(1)}, bf16[2,912,128]{2,1,0:T(8,128)(2,1)S(1)}, u32[]{:S(2)}, u32[]{:S(2)}) collective-permute-start(bf16[2,912,128]{2,1,0:T(8,128)(2,1)S(1)} %get-tuple-element.214), channel_id=1, source_target_pairs={{0,2},{1,3},{2,0},{3,1},{4,6},{5,7},{6,4},{7,5},{8,10},{9,11},{10,... | collective-permute-start | bytes 1400840 | tf_op jit(solution)/shard_map/ppermute | solution.py:336
  131.1 2.4 %adjoint0.1 = (f32[64,128]{1,0:T(8,128)S(1)}, bf16[256,128]{1,0:T(8,128)(2,1)S(1)}) custom-call(s32[2,3]{1,0:T(2,128)S(1)} %copy-done.8, f32[256,128]{1,0:T(8,128)S(1)} %get-tuple-element.218.refs_1_.refs_3_, f32[256,128]{1,0:T(8,128)S(1)} %get-tuple-element.219.refs_2_, f32[64,640]{1,0:T(8,128)S(1)} %get-tuple-element.145.refs_2_.refs_6_.refs_1_.refs_3_.refs_4_, ...), custom_call_target="tpu_custom_call" | custom-call | flops 40000000000 | bytes 1 | tf_op jit(solution)/shard_map/adjoint0/pallas_call | solution.py:108
  133.6 1.9 %grad_normed0.1 = (f32[272,256]{1,0:T(8,128)S(1)}, bf16[272,256]{1,0:T(8,128)(2,1)S(1)}, bf16[272,256]{1,0:T(8,128)(2,1)S(1)}, bf16[272,256]{1,0:T(8,128)(2,1)S(1)}) custom-call(s32[2,3]{1,0:T(2,128)S(1)} %copy-done.8, bf16[256,768]{1,0:T(8,128)(2,1)S(1)} %get-tuple-element.197.refs_1_, bf16[256,128]{1,0:T(8,128)(2,1)S(1)} %get-tuple-element.220.refs_2_.refs_5_, ...), custom_call_target="tpu_custom_call" | custom-call | flops 40000000000 | bytes 1 | tf_op jit(solution)/shard_map/grad_normed0/pallas_call | solution.py:108
  135.4 1.8 %collective-permute-start.56 = (bf16[272,256]{1,0:T(8,128)(2,1)S(1)}, bf16[272,256]{1,0:T(8,128)(2,1)S(1)}, u32[]{:S(2)}, u32[]{:S(2)}) collective-permute-start(bf16[272,256]{1,0:T(8,128)(2,1)S(1)} %get-tuple-element.234), channel_id=1, source_target_pairs={{0,12},{4,8},{8,4},{12,0},{1,13},{5,9},{9,5},{13,1},{2,14},{6,10},... | collective-permute-start | bytes 417800 | tf_op jit(solution)/shard_map/ppermute | solution.py:336
  137.7 1.5 states_before0.1.refs_7_.refs_2_
  139.2 2.3 %collective-permute-start.58 = (bf16[272,256]{1,0:T(8,128)(2,1)S(1)}, bf16[272,256]{1,0:T(8,128)(2,1)S(1)}, u32[]{:S(2)}, u32[]{:S(2)}) collective-permute-start(bf16[272,256]{1,0:T(8,128)(2,1)S(1)} %get-tuple-element.236), channel_id=1, source_target_pairs={{0,4},{4,0},{8,12},{12,8},{1,5},{5,1},{9,13},{13,9},{2,6},{6,2},{1... | collective-permute-start | bytes 417800 | tf_op jit(solution)/shard_map/ppermute | solution.py:336
  145.2 2.8 %ssm_grads0.1 = (f32[640,256]{1,0:T(8,128)S(1)}, f32[640,256]{1,0:T(8,128)S(1)}) custom-call(s32[2,3]{1,0:T(2,128)S(1)} %copy-done.8, f32[256,128]{1,0:T(8,128)S(1)} %copy-done.13, f32[256,64,128]{2,1,0:T(8,128)S(1)} %states_before0.1.refs_7_.refs_2_, f32[256,128]{1,0:T(8,128)S(1)} %get-tuple-element.218.refs_1_.refs_3_, ...), custom_call_target="tpu_custom_call" | custom-call | flops 40000000000 | bytes 1 | tf_op jit(solution)/shard_map/ssm_grads0/pallas_call | solution.py:108
  149.1 1.2 layer_grad0.1
  152.5 1.5 collective-permute-start.61
  154.0 1.1 collective-permute-start.62
  156.9 1.8 %own_columns.1 = (f32[1,256,768]{2,1,0:T(8,128)}, f32[1,128,768]{2,1,0:T(8,128)}, f32[1,192,1024]{2,1,0:T(8,128)}, f32[1,2,256,256]{3,2,1,0:T(8,128)}, f32[8,128]{1,0:T(8,128)S(1)}) custom-call(s32[2,3]{1,0:T(2,128)S(1)} %copy-done.8, bf16[272,256]{1,0:T(8,128)(2,1)S(1)} %collective-permute-done.59.refs_4_.refs_1_, ...), custom_call_target="tpu_custom_call" | custom-call | flops 1 | bytes 1 | tf_op jit(solution)/shard_map/own_columns/pallas_call | solution.py:108
  162.0 2.6 %finish.1 = (f32[1,256,768]{2,1,0:T(8,128)}, f32[1,128,768]{2,1,0:T(8,128)}, f32[1,192,1024]{2,1,0:T(8,128)}, f32[1,192]{1,0:T(1,128)}, f32[1,192]{1,0:T(1,128)}...) custom-call(s32[2,3]{1,0:T(2,128)S(1)} %copy-done.8, ...), custom_call_target="tpu_custom_call", output_to_operand_aliasing={{0}: (4, {}), {1}: (5, {}), {2}: (6, {})} | custom-call | flops 1 | bytes 1 | tf_op jit(solution)/shard_map/finish/pallas_call | solution.py:108
  (156 shorter events, 31.0 us)
Async XLA Ops:
  3.1 2.1 %collective-permute-start = (f32[64,640]{1,0:T(8,128)}, f32[64,640]{1,0:T(8,128)S(1)}, u32[]{:S(2)}, u32[]{:S(2)}) collective-permute-start(f32[64,640]{1,0:T(8,128)} %make_pack.1.refs_2_), channel_id=1, source_target_pairs={{0,16},{16,0},{1,17},{17,1},{2,18},{18,2},{3,19},{19,3},{4,20},{20... | collective-permute-start | bytes 491528 | tf_op jit(solution)/shard_map/ppermute | solution.py:279
  3.8 7.8 %collective-permute-start.5 = (bf16[1024,768]{1,0:T(8,128)(2,1)S(1)}, bf16[1024,768]{1,0:T(8,128)(2,1)S(1)}, u32[]{:S(2)}, u32[]{:S(2)}) collective-permute-start(bf16[1024,768]{1,0:T(8,128)(2,1)S(1)} %bitcast.13), channel_id=1, source_target_pairs={{0,16},{16,0},{1,17},{17,1},{2,18},{18,2},{3,19},{19,3},{4,20},{20... | collective-permute-start | bytes 4718600 | tf_op jit(solution)/shard_map/ppermute | solution.py:279
  7.4 6.0 %collective-permute-start.4 = (f32[64,128]{1,0:T(8,128)S(1)}, f32[64,128]{1,0:T(8,128)S(1)}, u32[]{:S(2)}, u32[]{:S(2)}) collective-permute-start(f32[64,128]{1,0:T(8,128)S(1)} %get-tuple-element.146), channel_id=1, source_target_pairs={{0,3},{1,2},{2,1},{3,0},{4,7},{5,6},{6,5},{7,4},{8,11},{9,10},{10,... | collective-permute-start | bytes 98312 | tf_op jit(solution)/shard_map/ppermute | solution.py:336
  10.9 3.9 %collective-permute-start.3 = (f32[64,128]{1,0:T(8,128)S(1)}, f32[64,128]{1,0:T(8,128)S(1)}, u32[]{:S(2)}, u32[]{:S(2)}) collective-permute-start(f32[64,128]{1,0:T(8,128)S(1)} %get-tuple-element.146), channel_id=1, source_target_pairs={{0,2},{1,3},{2,0},{3,1},{4,6},{5,7},{6,4},{7,5},{8,10},{9,11},{10,... | collective-permute-start | bytes 98312 | tf_op jit(solution)/shard_map/ppermute | solution.py:336
  11.3 3.9 %collective-permute-start.2 = (f32[64,128]{1,0:T(8,128)S(1)}, f32[64,128]{1,0:T(8,128)S(1)}, u32[]{:S(2)}, u32[]{:S(2)}) collective-permute-start(f32[64,128]{1,0:T(8,128)S(1)} %get-tuple-element.146), channel_id=1, source_target_pairs={{0,1},{1,0},{2,3},{3,2},{4,5},{5,4},{6,7},{7,6},{8,9},{9,8},{10,11... | collective-permute-start | bytes 98312 | tf_op jit(solution)/shard_map/ppermute | solution.py:336
  11.6 10.4 %collective-permute-start.9 = (bf16[512,768]{1,0:T(8,128)(2,1)S(1)}, bf16[512,768]{1,0:T(8,128)(2,1)S(1)}, u32[]{:S(2)}, u32[]{:S(2)}) collective-permute-start(bf16[512,768]{1,0:T(8,128)(2,1)S(1)} %bitcast.19), channel_id=1, source_target_pairs={{0,16},{16,0},{1,17},{17,1},{2,18},{18,2},{3,19},{19,3},{4,20},{20... | collective-permute-start | bytes 2359304 | tf_op jit(solution)/shard_map/ppermute | solution.py:279
  11.6 10.4 %collective-permute-start.10 = (bf16[768,1024]{1,0:T(8,128)(2,1)S(1)}, bf16[768,1024]{1,0:T(8,128)(2,1)S(1)}, u32[]{:S(2)}, u32[]{:S(2)}) collective-permute-start(bf16[768,1024]{1,0:T(8,128)(2,1)S(1)} %bitcast.16), channel_id=1, source_target_pairs={{0,16},{16,0},{1,17},{17,1},{2,18},{18,2},{3,19},{19,3},{4,20},{20... | collective-permute-start | bytes 4718600 | tf_op jit(solution)/shard_map/ppermute | solution.py:279
  17.5 6.1 %collective-permute-start.8 = (bf16[256,128]{1,0:T(8,128)(2,1)S(1)}, bf16[256,128]{1,0:T(8,128)(2,1)S(1)}, u32[]{:S(2)}, u32[]{:S(2)}) collective-permute-start(bf16[256,128]{1,0:T(8,128)(2,1)S(1)} %get-tuple-element.148.refs_5_.refs_1_), channel_id=1, source_target_pairs={{0,12},{4,8},{8,4},{12,0},{1,13},{5,9},{9,5},{13,1},{2,14},{6,10},... | collective-permute-start | bytes 196616 | tf_op jit(solution)/shard_map/ppermute | solution.py:336
  21.1 5.2 %collective-permute-start.7 = (bf16[256,128]{1,0:T(8,128)(2,1)S(1)}, bf16[256,128]{1,0:T(8,128)(2,1)S(1)}, u32[]{:S(2)}, u32[]{:S(2)}) collective-permute-start(bf16[256,128]{1,0:T(8,128)(2,1)S(1)} %get-tuple-element.148.refs_5_.refs_1_), channel_id=1, source_target_pairs={{0,8},{4,12},{8,0},{12,4},{1,9},{5,13},{9,1},{13,5},{2,10},{6,14},... | collective-permute-start | bytes 196616 | tf_op jit(solution)/shard_map/ppermute | solution.py:336
  21.1 5.2 %collective-permute-start.6 = (bf16[256,128]{1,0:T(8,128)(2,1)S(1)}, bf16[256,128]{1,0:T(8,128)(2,1)S(1)}, u32[]{:S(2)}, u32[]{:S(2)}) collective-permute-start(bf16[256,128]{1,0:T(8,128)(2,1)S(1)} %get-tuple-element.148.refs_5_.refs_1_), channel_id=1, source_target_pairs={{0,4},{4,0},{8,12},{12,8},{1,5},{5,1},{9,13},{13,9},{2,6},{6,2},{1... | collective-permute-start | bytes 196616 | tf_op jit(solution)/shard_map/ppermute | solution.py:336
  27.9 8.3 %collective-permute-start.11 = (bf16[256,256]{1,0:T(8,128)(2,1)S(1)}, bf16[256,256]{1,0:T(8,128)(2,1)S(1)}, u32[]{:S(2)}, u32[]{:S(2)}) collective-permute-start(bf16[256,256]{1,0:T(8,128)(2,1)S(1)} %get-tuple-element.154), channel_id=1, source_target_pairs={{0,12},{4,8},{8,4},{12,0},{1,13},{5,9},{9,5},{13,1},{2,14},{6,10},... | collective-permute-start | bytes 393224 | tf_op jit(solution)/shard_map/ppermute | solution.py:336
  30.1 10.1 %collective-permute-start.12 = (bf16[256,256]{1,0:T(8,128)(2,1)S(1)}, bf16[256,256]{1,0:T(8,128)(2,1)S(1)}, u32[]{:S(2)}, u32[]{:S(2)}) collective-permute-start(bf16[256,256]{1,0:T(8,128)(2,1)S(1)} %get-tuple-element.155), channel_id=1, source_target_pairs={{0,8},{4,12},{8,0},{12,4},{1,9},{5,13},{9,1},{13,5},{2,10},{6,14},... | collective-permute-start | bytes 393224 | tf_op jit(solution)/shard_map/ppermute | solution.py:336
  30.1 10.1 %collective-permute-start.13 = (bf16[256,256]{1,0:T(8,128)(2,1)S(1)}, bf16[256,256]{1,0:T(8,128)(2,1)S(1)}, u32[]{:S(2)}, u32[]{:S(2)}) collective-permute-start(bf16[256,256]{1,0:T(8,128)(2,1)S(1)} %get-tuple-element.156), channel_id=1, source_target_pairs={{0,4},{4,0},{8,12},{12,8},{1,5},{5,1},{9,13},{13,9},{2,6},{6,2},{1... | collective-permute-start | bytes 393224 | tf_op jit(solution)/shard_map/ppermute | solution.py:336
  40.8 6.9 %collective-permute-start.16 = (bf16[256,256]{1,0:T(8,128)(2,1)S(1)}, bf16[256,256]{1,0:T(8,128)(2,1)S(1)}, u32[]{:S(2)}, u32[]{:S(2)}) collective-permute-start(bf16[256,256]{1,0:T(8,128)(2,1)S(1)} %get-tuple-element.159.refs_4_.refs_1_), channel_id=1, source_target_pairs={{0,8},{4,12},{8,0},{12,4},{1,9},{5,13},{9,1},{13,5},{2,10},{6,14},... | collective-permute-start | bytes 393224 | tf_op jit(solution)/shard_map/ppermute | solution.py:336
  40.9 8.4 %collective-permute-start.15 = (bf16[256,256]{1,0:T(8,128)(2,1)S(1)}, bf16[256,256]{1,0:T(8,128)(2,1)S(1)}, u32[]{:S(2)}, u32[]{:S(2)}) collective-permute-start(bf16[256,256]{1,0:T(8,128)(2,1)S(1)} %get-tuple-element.159.refs_4_.refs_1_), channel_id=1, source_target_pairs={{0,4},{4,0},{8,12},{12,8},{1,5},{5,1},{9,13},{13,9},{2,6},{6,2},{1... | collective-permute-start | bytes 393224 | tf_op jit(solution)/shard_map/ppermute | solution.py:336
  47.7 5.0 %collective-permute-start.17 = (bf16[256,256]{1,0:T(8,128)(2,1)S(1)}, bf16[256,256]{1,0:T(8,128)(2,1)S(1)}, u32[]{:S(2)}, u32[]{:S(2)}) collective-permute-start(bf16[256,256]{1,0:T(8,128)(2,1)S(1)} %collective-permute-done.16.refs_3_), channel_id=1, source_target_pairs={{0,4},{4,0},{8,12},{12,8},{1,5},{5,1},{9,13},{13,9},{2,6},{6,2},{1... | collective-permute-start | bytes 393224 | tf_op jit(solution)/shard_map/ppermute | solution.py:336
  47.8 19.6 %collective-permute-start.27 = (f32[256,256]{1,0:T(8,128)S(1)}, f32[256,256]{1,0:T(8,128)S(1)}, u32[]{:S(2)}, u32[]{:S(2)}) collective-permute-start(f32[256,256]{1,0:T(8,128)S(1)} %get-tuple-element.174.refs_3_.refs_7_), channel_id=1, source_target_pairs={{0,16},{16,0},{1,17},{17,1},{2,18},{18,2},{3,19},{19,3},{4,20},{20... | collective-permute-start | bytes 786440 | tf_op jit(solution)/shard_map/ppermute | solution.py:279
  48.7 23.2 %collective-permute-start.14 = (bf16[2304,256]{1,0:T(8,128)(2,1)S(1)}, bf16[2304,256]{1,0:T(8,128)(2,1)S(1)}, u32[]{:S(2)}, u32[]{:S(2)}) collective-permute-start(bf16[2304,256]{1,0:T(8,128)(2,1)S(1)} %turn0.1.refs_7_.refs_1_.refs_8_), channel_id=1, source_target_pairs={{0,16},{16,0},{1,17},{17,1},{2,18},{18,2},{3,19},{19,3},{4,20},{20... | collective-permute-start | bytes 3538952 | tf_op jit(solution)/shard_map/ppermute | solution.py:279
  55.2 5.5 %collective-permute-start.20 = (f32[64,128]{1,0:T(8,128)S(1)}, f32[64,128]{1,0:T(8,128)S(1)}, u32[]{:S(2)}, u32[]{:S(2)}) collective-permute-start(f32[64,128]{1,0:T(8,128)S(1)} %get-tuple-element.163.refs_6_), channel_id=1, source_target_pairs={{0,3},{1,2},{2,1},{3,0},{4,7},{5,6},{6,5},{7,4},{8,11},{9,10},{10,... | collective-permute-start | bytes 98312 | tf_op jit(solution)/shard_map/ppermute | solution.py:336
  58.0 4.8 %collective-permute-start.19 = (f32[64,128]{1,0:T(8,128)S(1)}, f32[64,128]{1,0:T(8,128)S(1)}, u32[]{:S(2)}, u32[]{:S(2)}) collective-permute-start(f32[64,128]{1,0:T(8,128)S(1)} %get-tuple-element.163.refs_6_), channel_id=1, source_target_pairs={{0,2},{1,3},{2,0},{3,1},{4,6},{5,7},{6,4},{7,5},{8,10},{9,11},{10,... | collective-permute-start | bytes 98312 | tf_op jit(solution)/shard_map/ppermute | solution.py:336
  58.2 4.7 %collective-permute-start.18 = (f32[64,128]{1,0:T(8,128)S(1)}, f32[64,128]{1,0:T(8,128)S(1)}, u32[]{:S(2)}, u32[]{:S(2)}) collective-permute-start(f32[64,128]{1,0:T(8,128)S(1)} %get-tuple-element.163.refs_6_), channel_id=1, source_target_pairs={{0,1},{1,0},{2,3},{3,2},{4,5},{5,4},{6,7},{7,6},{8,9},{9,8},{10,11... | collective-permute-start | bytes 98312 | tf_op jit(solution)/shard_map/ppermute | solution.py:336
  60.7 8.9 %collective-permute-start.24 = (bf16[256,128]{1,0:T(8,128)(2,1)S(1)}, bf16[256,128]{1,0:T(8,128)(2,1)S(1)}, u32[]{:S(2)}, u32[]{:S(2)}) collective-permute-start(bf16[256,128]{1,0:T(8,128)(2,1)S(1)} %get-tuple-element.171), channel_id=1, source_target_pairs={{0,12},{4,8},{8,4},{12,0},{1,13},{5,9},{9,5},{13,1},{2,14},{6,10},... | collective-permute-start | bytes 196616 | tf_op jit(solution)/shard_map/ppermute | solution.py:336
  62.9 7.6 %collective-permute-start.25 = (bf16[256,128]{1,0:T(8,128)(2,1)S(1)}, bf16[256,128]{1,0:T(8,128)(2,1)S(1)}, u32[]{:S(2)}, u32[]{:S(2)}) collective-permute-start(bf16[256,128]{1,0:T(8,128)(2,1)S(1)} %get-tuple-element.172), channel_id=1, source_target_pairs={{0,8},{4,12},{8,0},{12,4},{1,9},{5,13},{9,1},{13,5},{2,10},{6,14},... | collective-permute-start | bytes 196616 | tf_op jit(solution)/shard_map/ppermute | solution.py:336
  62.9 9.0 %collective-permute-start.26 = (bf16[256,128]{1,0:T(8,128)(2,1)S(1)}, bf16[256,128]{1,0:T(8,128)(2,1)S(1)}, u32[]{:S(2)}, u32[]{:S(2)}) collective-permute-start(bf16[256,128]{1,0:T(8,128)(2,1)S(1)} %get-tuple-element.173), channel_id=1, source_target_pairs={{0,4},{4,0},{8,12},{12,8},{1,5},{5,1},{9,13},{13,9},{2,6},{6,2},{1... | collective-permute-start | bytes 196616 | tf_op jit(solution)/shard_map/ppermute | solution.py:336
  67.4 8.9 %collective-permute-start.23 = (bf16[256,128]{1,0:T(8,128)(2,1)S(1)}, bf16[256,128]{1,0:T(8,128)(2,1)S(1)}, u32[]{:S(2)}, u32[]{:S(2)}) collective-permute-start(bf16[256,128]{1,0:T(8,128)(2,1)S(1)} %get-tuple-element.168.refs_1_.refs_6_), channel_id=1, source_target_pairs={{0,12},{4,8},{8,4},{12,0},{1,13},{5,9},{9,5},{13,1},{2,14},{6,10},... | collective-permute-start | bytes 196616 | tf_op jit(solution)/shard_map/ppermute | solution.py:336
  69.6 7.5 %collective-permute-start.22 = (bf16[256,128]{1,0:T(8,128)(2,1)S(1)}, bf16[256,128]{1,0:T(8,128)(2,1)S(1)}, u32[]{:S(2)}, u32[]{:S(2)}) collective-permute-start(bf16[256,128]{1,0:T(8,128)(2,1)S(1)} %get-tuple-element.168.refs_1_.refs_6_), channel_id=1, source_target_pairs={{0,8},{4,12},{8,0},{12,4},{1,9},{5,13},{9,1},{13,5},{2,10},{6,14},... | collective-permute-start | bytes 196616 | tf_op jit(solution)/shard_map/ppermute | solution.py:336
  70.5 6.5 %collective-permute-start.21 = (bf16[256,128]{1,0:T(8,128)(2,1)S(1)}, bf16[256,128]{1,0:T(8,128)(2,1)S(1)}, u32[]{:S(2)}, u32[]{:S(2)}) collective-permute-start(bf16[256,128]{1,0:T(8,128)(2,1)S(1)} %get-tuple-element.168.refs_1_.refs_6_), channel_id=1, source_target_pairs={{0,4},{4,0},{8,12},{12,8},{1,5},{5,1},{9,13},{13,9},{2,6},{6,2},{1... | collective-permute-start | bytes 196616 | tf_op jit(solution)/shard_map/ppermute | solution.py:336
  73.5 6.6 %collective-permute-start.30 = (f32[64,128]{1,0:T(8,128)S(1)}, f32[64,128]{1,0:T(8,128)S(1)}, u32[]{:S(2)}, u32[]{:S(2)}) collective-permute-start(f32[64,128]{1,0:T(8,128)S(1)} %get-tuple-element.177), channel_id=1, source_target_pairs={{0,3},{1,2},{2,1},{3,0},{4,7},{5,6},{6,5},{7,4},{8,11},{9,10},{10,... | collective-permute-start | bytes 98312 | tf_op jit(solution)/shard_map/ppermute | solution.py:336
  76.2 3.9 %collective-permute-start.29 = (f32[64,128]{1,0:T(8,128)S(1)}, f32[64,128]{1,0:T(8,128)S(1)}, u32[]{:S(2)}, u32[]{:S(2)}) collective-permute-start(f32[64,128]{1,0:T(8,128)S(1)} %get-tuple-element.177), channel_id=1, source_target_pairs={{0,2},{1,3},{2,0},{3,1},{4,6},{5,7},{6,4},{7,5},{8,10},{9,11},{10,... | collective-permute-start | bytes 98312 | tf_op jit(solution)/shard_map/ppermute | solution.py:336
  76.3 3.9 %collective-permute-start.28 = (f32[64,128]{1,0:T(8,128)S(1)}, f32[64,128]{1,0:T(8,128)S(1)}, u32[]{:S(2)}, u32[]{:S(2)}) collective-permute-start(f32[64,128]{1,0:T(8,128)S(1)} %get-tuple-element.177), channel_id=1, source_target_pairs={{0,1},{1,0},{2,3},{3,2},{4,5},{5,4},{6,7},{7,6},{8,9},{9,8},{10,11... | collective-permute-start | bytes 98312 | tf_op jit(solution)/shard_map/ppermute | solution.py:336
  84.5 9.5 %collective-permute-start.31 = (bf16[272,256]{1,0:T(8,128)(2,1)S(1)}, bf16[272,256]{1,0:T(8,128)(2,1)S(1)}, u32[]{:S(2)}, u32[]{:S(2)}) collective-permute-start(bf16[272,256]{1,0:T(8,128)(2,1)S(1)} %get-tuple-element.182), channel_id=1, source_target_pairs={{0,12},{4,8},{8,4},{12,0},{1,13},{5,9},{9,5},{13,1},{2,14},{6,10},... | collective-permute-start | bytes 417800 | tf_op jit(solution)/shard_map/ppermute | solution.py:336
  86.5 7.8 %collective-permute-start.32 = (bf16[272,256]{1,0:T(8,128)(2,1)S(1)}, bf16[272,256]{1,0:T(8,128)(2,1)S(1)}, u32[]{:S(2)}, u32[]{:S(2)}) collective-permute-start(bf16[272,256]{1,0:T(8,128)(2,1)S(1)} %get-tuple-element.183), channel_id=1, source_target_pairs={{0,8},{4,12},{8,0},{12,4},{1,9},{5,13},{9,1},{13,5},{2,10},{6,14},... | collective-permute-start | bytes 417800 | tf_op jit(solution)/shard_map/ppermute | solution.py:336
  86.7 7.6 %collective-permute-start.33 = (bf16[272,256]{1,0:T(8,128)(2,1)S(1)}, bf16[272,256]{1,0:T(8,128)(2,1)S(1)}, u32[]{:S(2)}, u32[]{:S(2)}) collective-permute-start(bf16[272,256]{1,0:T(8,128)(2,1)S(1)} %get-tuple-element.184), channel_id=1, source_target_pairs={{0,4},{4,0},{8,12},{12,8},{1,5},{5,1},{9,13},{13,9},{2,6},{6,2},{1... | collective-permute-start | bytes 417800 | tf_op jit(solution)/shard_map/ppermute | solution.py:336
  89.8 10.4 %collective-permute-start.37 = (bf16[2304,256]{1,0:T(8,128)(2,1)S(1)}, bf16[2304,256]{1,0:T(8,128)(2,1)S(1)}, u32[]{:S(2)}, u32[]{:S(2)}) collective-permute-start(bf16[2304,256]{1,0:T(8,128)(2,1)S(1)} %turn1.1.refs_4_.refs_7_.refs_1_), channel_id=1, source_target_pairs={{0,16},{16,0},{1,17},{17,1},{2,18},{18,2},{3,19},{19,3},{4,20},{20... | collective-permute-start | bytes 3538952 | tf_op jit(solution)/shard_map/ppermute | solution.py:279
  90.6 9.7 %collective-permute-start.38 = (bf16[256,1280]{1,0:T(8,128)(2,1)S(1)}, bf16[256,1280]{1,0:T(8,128)(2,1)S(1)}, u32[]{:S(2)}, u32[]{:S(2)}) collective-permute-start(bf16[256,1280]{1,0:T(8,128)(2,1)S(1)} %get-tuple-element.194), channel_id=1, source_target_pairs={{0,16},{16,0},{1,17},{17,1},{2,18},{18,2},{3,19},{19,3},{4,20},{20... | collective-permute-start | bytes 1966088 | tf_op jit(solution)/shard_map/ppermute | solution.py:279
  95.8 10.8 %collective-permute-start.36 = (bf16[256,256]{1,0:T(8,128)(2,1)S(1)}, bf16[256,256]{1,0:T(8,128)(2,1)S(1)}, u32[]{:S(2)}, u32[]{:S(2)}) collective-permute-start(bf16[256,256]{1,0:T(8,128)(2,1)S(1)} %get-tuple-element.192.refs_5_.refs_1_), channel_id=1, source_target_pairs={{0,12},{4,8},{8,4},{12,0},{1,13},{5,9},{9,5},{13,1},{2,14},{6,10},... | collective-permute-start | bytes 393224 | tf_op jit(solution)/shard_map/ppermute | solution.py:336
  97.8 11.1 %collective-permute-start.35 = (bf16[256,256]{1,0:T(8,128)(2,1)S(1)}, bf16[256,256]{1,0:T(8,128)(2,1)S(1)}, u32[]{:S(2)}, u32[]{:S(2)}) collective-permute-start(bf16[256,256]{1,0:T(8,128)(2,1)S(1)} %get-tuple-element.192.refs_5_.refs_1_), channel_id=1, source_target_pairs={{0,8},{4,12},{8,0},{12,4},{1,9},{5,13},{9,1},{13,5},{2,10},{6,14},... | collective-permute-start | bytes 393224 | tf_op jit(solution)/shard_map/ppermute | solution.py:336
  97.8 11.1 %collective-permute-start.34 = (bf16[256,256]{1,0:T(8,128)(2,1)S(1)}, bf16[256,256]{1,0:T(8,128)(2,1)S(1)}, u32[]{:S(2)}, u32[]{:S(2)}) collective-permute-start(bf16[256,256]{1,0:T(8,128)(2,1)S(1)} %get-tuple-element.192.refs_5_.refs_1_), channel_id=1, source_target_pairs={{0,4},{4,0},{8,12},{12,8},{1,5},{5,1},{9,13},{13,9},{2,6},{6,2},{1... | collective-permute-start | bytes 393224 | tf_op jit(solution)/shard_map/ppermute | solution.py:336
  103.4 13.0 %collective-permute-start.44 = (bf16[2,912,128]{2,1,0:T(8,128)(2,1)S(1)}, bf16[2,912,128]{2,1,0:T(8,128)(2,1)S(1)}, u32[]{:S(2)}, u32[]{:S(2)}) collective-permute-start(bf16[2,912,128]{2,1,0:T(8,128)(2,1)S(1)} %get-tuple-element.208), channel_id=1, source_target_pairs={{0,2},{1,3},{2,0},{3,1},{4,6},{5,7},{6,4},{7,5},{8,10},{9,11},{10,... | collective-permute-start | bytes 1400840 | tf_op jit(solution)/shard_map/ppermute | solution.py:336
  105.4 12.3 %collective-permute-start.43 = (bf16[2,1024,128]{2,1,0:T(8,128)(2,1)S(1)}, bf16[2,1024,128]{2,1,0:T(8,128)(2,1)S(1)}, u32[]{:S(2)}, u32[]{:S(2)}) collective-permute-start(bf16[2,1024,128]{2,1,0:T(8,128)(2,1)S(1)} %get-tuple-element.206), channel_id=1, source_target_pairs={{0,1},{1,0},{2,3},{3,2},{4,5},{5,4},{6,7},{7,6},{8,9},{9,8},{10,11... | collective-permute-start | bytes 1572872 | tf_op jit(solution)/shard_map/ppermute | solution.py:336
  111.3 8.4 %collective-permute-start.40 = (bf16[256,128]{1,0:T(8,128)(2,1)S(1)}, bf16[256,128]{1,0:T(8,128)(2,1)S(1)}, u32[]{:S(2)}, u32[]{:S(2)}) collective-permute-start(bf16[256,128]{1,0:T(8,128)(2,1)S(1)} %get-tuple-element.203), channel_id=1, source_target_pairs={{0,12},{4,8},{8,4},{12,0},{1,13},{5,9},{9,5},{13,1},{2,14},{6,10},... | collective-permute-start | bytes 196616 | tf_op jit(solution)/shard_map/ppermute | solution.py:336
  113.2 7.2 %collective-permute-start.41 = (bf16[256,128]{1,0:T(8,128)(2,1)S(1)}, bf16[256,128]{1,0:T(8,128)(2,1)S(1)}, u32[]{:S(2)}, u32[]{:S(2)}) collective-permute-start(bf16[256,128]{1,0:T(8,128)(2,1)S(1)} %get-tuple-element.204), channel_id=1, source_target_pairs={{0,8},{4,12},{8,0},{12,4},{1,9},{5,13},{9,1},{13,5},{2,10},{6,14},... | collective-permute-start | bytes 196616 | tf_op jit(solution)/shard_map/ppermute | solution.py:336
  113.2 7.2 %collective-permute-start.42 = (bf16[256,128]{1,0:T(8,128)(2,1)S(1)}, bf16[256,128]{1,0:T(8,128)(2,1)S(1)}, u32[]{:S(2)}, u32[]{:S(2)}) collective-permute-start(bf16[256,128]{1,0:T(8,128)(2,1)S(1)} %get-tuple-element.205), channel_id=1, source_target_pairs={{0,4},{4,0},{8,12},{12,8},{1,5},{5,1},{9,13},{13,9},{2,6},{6,2},{1... | collective-permute-start | bytes 196616 | tf_op jit(solution)/shard_map/ppermute | solution.py:336
  116.4 7.9 %collective-permute-start.39 = (bf16[256,1280]{1,0:T(8,128)(2,1)S(1)}, bf16[256,1280]{1,0:T(8,128)(2,1)S(1)}, u32[]{:S(2)}, u32[]{:S(2)}) collective-permute-start(bf16[256,1280]{1,0:T(8,128)(2,1)S(1)} %get-tuple-element.201), channel_id=1, source_target_pairs={{0,16},{16,0},{1,17},{17,1},{2,18},{18,2},{3,19},{19,3},{4,20},{20... | collective-permute-start | bytes 1966088 | tf_op jit(solution)/shard_map/ppermute | solution.py:279
  118.5 12.7 %collective-permute-start.48 = (bf16[1,912,128]{2,1,0:T(8,128)(2,1)S(1)}, bf16[1,912,128]{2,1,0:T(8,128)(2,1)S(1)}, u32[]{:S(2)}, u32[]{:S(2)}) collective-permute-start(bf16[1,912,128]{2,1,0:T(8,128)(2,1)S(1)} %get-tuple-element.217), channel_id=1, source_target_pairs={{0,1},{1,0},{2,3},{3,2},{4,5},{5,4},{6,7},{7,6},{8,9},{9,8},{10,11... | collective-permute-start | bytes 700424 | tf_op jit(solution)/shard_map/ppermute | solution.py:336
  119.7 11.4 %collective-permute-start.47 = (bf16[1,1024,128]{2,1,0:T(8,128)(2,1)S(1)}, bf16[1,1024,128]{2,1,0:T(8,128)(2,1)S(1)}, u32[]{:S(2)}, u32[]{:S(2)}) collective-permute-start(bf16[1,1024,128]{2,1,0:T(8,128)(2,1)S(1)} %get-tuple-element.215), channel_id=1, source_target_pairs={{0,2},{1,3},{2,0},{3,1},{4,6},{5,7},{6,4},{7,5},{8,10},{9,11},{10,... | collective-permute-start | bytes 786440 | tf_op jit(solution)/shard_map/ppermute | solution.py:336
  122.0 5.8 %collective-permute-start.51 = (f32[64,128]{1,0:T(8,128)S(1)}, f32[64,128]{1,0:T(8,128)S(1)}, u32[]{:S(2)}, u32[]{:S(2)}) collective-permute-start(f32[64,128]{1,0:T(8,128)S(1)} %get-tuple-element.210.refs_5_), channel_id=1, source_target_pairs={{0,3},{1,2},{2,1},{3,0},{4,7},{5,6},{6,5},{7,4},{8,11},{9,10},{10,... | collective-permute-start | bytes 98312 | tf_op jit(solution)/shard_map/ppermute | solution.py:336
  123.6 4.8 %collective-permute-start.50 = (f32[64,128]{1,0:T(8,128)S(1)}, f32[64,128]{1,0:T(8,128)S(1)}, u32[]{:S(2)}, u32[]{:S(2)}) collective-permute-start(f32[64,128]{1,0:T(8,128)S(1)} %get-tuple-element.210.refs_5_), channel_id=1, source_target_pairs={{0,2},{1,3},{2,0},{3,1},{4,6},{5,7},{6,4},{7,5},{8,10},{9,11},{10,... | collective-permute-start | bytes 98312 | tf_op jit(solution)/shard_map/ppermute | solution.py:336
  124.3 5.9 %collective-permute-start.49 = (f32[64,128]{1,0:T(8,128)S(1)}, f32[64,128]{1,0:T(8,128)S(1)}, u32[]{:S(2)}, u32[]{:S(2)}) collective-permute-start(f32[64,128]{1,0:T(8,128)S(1)} %get-tuple-element.210.refs_5_), channel_id=1, source_target_pairs={{0,1},{1,0},{2,3},{3,2},{4,5},{5,4},{6,7},{7,6},{8,9},{9,8},{10,11... | collective-permute-start | bytes 98312 | tf_op jit(solution)/shard_map/ppermute | solution.py:336
  127.8 11.4 %collective-permute-start.52 = (bf16[2,256,256]{2,1,0:T(8,128)(2,1)S(1)}, bf16[2,256,256]{2,1,0:T(8,128)(2,1)S(1)}, u32[]{:S(2)}, u32[]{:S(2)}) collective-permute-start(bf16[2,256,256]{2,1,0:T(8,128)(2,1)S(1)} %get-tuple-element.224), channel_id=1, source_target_pairs={{0,4},{4,0},{8,12},{12,8},{1,5},{5,1},{9,13},{13,9},{2,6},{6,2},{1... | collective-permute-start | bytes 786440 | tf_op jit(solution)/shard_map/ppermute | solution.py:336
  128.5 14.3 %collective-permute-start.46 = (bf16[2,912,128]{2,1,0:T(8,128)(2,1)S(1)}, bf16[2,912,128]{2,1,0:T(8,128)(2,1)S(1)}, u32[]{:S(2)}, u32[]{:S(2)}) collective-permute-start(bf16[2,912,128]{2,1,0:T(8,128)(2,1)S(1)} %get-tuple-element.214), channel_id=1, source_target_pairs={{0,2},{1,3},{2,0},{3,1},{4,6},{5,7},{6,4},{7,5},{8,10},{9,11},{10,... | collective-permute-start | bytes 1400840 | tf_op jit(solution)/shard_map/ppermute | solution.py:336
  130.2 12.9 %collective-permute-start.45 = (bf16[2,1024,128]{2,1,0:T(8,128)(2,1)S(1)}, bf16[2,1024,128]{2,1,0:T(8,128)(2,1)S(1)}, u32[]{:S(2)}, u32[]{:S(2)}) collective-permute-start(bf16[2,1024,128]{2,1,0:T(8,128)(2,1)S(1)} %get-tuple-element.212), channel_id=1, source_target_pairs={{0,1},{1,0},{2,3},{3,2},{4,5},{5,4},{6,7},{7,6},{8,9},{9,8},{10,11... | collective-permute-start | bytes 1572872 | tf_op jit(solution)/shard_map/ppermute | solution.py:336
  135.4 12.6 %collective-permute-start.56 = (bf16[272,256]{1,0:T(8,128)(2,1)S(1)}, bf16[272,256]{1,0:T(8,128)(2,1)S(1)}, u32[]{:S(2)}, u32[]{:S(2)}) collective-permute-start(bf16[272,256]{1,0:T(8,128)(2,1)S(1)} %get-tuple-element.234), channel_id=1, source_target_pairs={{0,12},{4,8},{8,4},{12,0},{1,13},{5,9},{9,5},{13,1},{2,14},{6,10},... | collective-permute-start | bytes 417800 | tf_op jit(solution)/shard_map/ppermute | solution.py:336
  137.3 11.9 %collective-permute-start.57 = (bf16[272,256]{1,0:T(8,128)(2,1)S(1)}, bf16[272,256]{1,0:T(8,128)(2,1)S(1)}, u32[]{:S(2)}, u32[]{:S(2)}) collective-permute-start(bf16[272,256]{1,0:T(8,128)(2,1)S(1)} %get-tuple-element.235), channel_id=1, source_target_pairs={{0,8},{4,12},{8,0},{12,4},{1,9},{5,13},{9,1},{13,5},{2,10},{6,14},... | collective-permute-start | bytes 417800 | tf_op jit(solution)/shard_map/ppermute | solution.py:336
  139.2 10.0 %collective-permute-start.58 = (bf16[272,256]{1,0:T(8,128)(2,1)S(1)}, bf16[272,256]{1,0:T(8,128)(2,1)S(1)}, u32[]{:S(2)}, u32[]{:S(2)}) collective-permute-start(bf16[272,256]{1,0:T(8,128)(2,1)S(1)} %get-tuple-element.236), channel_id=1, source_target_pairs={{0,4},{4,0},{8,12},{12,8},{1,5},{5,1},{9,13},{13,9},{2,6},{6,2},{1... | collective-permute-start | bytes 417800 | tf_op jit(solution)/shard_map/ppermute | solution.py:336
  143.9 11.1 %collective-permute-start.54 = (bf16[1,912,128]{2,1,0:T(8,128)(2,1)S(1)}, bf16[1,912,128]{2,1,0:T(8,128)(2,1)S(1)}, u32[]{:S(2)}, u32[]{:S(2)}) collective-permute-start(bf16[1,912,128]{2,1,0:T(8,128)(2,1)S(1)} %get-tuple-element.230), channel_id=1, source_target_pairs={{0,1},{1,0},{2,3},{3,2},{4,5},{5,4},{6,7},{7,6},{8,9},{9,8},{10,11... | collective-permute-start | bytes 700424 | tf_op jit(solution)/shard_map/ppermute | solution.py:336
  144.9 11.2 %collective-permute-start.53 = (bf16[1,1024,128]{2,1,0:T(8,128)(2,1)S(1)}, bf16[1,1024,128]{2,1,0:T(8,128)(2,1)S(1)}, u32[]{:S(2)}, u32[]{:S(2)}) collective-permute-start(bf16[1,1024,128]{2,1,0:T(8,128)(2,1)S(1)} %get-tuple-element.228), channel_id=1, source_target_pairs={{0,2},{1,3},{2,0},{3,1},{4,6},{5,7},{6,4},{7,5},{8,10},{9,11},{10,... | collective-permute-start | bytes 786440 | tf_op jit(solution)/shard_map/ppermute | solution.py:336
  148.1 3.8 %collective-permute-start.55 = (f32[640,256]{1,0:T(8,128)S(1)}, f32[640,256]{1,0:T(8,128)S(1)}, u32[]{:S(2)}, u32[]{:S(2)}) collective-permute-start(f32[640,256]{1,0:T(8,128)S(1)} %get-tuple-element.233), channel_id=1, source_target_pairs={{0,16},{16,0},{1,17},{17,1},{2,18},{18,2},{3,19},{19,3},{4,20},{20... | collective-permute-start | bytes 1966088 | tf_op jit(solution)/shard_map/ppermute | solution.py:279
  150.5 9.1 %collective-permute-start.64 = (bf16[1,256,256]{2,1,0:T(8,128)(2,1)S(1)}, bf16[1,256,256]{2,1,0:T(8,128)(2,1)S(1)}, u32[]{:S(2)}, u32[]{:S(2)}) collective-permute-start(bf16[1,256,256]{2,1,0:T(8,128)(2,1)S(1)} %get-tuple-element.250), channel_id=1, source_target_pairs={{0,8},{4,12},{8,0},{12,4},{1,9},{5,13},{9,1},{13,5},{2,10},{6,14},... | collective-permute-start | bytes 393224 | tf_op jit(solution)/shard_map/ppermute | solution.py:336
  152.5 7.8 %collective-permute-start.61 = (bf16[464,128]{1,0:T(8,128)(2,1)S(1)}, bf16[464,128]{1,0:T(8,128)(2,1)S(1)}, u32[]{:S(2)}, u32[]{:S(2)}) collective-permute-start(bf16[464,128]{1,0:T(8,128)(2,1)S(1)} %get-tuple-element.244), channel_id=1, source_target_pairs={{0,3},{1,2},{2,1},{3,0},{4,7},{5,6},{6,5},{7,4},{8,11},{9,10},{10,... | collective-permute-start | bytes 356360 | tf_op jit(solution)/shard_map/ppermute | solution.py:336
  154.0 7.3 %collective-permute-start.62 = (bf16[464,128]{1,0:T(8,128)(2,1)S(1)}, bf16[464,128]{1,0:T(8,128)(2,1)S(1)}, u32[]{:S(2)}, u32[]{:S(2)}) collective-permute-start(bf16[464,128]{1,0:T(8,128)(2,1)S(1)} %get-tuple-element.245), channel_id=1, source_target_pairs={{0,2},{1,3},{2,0},{3,1},{4,6},{5,7},{6,4},{7,5},{8,10},{9,11},{10,... | collective-permute-start | bytes 356360 | tf_op jit(solution)/shard_map/ppermute | solution.py:336
  155.1 6.2 %collective-permute-start.63 = (bf16[464,128]{1,0:T(8,128)(2,1)S(1)}, bf16[464,128]{1,0:T(8,128)(2,1)S(1)}, u32[]{:S(2)}, u32[]{:S(2)}) collective-permute-start(bf16[464,128]{1,0:T(8,128)(2,1)S(1)} %get-tuple-element.246), channel_id=1, source_target_pairs={{0,1},{1,0},{2,3},{3,2},{4,5},{5,4},{6,7},{7,6},{8,9},{9,8},{10,11... | collective-permute-start | bytes 356360 | tf_op jit(solution)/shard_map/ppermute | solution.py:336
  156.8 5.1 %collective-permute-start.60 = (bf16[1936,128]{1,0:T(8,128)(2,1)S(1)}, bf16[1936,128]{1,0:T(8,128)(2,1)S(1)}, u32[]{:S(2)}, u32[]{:S(2)}) collective-permute-start(bf16[1936,128]{1,0:T(8,128)(2,1)S(1)} %get-tuple-element.243), channel_id=1, source_target_pairs={{0,16},{16,0},{1,17},{17,1},{2,18},{18,2},{3,19},{19,3},{4,20},{20... | collective-permute-start | bytes 1486856 | tf_op jit(solution)/shard_map/ppermute | solution.py:279
  160.2 1.8 %collective-permute-start.65 = (f32[256,256]{1,0:T(8,128)S(1)}, f32[256,256]{1,0:T(8,128)S(1)}, u32[]{:S(2)}, u32[]{:S(2)}) collective-permute-start(f32[256,256]{1,0:T(8,128)S(1)} %layer_output1.1.refs_9_), channel_id=1, source_target_pairs={{0,16},{16,0},{1,17},{17,1},{2,18},{18,2},{3,19},{19,3},{4,20},{20... | collective-permute-start | bytes 786440 | tf_op jit(solution)/shard_map/ppermute | solution.py:279
  (24 other events, 102.8 us)
